TPU v7x, 32 devices: a whole 2x2x4 slice. The times are simulated.
32 devices in a mesh: fsdp: 8 (over z, x), tp: 4 (over y, core).
Axes of the slice: x: 2, y: 2, z: 4, core: 2. Of those that a mesh axis runs over, the one named last changes fastest.
Arguments:
- tokens: bfloat16 [4096, 2048], P('fsdp'), may hold values from -6 to 6
- qkv_weight: bfloat16 [2048, 3, 2048], P('fsdp', None, 'tp'), may hold values from -0.125 to 0.125
- qkv_bias: bfloat16 [3, 8, 256], P(None, 'tp', 'fsdp'), may hold values from -1.796875 to 1.796875
- dense_weight: bfloat16 [2048, 2048], P('tp', 'fsdp'), may hold values from -0.75 to 0.75
- dense_bias: bfloat16 [2048], P('fsdp'), may hold values from -1.796875 to 1.796875
- fc_in_weight: bfloat16 [2048, 8192], P('fsdp', 'tp'), may hold values from -0.125 to 0.125
- fc_in_bias: bfloat16 [128, 64], P('tp', 'fsdp'), may hold values from -1.796875 to 1.796875
- fc_out_weight: bfloat16 [8192, 2048], P('tp', 'fsdp'), may hold values from -0.0625 to 0.0625
- fc_out_bias: bfloat16 [2048], P('fsdp'), may hold values from -1.796875 to 1.796875
- norm1_gain: bfloat16 [2048], P('fsdp'), may hold values from 0.099609375 to 1.8984375
- norm1_shift: bfloat16 [2048], P('fsdp'), may hold values from -1.796875 to 1.796875
- norm2_gain: bfloat16 [2048], P('fsdp'), may hold values from 0.099609375 to 1.8984375
- norm2_shift: bfloat16 [2048], P('fsdp'), may hold values from -1.796875 to 1.796875
- cotangent: bfloat16 [4096, 2048], P('fsdp'), may hold values from -6 to 6
- subset_ids: int32 [4096], P('fsdp'), may hold values from 0 to 21, as said below
- seq_starts: int32 [4], replicated, may hold values from 0 to 4096, as said below
Outputs:
- mixed: bfloat16 [4096, 2048], P('fsdp', 'tp')
- tokens_grad: bfloat16 [4096, 2048], P('fsdp', 'tp')
- qkv_weight_grad: float32 [2048, 3, 2048], P('fsdp', None, 'tp')
- qkv_bias_grad: float32 [3, 8, 256], P(None, 'tp', 'fsdp')
- dense_weight_grad: float32 [2048, 2048], P('tp', 'fsdp')
- dense_bias_grad: float32 [2048], P('fsdp')
- fc_in_weight_grad: float32 [2048, 8192], P('fsdp', 'tp')
- fc_in_bias_grad: float32 [128, 64], P('tp', 'fsdp')
- fc_out_weight_grad: float32 [8192, 2048], P('tp', 'fsdp')
- fc_out_bias_grad: float32 [2048], P('fsdp')
- norm1_gain_grad: float32 [2048], P('fsdp')
- norm1_shift_grad: float32 [2048], P('fsdp')
- norm2_gain_grad: float32 [2048], P('fsdp')
- norm2_shift_grad: float32 [2048], P('fsdp')
Inputs may be any that keep to these rules, and one draw needn't show every extreme that they name: `subset_ids`: rows are mostly grouped in order: about half of the rows carry the subset of their place among 22 equal runs of rows, the rest a random subset; every subset appears. seq_starts[0] = 0; the starts increase until they reach 4096, and all later entries equal 4096 and start no document. Every document has at most 2048 rows and at least one has 2048; every document but the last has at least 1536 rows.
All inputs are finite; a program needn't handle non-finite values.
Results may differ from a plain program's by a relative error of at most 0.012.
Values may be sent and summed in bfloat16 or wider, within the bound.
A program may use at most 256 MiB of HBM per device.

v0:
```python
import math

import jax
import jax.numpy as jnp
from jax import lax
from jax.sharding import PartitionSpec as P

HDIM = 256
ROT = 64
SUBSETS = 22
REACH = 4


EPS = 1e-05


def shifted(value, axis, steps):
    count = lax.axis_size(axis)
    leading, last = (max(0, -steps), min(count, count - steps))
    return lax.ppermute(value, axis, [(source, source + steps) for source in range(leading, last)])


def norm_rows(values, gain, shift):
    mean = jnp.mean(values, axis=-1, keepdims=True)
    centred = values - mean
    spread = jnp.mean(centred * centred, axis=-1, keepdims=True)
    return centred * lax.rsqrt(spread + EPS) * gain + shift


def gelu_exact(values):
    return jax.nn.gelu(values, approximate=False)


def rotate(values, positions):
    half = ROT // 2
    steps = jnp.arange(half, dtype=jnp.float32)
    freq = 1.0 / 10000.0 ** (steps * 2.0 / ROT)
    angle = positions[:, None] * freq[None, :]
    cosine = jnp.cos(angle)[:, None, :]
    sine = jnp.sin(angle)[:, None, :]
    first = values[..., :half]
    second = values[..., half:ROT]
    return jnp.concatenate(
        [first * cosine - second * sine, second * cosine + first * sine, values[..., ROT:]], axis=-1
    )


def locate(indices, starts):
    above = indices[:, None] >= starts[None, :]
    doc_ids = jnp.sum(above.astype(jnp.int32), axis=1) - 1
    pick = doc_ids[:, None] == jnp.arange(starts.shape[0], dtype=jnp.int32)[None, :]
    first = jnp.sum(jnp.where(pick, starts[None, :], 0), axis=1)
    return (doc_ids, (indices - first).astype(jnp.float32))


def inner(left, right):
    return lax.dot_general(
        left, right, (((0,), (0,)), ((), ())), preferred_element_type=jnp.float32
    )


def against(left, right):
    return lax.dot_general(
        left, right, (((1,), (1,)), ((), ())), preferred_element_type=jnp.float32
    )


def on_device(
    tokens,
    qkv_weight,
    qkv_bias,
    dense_weight,
    dense_bias,
    fc_in_weight,
    fc_in_bias,
    fc_out_weight,
    fc_out_bias,
    norm1_gain,
    norm1_shift,
    norm2_gain,
    norm2_shift,
    cotangent,
    subset_ids,
    seq_starts,
):
    f32 = jnp.float32
    bf16 = jnp.bfloat16
    rows = tokens.shape[0]
    width = tokens.shape[1]
    shards = lax.axis_size("fsdp")
    start_row = lax.axis_index("fsdp") * rows
    total = rows * shards
    scale = 1.0 / math.sqrt(HDIM)
    heads_here = qkv_weight.shape[2] // HDIM
    head_cols = heads_here * HDIM
    params = (
        qkv_weight,
        dense_weight,
        fc_in_weight,
        fc_out_weight,
        qkv_bias,
        dense_bias,
        fc_in_bias,
        fc_out_bias,
        norm1_gain,
        norm1_shift,
        norm2_gain,
        norm2_shift,
    )
    full = (
        lax.all_gather(params[0], "fsdp", axis=0, tiled=True),
        lax.all_gather(params[1], "fsdp", axis=1, tiled=True),
        lax.all_gather(params[2], "fsdp", axis=0, tiled=True),
        lax.all_gather(params[3], "fsdp", axis=1, tiled=True),
        lax.all_gather(params[4], "fsdp", axis=2, tiled=True),
        lax.all_gather(params[5], "fsdp", axis=0, tiled=True),
        lax.all_gather(params[6], "fsdp", axis=1, tiled=True),
        lax.all_gather(params[7], "fsdp", axis=0, tiled=True),
        lax.all_gather(params[8], "fsdp", axis=0, tiled=True),
        lax.all_gather(params[9], "fsdp", axis=0, tiled=True),
        lax.all_gather(params[10], "fsdp", axis=0, tiled=True),
        lax.all_gather(params[11], "fsdp", axis=0, tiled=True),
    )
    (
        w_qkv,
        w_dense,
        w_in,
        w_out,
        b_qkv,
        b_dense,
        b_in,
        b_out,
        gain_one,
        shift_one,
        gain_two,
        shift_two,
    ) = full
    x = tokens.astype(f32)
    here = start_row + jnp.arange(rows, dtype=jnp.int32)
    docs_here, pos_here = locate(here, seq_starts)
    normed_one, norm_one_pull = jax.vjp(norm_rows, x, gain_one.astype(f32), shift_one.astype(f32))
    h_one = normed_one.astype(bf16)
    qkv = jnp.dot(
        h_one, w_qkv.reshape(width, 3 * head_cols), preferred_element_type=f32
    ) + b_qkv.astype(f32).reshape(3 * head_cols)
    qkv = qkv.reshape(rows, 3, heads_here, HDIM)
    q_three = rotate(qkv[:, 0], pos_here).astype(bf16)
    k_three = rotate(qkv[:, 1], pos_here).astype(bf16)
    v_three = qkv[:, 2].astype(bf16)
    packed = jnp.stack([k_three.reshape(rows, head_cols), v_three.reshape(rows, head_cols)], axis=1)
    pieces = []
    for dist in range(REACH, 0, -1):
        pieces.append(shifted(packed, "fsdp", dist))
    pieces.append(packed)
    window = jnp.concatenate(pieces, axis=0)
    span = window.shape[0]
    cols = start_row - REACH * rows + jnp.arange(span, dtype=jnp.int32)
    docs_cols, _ = locate(cols, seq_starts)
    allowed = (cols[None, :] <= here[:, None]) & (docs_cols[None, :] == docs_here[:, None])
    key_win = window[:, 0].reshape(span, heads_here, HDIM)
    value_win = window[:, 1].reshape(span, heads_here, HDIM)
    scores = jnp.einsum("qhd,khd->hqk", q_three, key_win, preferred_element_type=f32) * scale
    masked = jnp.where(allowed[None], scores, -1e30)
    top = jnp.max(masked, axis=2, keepdims=True)
    expo = jnp.exp(masked - top)
    probs = expo / jnp.sum(expo, axis=2, keepdims=True)
    probs_b = probs.astype(bf16)
    attended = jnp.einsum("hqk,khd->qhd", probs_b, value_win, preferred_element_type=f32)
    att_b = attended.reshape(rows, head_cols).astype(bf16)
    normed_two, norm_two_pull = jax.vjp(norm_rows, x, gain_two.astype(f32), shift_two.astype(f32))
    h_two = normed_two.astype(bf16)
    pre = jnp.dot(h_two, w_in, preferred_element_type=f32) + b_in.astype(f32).reshape(w_in.shape[1])
    act, gelu_pull = jax.vjp(gelu_exact, pre)
    act_b = act.astype(bf16)
    partial_value = jnp.dot(att_b, w_dense, preferred_element_type=f32) + jnp.dot(
        act_b, w_out, preferred_element_type=f32
    )
    share = lax.psum_scatter(partial_value, "tp", scatter_dimension=1, tiled=True)
    part_w = width // lax.axis_size("tp")
    offset = lax.axis_index("tp") * part_w
    bias_part = lax.dynamic_slice_in_dim(
        b_dense.astype(f32), offset, part_w, 0
    ) + lax.dynamic_slice_in_dim(b_out.astype(f32), offset, part_w, 0)
    mixed = (lax.dynamic_slice_in_dim(x, offset, part_w, 1) + share + bias_part).astype(bf16)
    w_qkv, w_dense, w_in, w_out = (
        lax.all_gather(qkv_weight, "fsdp", axis=0, tiled=True),
        lax.all_gather(dense_weight, "fsdp", axis=1, tiled=True),
        lax.all_gather(fc_in_weight, "fsdp", axis=0, tiled=True),
        lax.all_gather(fc_out_weight, "fsdp", axis=1, tiled=True),
    )
    match = subset_ids[:, None] == jnp.arange(SUBSETS, dtype=jnp.int32)[None, :]
    local_counts = jnp.sum(match.astype(jnp.int32), axis=0)
    counts = lax.psum(local_counts, "fsdp").astype(f32)
    table = total / (SUBSETS * counts)
    row_scale = jnp.sum(jnp.where(match, table[None, :], 0.0), axis=1)
    carried = cotangent.astype(f32) * row_scale[:, None]
    grad_b = carried.astype(bf16)
    bias_grad = jnp.sum(grad_b.astype(f32), axis=0)
    dense_grad = inner(att_b, grad_b)
    out_grad = inner(act_b, grad_b)
    d_pre = gelu_pull(against(grad_b, w_out))[0].astype(bf16)
    in_grad = inner(h_two, d_pre)
    in_bias_grad = jnp.sum(d_pre.astype(f32), axis=0).reshape(b_in.shape)
    e_two = against(d_pre, w_in)
    d_att = against(grad_b, w_dense).astype(bf16)
    do_three = d_att.reshape(rows, heads_here, HDIM)
    dprob = jnp.einsum("qhd,khd->hqk", do_three, value_win, preferred_element_type=f32)
    delta = jnp.sum(probs * dprob, axis=2, keepdims=True)
    dscore = (probs * (dprob - delta)).astype(bf16)
    dq = jnp.einsum("hqk,khd->qhd", dscore, key_win, preferred_element_type=f32) * scale
    dk_win = jnp.einsum("hqk,qhd->khd", dscore, q_three, preferred_element_type=f32) * scale
    dv_win = jnp.einsum("hqk,qhd->khd", probs_b, do_three, preferred_element_type=f32)
    grads_win = jnp.stack(
        [dk_win.reshape(span, head_cols), dv_win.reshape(span, head_cols)], axis=1
    )
    dkv = grads_win[REACH * rows :]
    for dist in range(1, REACH + 1):
        begin = (REACH - dist) * rows
        dkv = dkv + shifted(grads_win[begin : begin + rows], "fsdp", -dist)
    _, unrotate = jax.vjp(lambda values: rotate(values, pos_here), qkv[:, 0])
    dq_raw = unrotate(dq)[0]
    dk_raw = unrotate(dkv[:, 0].reshape(rows, heads_here, HDIM))[0]
    d_qkv = (
        jnp.stack([dq_raw, dk_raw, dkv[:, 1].reshape(rows, heads_here, HDIM)], axis=1)
        .reshape(rows, 3 * head_cols)
        .astype(bf16)
    )
    qkv_grad = inner(h_one, d_qkv).reshape(width, 3, head_cols)
    qkv_bias_grad = jnp.sum(d_qkv.astype(f32), axis=0).reshape(3, heads_here, HDIM)
    e_one = against(d_qkv, w_qkv.reshape(width, 3 * head_cols))
    e_one, e_two = lax.psum((e_one, e_two), "tp")
    dx_one, gain_one_grad, shift_one_grad = norm_one_pull(e_one)
    dx_two, gain_two_grad, shift_two_grad = norm_two_pull(e_two)
    dx_full = carried + dx_one + dx_two
    tokens_grad = lax.dynamic_slice_in_dim(dx_full, offset, part_w, 1).astype(bf16)
    grads = (
        qkv_grad,
        dense_grad,
        in_grad,
        out_grad,
        qkv_bias_grad,
        bias_grad,
        in_bias_grad,
        bias_grad,
        gain_one_grad,
        shift_one_grad,
        gain_two_grad,
        shift_two_grad,
    )
    parts = (
        lax.psum_scatter(grads[0], "fsdp", scatter_dimension=0, tiled=True),
        lax.psum_scatter(grads[1], "fsdp", scatter_dimension=1, tiled=True),
        lax.psum_scatter(grads[2], "fsdp", scatter_dimension=0, tiled=True),
        lax.psum_scatter(grads[3], "fsdp", scatter_dimension=1, tiled=True),
        lax.psum_scatter(grads[4], "fsdp", scatter_dimension=2, tiled=True),
        lax.psum_scatter(grads[5], "fsdp", scatter_dimension=0, tiled=True),
        lax.psum_scatter(grads[6], "fsdp", scatter_dimension=1, tiled=True),
        lax.psum_scatter(grads[7], "fsdp", scatter_dimension=0, tiled=True),
        lax.psum_scatter(grads[8], "fsdp", scatter_dimension=0, tiled=True),
        lax.psum_scatter(grads[9], "fsdp", scatter_dimension=0, tiled=True),
        lax.psum_scatter(grads[10], "fsdp", scatter_dimension=0, tiled=True),
        lax.psum_scatter(grads[11], "fsdp", scatter_dimension=0, tiled=True),
    )
    return (
        mixed,
        tokens_grad,
        parts[0],
        parts[4],
        parts[1],
        parts[5],
        parts[2],
        parts[6],
        parts[3],
        parts[7],
        parts[8],
        parts[9],
        parts[10],
        parts[11],
    )


def solution(mesh):
    in_specs = (
        P("fsdp", None),
        P("fsdp", None, "tp"),
        P(None, "tp", "fsdp"),
        P("tp", "fsdp"),
        P("fsdp"),
        P("fsdp", "tp"),
        P("tp", "fsdp"),
        P("tp", "fsdp"),
        P("fsdp"),
        P("fsdp"),
        P("fsdp"),
        P("fsdp"),
        P("fsdp"),
        P("fsdp", None),
        P("fsdp"),
        P(),
    )
    out_specs = (
        P("fsdp", "tp"),
        P("fsdp", "tp"),
        P("fsdp", None, "tp"),
        P(None, "tp", "fsdp"),
        P("tp", "fsdp"),
        P("fsdp"),
        P("fsdp", "tp"),
        P("tp", "fsdp"),
        P("tp", "fsdp"),
        P("fsdp"),
        P("fsdp"),
        P("fsdp"),
        P("fsdp"),
        P("fsdp"),
    )
    return jax.shard_map(
        on_device, mesh=mesh, in_specs=in_specs, out_specs=out_specs, check_vma=False
    )
```

profile of v0, /device:TPU:0, one launch (start us, length us, event | category | flops | bytes accessed | tf_op | source)
XLA Modules:
  0.0 2017.3 jit_solution(739427186055519386)
XLA Ops:
  12.9 22.4 %all-gather = bf16[8,1,256]{2,1,0:T(2,128)(2,1)S(1)} all-gather(bf16[1,1,256]{2,1,0:T(2,128)(2,1)S(1)} %reshape.277), channel_id=1, replica_groups=mesh['fsdp'=8,'tp'=4] {'fsdp'}, dimensions={0}, use_global_device_ids=true | all-gather | bytes 4608 | tf_op jit(solution)/shard_map/all_gather | solution.py:119
  35.4 16.5 all-gather.1
  52.0 32.8 %all_gather.43 = bf16[3,2,256]{0,1,2:T(2,128)(2,1)S(1)} all-gather(bf16[3,2,32]{0,1,2:T(2,128)(2,1)S(1)} %copy.137), channel_id=1, replica_groups=mesh['fsdp'=8,'tp'=4] {'fsdp'}, dimensions={2}, use_global_device_ids=true | all-gather | bytes 3456 | tf_op jit(solution)/shard_map/all_gather | solution.py:115
  87.2 28.0 %all-gather.11.cloned.1.call-done = bf16[2048,3,512]{0,2,1:T(8,128)(2,1)} async-done(((bf16[256,3,512]{0,2,1:T(8,128)(2,1)}), bf16[2048,3,512]{0,2,1:T(8,128)(2,1)}) %all-gather.11.cloned.1.call-update) | async-done | bytes 6291472 | tf_op jit(solution)/shard_map/all_gather | solution.py:111
  115.1 7.9 convolution_add_fusion.1
  123.0 5.2 reshape.272
  142.1 4.5 collective-permute-start
  146.6 3.4 collective-permute-start.1
  154.5 74.2 %psum.21 = s32[22]{0:T(128)S(1)} all-reduce(s32[22]{0:T(128)S(1)} %convert_reduce_fusion.4), channel_id=1, replica_groups=mesh['fsdp'=8,'tp'=4] {'fsdp'}, use_global_device_ids=true, to_apply=%region_9.10 | all-reduce | flops 22 | bytes 176 | tf_op jit(solution)/shard_map/psum | solution.py:193
  228.7 4.9 collective-permute-start.3
  233.7 4.4 convolution_convert_fusion
  243.1 18.3 collective-permute-done.3
  262.8 2.7 fusion.51
  265.4 10.3 fusion.54
  275.7 9.3 fusion.11
  285.0 8.1 multiply_reduce_fusion
  295.7 3.0 convolution_multiply_fusion
  298.7 2.8 copy-done.2
  301.5 4.0 fusion.21
  310.7 387.0 %all-gather.2 = bf16[8,1,256]{2,1,0:T(2,128)(2,1)S(1)} all-gather(bf16[1,1,256]{2,1,0:T(2,128)(2,1)S(1)} %reshape.281), channel_id=1, replica_groups=mesh['fsdp'=8,'tp'=4] {'fsdp'}, dimensions={0}, use_global_device_ids=true | all-gather | bytes 4608 | tf_op jit(solution)/shard_map/all_gather | solution.py:121
  697.7 120.5 %all_gather.48 = bf16[32,64]{0,1:T(8,128)(2,1)S(1)} all-gather(bf16[32,8]{0,1:T(8,128)(2,1)S(1)} %copy-done.24), channel_id=1, replica_groups=mesh['fsdp'=8,'tp'=4] {'fsdp'}, dimensions={1}, use_global_device_ids=true | all-gather | bytes 4608 | tf_op jit(solution)/shard_map/all_gather | solution.py:117
  818.4 16.3 all-gather.3
  834.7 5.0 fusion.25
  841.1 5.0 fusion.20
  858.3 2.6 copy.153
  862.1 8.7 fusion.56
  871.1 17.9 multiply_convert_fusion.1
  888.9 13.7 convert_reduce_fusion
  902.7 8.3 fusion.57
  912.1 7.7 fusion.26
  919.8 7.7 fusion.55
  927.5 3.3 convolution_add_fusion
  930.9 4.9 fusion.41
  935.9 8.6 fusion.23
  944.6 10.1 fusion.37
  954.8 12.7 fusion.39
  972.0 18.5 all-gather.4
  990.5 16.3 all-gather.5
  1006.9 4.1 convert_reduce_fusion.1
  1012.6 72.6 %all-reduce.16.cloned.1.call-done = (f32[512,2048]{1,0:T(8,128)}, f32[512,2048]{1,0:T(8,128)}) async-done(((f32[512,2048]{1,0:T(8,128)}, f32[512,2048]{1,0:T(8,128)}), (f32[512,2048]{1,0:T(8,128)}, f32[512,2048]{1,0:T(8,128)})) %all-reduce.16.cloned.1.call-update) | async-done | bytes 8388624 | tf_op jit(solution)/shard_map/psum | solution.py:231
  1085.2 5.3 multiply_reduce_fusion.2
  1090.5 37.9 %all-reduce.12 = (f32[2048]{0:T(1024)S(1)}, f32[32,64]{1,0:T(8,128)S(1)}, f32[2048]{0:T(1024)S(1)}, f32[2048]{0:T(1024)S(1)}, f32[2048]{0:T(1024)S(1)}, /*index=5*/f32[2048]{0:T(1024)S(1)}) all-reduce(f32[2048]{0:T(1024)S(1)} %get-tuple-element.133, f32[32,64]{1,0:T(8,128)S(1)} %reshape.274, ...), channel_id=6, replica_groups=mesh['fsdp'=8,'tp'=4] {'fsdp'}, use_global_device_ids=true, to_apply=%region_23.24.clone | all-reduce | flops 12288 | bytes 98304
  1131.8 4.7 fusion.48
  1138.9 2.6 add_convert_fusion.3
  1141.5 84.1 %reduce-scatter.14.cloned.1.call-done = f32[512,256]{1,0:T(8,128)} async-done(((f32[512,2048]{1,0:T(8,128)}), f32[512,256]{1,0:T(8,128)}) %reduce-scatter.14.cloned.1.call-update) | async-done | bytes 524304 | tf_op jit(solution)/shard_map/reduce_scatter | solution.py:252
  1225.5 211.8 %reduce-scatter.12.cloned.1.call-done = f32[256,3,512]{2,0,1:T(8,128)} async-done(((f32[2048,3,512]{2,0,1:T(8,128)}), f32[256,3,512]{2,0,1:T(8,128)}) %reduce-scatter.12.cloned.1.call-update) | async-done | bytes 1572880 | tf_op jit(solution)/shard_map/reduce_scatter | solution.py:251
  1437.3 286.0 %reduce-scatter.16.cloned.1.call-done = f32[256,2048]{1,0:T(8,128)} async-done(((f32[2048,2048]{1,0:T(8,128)}), f32[256,2048]{1,0:T(8,128)}) %reduce-scatter.16.cloned.1.call-update) | async-done | bytes 2097168 | tf_op jit(solution)/shard_map/reduce_scatter | solution.py:253
  1723.2 286.7 %reduce-scatter.18.cloned.1.call-done = f32[2048,256]{1,0:T(8,128)} async-done(((f32[2048,2048]{1,0:T(8,128)}), f32[2048,256]{1,0:T(8,128)}) %reduce-scatter.18.cloned.1.call-update) | async-done | bytes 2097168 | tf_op jit(solution)/shard_map/reduce_scatter | solution.py:254
  (203 shorter events, 68.2 us)
Async XLA Ops:
  7.2 4.7 copy-start
  7.2 5.7 copy-start.27
  7.2 28.2 %copy-start.28 = (bf16[256]{0:T(256)(128)(2,1)S(1)}, bf16[256]{0:T(256)(128)(2,1)}, u32[]{:S(2)}) copy-start(bf16[256]{0:T(256)(128)(2,1)} %param.26) | copy-start | bytes 1540
  7.2 44.7 %copy-start.25 = (bf16[3,2,32]{2,1,0:T(2,128)(2,1)S(1)}, bf16[3,2,32]{2,1,0:T(2,128)(2,1)}, u32[]{:S(2)}) copy-start(bf16[3,2,32]{2,1,0:T(2,128)(2,1)} %param.18) | copy-start | bytes 1156
  7.2 107.9 %all-gather.11.cloned.1.call-start = ((), (), s32[]{:S(2)}) async-start(), calls=%async_computation.6 | async-start | bytes 7077888 | tf_op jit(solution)/shard_map/all_gather | solution.py:111
  9.7 75.3 %copy-start.22 = (s32[4]{0:T(128)S(1)}, s32[4]{0:T(128)}, u32[]{:S(2)}) copy-start(s32[4]{0:T(128)} %param.31) | copy-start | bytes 52
  9.7 75.6 %copy-start.19 = (s32[512]{0:T(512)S(1)}, s32[512]{0:T(512)}, u32[]{:S(2)}) copy-start(s32[512]{0:T(512)} %param.30) | copy-start | bytes 6148
  9.7 224.0 %all-gather.13.cloned.1.call-start = ((), (), s32[]{:S(2)}) async-start(), calls=%async_computation.7 | async-start | bytes 2359296 | tf_op jit(solution)/shard_map/all_gather | solution.py:112
  10.5 860.6 %all-gather.15.cloned.1.call-start = ((), (), s32[]{:S(2)}) async-start(), calls=%async_computation.8 | async-start | bytes 9437184 | tf_op jit(solution)/shard_map/all_gather | solution.py:113
  11.2 877.7 %all-gather.17.cloned.1.call-start = ((), (), s32[]{:S(2)}) async-start(), calls=%async_computation.9 | async-start | bytes 9437184 | tf_op jit(solution)/shard_map/all_gather | solution.py:114
  11.8 999.2 %reduce-scatter.20.cloned.1.call-start = ((), (), s32[]{:S(2)}) async-start(), calls=%async_computation.15 | async-start | bytes 147456
  12.9 39.0 %copy-start.17 = (f32[512]{0:T(512)}, f32[512]{0:T(512)S(1)}, u32[]{:S(2)}) copy-start(f32[512]{0:T(512)S(1)} %multiply_reduce_fusion.5) | copy-start | bytes 6148
  35.4 87.6 %copy-start.15 = (f32[8,1,256]{2,1,0:T(1,128)}, f32[8,1,256]{2,1,0:T(1,128)S(1)}, u32[]{:S(2)}) copy-start(f32[8,1,256]{2,1,0:T(1,128)S(1)} %convert_element_type.164) | copy-start | bytes 24580
  51.9 71.1 %copy-start.20 = (f32[8,1,256]{2,1,0:T(1,128)}, f32[8,1,256]{2,1,0:T(1,128)S(1)}, u32[]{:S(2)}) copy-start(f32[8,1,256]{2,1,0:T(1,128)S(1)} %convert_element_type.165) | copy-start | bytes 24580
  142.1 97.0 %collective-permute-start = (bf16[512,2,512]{0,2,1:T(8,128)(2,1)}, bf16[512,2,512]{0,2,1:T(8,128)(2,1)}, u32[]{:S(2)}, u32[]{:S(2)}) collective-permute-start(bf16[512,2,512]{0,2,1:T(8,128)(2,1)} %pad_maximum_fusion.1), channel_id=1, source_target_pairs={{0,16},{4,20},{8,24},{12,28},{1,17},{5,21},{9,25},{13,29},{2,18},{... | collective-permute-start | bytes 3145736 | tf_op jit(solution)/shard_map/ppermute | solution.py:20
  146.6 93.9 %collective-permute-start.1 = (bf16[512,2,512]{0,2,1:T(8,128)(2,1)}, bf16[512,2,512]{0,2,1:T(8,128)(2,1)}, u32[]{:S(2)}, u32[]{:S(2)}) collective-permute-start(bf16[512,2,512]{0,2,1:T(8,128)(2,1)} %pad_maximum_fusion.1), channel_id=1, source_target_pairs={{0,12},{4,16},{8,20},{12,24},{16,28},{1,13},{5,17},{9,21},{13,25},... | collective-permute-start | bytes 3145736 | tf_op jit(solution)/shard_map/ppermute | solution.py:20
  150.0 91.8 %collective-permute-start.2 = (bf16[512,2,512]{0,2,1:T(8,128)(2,1)}, bf16[512,2,512]{0,2,1:T(8,128)(2,1)}, u32[]{:S(2)}, u32[]{:S(2)}) collective-permute-start(bf16[512,2,512]{0,2,1:T(8,128)(2,1)} %pad_maximum_fusion.1), channel_id=1, source_target_pairs={{0,8},{4,12},{8,16},{12,20},{16,24},{20,28},{1,9},{5,13},{9,17},{1... | collective-permute-start | bytes 3145736 | tf_op jit(solution)/shard_map/ppermute | solution.py:20
  228.7 32.7 %collective-permute-start.3 = (bf16[512,2,512]{0,2,1:T(8,128)(2,1)}, bf16[512,2,512]{0,2,1:T(8,128)(2,1)}, u32[]{:S(2)}, u32[]{:S(2)}) collective-permute-start(bf16[512,2,512]{0,2,1:T(8,128)(2,1)} %pad_maximum_fusion.1), channel_id=1, source_target_pairs={{0,4},{4,8},{8,12},{12,16},{16,20},{20,24},{24,28},{1,5},{5,9},{9,... | collective-permute-start | bytes 3145736 | tf_op jit(solution)/shard_map/ppermute | solution.py:20
  239.1 23.6 %copy-start.4 = (bf16[512,2,256]{0,2,1:T(8,128)(2,1)S(1)}, bf16[512,2,256]{0,2,1:T(8,128)(2,1)}, u32[]{:S(2)}) copy-start(bf16[512,2,256]{0,2,1:T(8,128)(2,1)} %copy.140) | copy-start | bytes 1572868
  239.1 23.6 %copy-start.5 = (bf16[512,1,2,256]{0,3,2,1:T(8,128)(2,1)S(1)}, bf16[512,1,2,256]{0,3,2,1:T(8,128)(2,1)}, u32[]{:S(2)}) copy-start(bf16[512,1,2,256]{0,3,2,1:T(8,128)(2,1)} %copy.141) | copy-start | bytes 1572868
  285.0 8.1 slice-start.2
  285.0 8.4 slice-start.3
  285.0 9.0 slice-start.4
  295.7 5.8 copy-start.2
  298.7 6.8 copy-start.1
  301.5 9.2 copy-start.29
  301.5 396.3 %copy-start.24 = (bf16[32,8]{0,1:T(8,128)(2,1)S(1)}, bf16[32,8]{0,1:T(8,128)(2,1)}, u32[]{:S(2)}) copy-start(bf16[32,8]{0,1:T(8,128)(2,1)} %param.22) | copy-start | bytes 1540
  301.5 516.9 %copy-start.30 = (bf16[256]{0:T(256)(128)(2,1)S(1)}, bf16[256]{0:T(256)(128)(2,1)}, u32[]{:S(2)}) copy-start(bf16[256]{0:T(256)(128)(2,1)} %param.28) | copy-start | bytes 1540
  305.5 535.6 %collective-permute-start.4 = (f32[512,2,512]{0,2,1:T(8,128)}, f32[512,2,512]{0,2,1:T(8,128)}, u32[]{:S(2)}, u32[]{:S(2)}) collective-permute-start(f32[512,2,512]{0,2,1:T(8,128)} %get-tuple-element.123), channel_id=1, source_target_pairs={{4,0},{8,4},{12,8},{16,12},{20,16},{24,20},{28,24},{5,1},{9,5},{13... | collective-permute-start | bytes 6291464 | tf_op jit(solution)/shard_map/ppermute | solution.py:20
  306.7 534.3 %collective-permute-start.5 = (f32[512,2,512]{0,2,1:T(8,128)}, f32[512,2,512]{0,2,1:T(8,128)}, u32[]{:S(2)}, u32[]{:S(2)}) collective-permute-start(f32[512,2,512]{0,2,1:T(8,128)} %get-tuple-element.124), channel_id=1, source_target_pairs={{8,0},{12,4},{16,8},{20,12},{24,16},{28,20},{9,1},{13,5},{17,9},{2... | collective-permute-start | bytes 6291464 | tf_op jit(solution)/shard_map/ppermute | solution.py:20
  308.0 533.0 %collective-permute-start.6 = (f32[512,2,512]{0,2,1:T(8,128)}, f32[512,2,512]{0,2,1:T(8,128)}, u32[]{:S(2)}, u32[]{:S(2)}) collective-permute-start(f32[512,2,512]{0,2,1:T(8,128)} %get-tuple-element.126), channel_id=1, source_target_pairs={{12,0},{16,4},{20,8},{24,12},{28,16},{13,1},{17,5},{21,9},{25,13},... | collective-permute-start | bytes 6291464 | tf_op jit(solution)/shard_map/ppermute | solution.py:20
  309.3 531.7 %collective-permute-start.7 = (f32[512,2,512]{0,2,1:T(8,128)}, f32[512,2,512]{0,2,1:T(8,128)}, u32[]{:S(2)}, u32[]{:S(2)}) collective-permute-start(f32[512,2,512]{0,2,1:T(8,128)} %get-tuple-element.125), channel_id=1, source_target_pairs={{16,0},{20,4},{24,8},{28,12},{17,1},{21,5},{25,9},{29,13},{18,2},{... | collective-permute-start | bytes 6291464 | tf_op jit(solution)/shard_map/ppermute | solution.py:20
  834.7 6.4 slice-start
  834.7 6.4 slice-start.1
  870.8 214.4 %all-reduce.16.cloned.1.call-start = ((), (), s32[]{:S(2)}) async-start(), calls=%async_computation.16 | async-start | bytes 16777216 | tf_op jit(solution)/shard_map/psum | solution.py:231
  888.9 13.8 copy-start.26
  911.1 227.8 %reduce-scatter.10.cloned.1.call-start = ((), (), s32[]{:S(2)}) async-start(), calls=%async_computation.10 | async-start | bytes 5242880 | tf_op jit(solution)/shard_map/reduce_scatter | solution.py:178
  919.8 7.7 copy-start.12
  930.8 5.0 copy-start.16
  930.8 5.0 copy-start.21
  930.8 294.7 %reduce-scatter.14.cloned.1.call-start = ((), (), s32[]{:S(2)}) async-start(), calls=%async_computation.12 | async-start | bytes 4718592 | tf_op jit(solution)/shard_map/reduce_scatter | solution.py:252
  935.8 501.5 %reduce-scatter.12.cloned.1.call-start = ((), (), s32[]{:S(2)}) async-start(), calls=%async_computation.11 | async-start | bytes 14155776 | tf_op jit(solution)/shard_map/reduce_scatter | solution.py:251
  944.6 778.7 %reduce-scatter.16.cloned.1.call-start = ((), (), s32[]{:S(2)}) async-start(), calls=%async_computation.13 | async-start | bytes 18874368 | tf_op jit(solution)/shard_map/reduce_scatter | solution.py:253
  954.7 1055.2 %reduce-scatter.18.cloned.1.call-start = ((), (), s32[]{:S(2)}) async-start(), calls=%async_computation.14 | async-start | bytes 18874368 | tf_op jit(solution)/shard_map/reduce_scatter | solution.py:254
  967.5 4.4 copy-start.31
  967.5 23.0 %copy-start.32 = (bf16[256]{0:T(256)(128)(2,1)S(1)}, bf16[256]{0:T(256)(128)(2,1)}, u32[]{:S(2)}) copy-start(bf16[256]{0:T(256)(128)(2,1)} %param.24) | copy-start | bytes 1540
  1085.2 46.6 %copy-start.18 = (f32[512]{0:T(512)S(1)}, f32[512]{0:T(512)}, u32[]{:S(2)}) copy-start(f32[512]{0:T(512)} %copy-done.17) | copy-start | bytes 6148
  1129.2 880.7 %copy-start.23 = (f32[256]{0:T(256)}, f32[256]{0:T(256)S(1)}, u32[]{:S(2)}) copy-start(f32[256]{0:T(256)S(1)} %dynamic-slice.1) | copy-start | bytes 3076
  (10 other events, 22.5 us)
Sparse Core Ops, SparseCore 0:
  10.7 104.4 all-gather.10
  117.2 61.4 all-gather.12
  180.8 190.3 all-gather.14
  373.1 217.8 all-gather.16
  870.9 59.4 reduce-scatter.19
  932.9 152.2 all-reduce.15
  1087.7 44.6 reduce-scatter.9
  1137.0 88.4 reduce-scatter.13
  1229.7 207.5 reduce-scatter.11
  1441.5 281.7 reduce-scatter.15
  1728.1 281.7 reduce-scatter.17
where the time goes:
time: 2030 us; the launch traced here: 2020 us
  waiting for transfers between devices  989 us (49%)
  blocking collectives  742 us (37%)
  matrix products  151 us (7%)
  local copies, waits for them, and re-layouts  49.5 us (2%)
  other arithmetic  47.5 us (2%)
  starting transfers between devices  20.9 us (1%)
    all_gather x1, blocking collectives, on_device(): lax.all_gather(params[10], 'fsdp', axis=0, tiled=True)  387 us
    reduce_scatter x1, waiting for transfers between devices, on_device(): lax.psum_scatter(grads[3], 'fsdp', scatter_dimension=1, tiled=True)  287 us
    reduce_scatter x1, waiting for transfers between devices, on_device(): lax.psum_scatter(grads[2], 'fsdp', scatter_dimension=0, tiled=True)  286 us
    reduce_scatter x1, waiting for transfers between devices, on_device(): lax.psum_scatter(grads[0], 'fsdp', scatter_dimension=0, tiled=True)  212 us
    all_gather x1, blocking collectives, on_device(): lax.all_gather(params[6], 'fsdp', axis=1, tiled=True)  120 us
    reduce_scatter x1, waiting for transfers between devices, on_device(): lax.psum_scatter(grads[1], 'fsdp', scatter_dimension=1, tiled=True)  84.1 us
    psum x1, blocking collectives, on_device(): counts = lax.psum(local_counts, 'fsdp').astype(f32)  74.2 us
    psum x1, waiting for transfers between devices, on_device(): e_one, e_two = lax.psum((e_one, e_two), 'tp')  72.6 us
  transfers between devices with their start and end apart: 19, of which 7 were waited for; matrix products, arithmetic and copies ran while one was open for 12% of the time, Pallas kernels for 0%

commit v1 on v0

v1 whole, which is shorter than its diff:
```python
import math

import jax
import jax.numpy as jnp
from jax import lax
from jax.sharding import PartitionSpec as P

HDIM = 256
ROT = 64
SUBSETS = 22
SEQ_LEN = 2048
EPS = 1e-05
F32 = jnp.float32
BF16 = jnp.bfloat16


def mm(left, right, dims):
    return lax.dot_general(left, right, (dims, ((), ())), preferred_element_type=F32)


def plain(left, right):
    return mm(left, right, ((1,), (0,)))


def inner(left, right):
    return mm(left, right, ((0,), (0,)))


def against(left, right):
    return mm(left, right, ((1,), (1,)))


def rotary_tables(positions):
    half = ROT // 2
    steps = jnp.arange(half, dtype=F32)
    freq = 1.0 / 10000.0 ** (steps * 2.0 / ROT)
    angle = positions[:, None] * freq[None, :]
    return jnp.cos(angle), jnp.sin(angle)


def rotate(values, cosine, sine):
    half = ROT // 2
    first = values[..., :half]
    second = values[..., half:ROT]
    return jnp.concatenate(
        [first * cosine - second * sine, second * cosine + first * sine, values[..., ROT:]], axis=-1
    )


def locate(indices, starts):
    above = indices[:, None] >= starts[None, :]
    doc_ids = jnp.sum(above.astype(jnp.int32), axis=1) - 1
    pick = doc_ids[:, None] == jnp.arange(starts.shape[0], dtype=jnp.int32)[None, :]
    first = jnp.sum(jnp.where(pick, starts[None, :], 0), axis=1)
    return (doc_ids, (indices - first).astype(F32))


def swap(value):
    count = lax.axis_size("fsdp")
    return lax.ppermute(value, "fsdp", [(s, s ^ 1) for s in range(count)])


def planes(value, steps, reach=None):
    count = lax.axis_size("fsdp")
    pairs = []
    for s in range(count):
        d = s + 2 * steps
        if 0 <= d < count:
            if reach is None or 0 <= s + 2 * reach < count:
                pairs.append((s, d))
    return lax.ppermute(value, "fsdp", pairs)


def gather_planes(chunk, d, dp):
    ups, downs = [chunk], [chunk]
    for _ in range(dp - 1):
        ups.append(planes(ups[-1], 1))
        downs.append(planes(downs[-1], -1))
    rows = chunk.shape[0]
    full = jnp.zeros((dp * rows, chunk.shape[1]), chunk.dtype)
    for s in range(dp):
        piece = chunk if s == 0 else jnp.where(d >= s, ups[s], downs[dp - s])
        full = lax.dynamic_update_slice_in_dim(full, piece, lax.rem(d - s + dp, dp) * rows, 0)
    return full


def reduce_planes(parts, d, dp):
    rows = parts.shape[0] // dp

    def block(k):
        where = jnp.clip(d + k, 0, dp - 1) * rows
        return lax.dynamic_slice_in_dim(parts, where, rows, 0).astype(F32)

    total = block(0)
    for sign in (1, -1):
        held = None
        for s in range(dp - 1):
            k = sign * (dp - 1 - s)
            value = block(k) if held is None else block(k) + held.astype(F32)
            held = planes(value.astype(BF16), sign, k)
        if held is not None:
            total = total + held.astype(F32)
    return total


def tp_scatter(value, t, count):
    rows, cols = value.shape
    part = cols // count
    value = value.reshape(rows, count, part)
    bit = 1
    while bit < count:
        n = value.shape[1]
        view = value.reshape(rows, n // 2, 2, part)
        mine = lax.rem(t // bit, 2)
        keep = lax.dynamic_index_in_dim(view, mine, 2, keepdims=False)
        send = lax.dynamic_index_in_dim(view, 1 - mine, 2, keepdims=False)
        got = lax.ppermute(send.astype(BF16), "tp", [(s, s ^ bit) for s in range(count)])
        value = keep.astype(F32) + got.astype(F32)
        bit *= 2
    return value.reshape(rows, part)


def tp_sum(value, count):
    bit = 1
    while bit < count:
        value = value + lax.ppermute(value, "tp", [(s, s ^ bit) for s in range(count)])
        bit *= 2
    return value


def half_of(value, which, axis):
    size = value.shape[axis] // 2
    return lax.dynamic_slice_in_dim(value, which * size, size, axis)


def pair_rows(value, i):
    got = swap(value)
    return jnp.where(i == 0, jnp.concatenate([value, got], 0), jnp.concatenate([got, value], 0))


def on_device(
    tokens,
    qkv_weight,
    qkv_bias,
    dense_weight,
    dense_bias,
    fc_in_weight,
    fc_in_bias,
    fc_out_weight,
    fc_out_bias,
    norm1_gain,
    norm1_shift,
    norm2_gain,
    norm2_shift,
    cotangent,
    subset_ids,
    seq_starts,
):
    rows, width = tokens.shape
    shards = lax.axis_size("fsdp")
    tps = lax.axis_size("tp")
    dp = shards // 2
    f = lax.axis_index("fsdp")
    t = lax.axis_index("tp")
    i = lax.rem(f, 2)
    d = f // 2
    total = rows * shards
    scale = 1.0 / math.sqrt(HDIM)
    feats = qkv_weight.shape[0]
    units = fc_in_weight.shape[1]
    head_cols = qkv_weight.shape[2]
    heads_here = head_cols // HDIM
    hd = qkv_bias.shape[2]
    ub = fc_in_bias.shape

    match = subset_ids[:, None] == jnp.arange(SUBSETS, dtype=jnp.int32)[None, :]
    counts = jnp.sum(match.astype(F32), axis=0)
    vecs = [norm1_gain, norm1_shift, norm2_gain, norm2_shift, dense_bias, fc_out_bias]
    pack = jnp.concatenate(
        [v.astype(F32) for v in vecs]
        + [qkv_bias.astype(F32).reshape(-1), fc_in_bias.astype(F32).reshape(-1), counts]
    )
    got = lax.all_gather(pack, "fsdp", axis=0, tiled=False)
    gain1, shift1, gain2, shift2, b_dense, b_out = [
        got[:, k * feats : (k + 1) * feats].reshape(width) for k in range(6)
    ]
    at = 6 * feats
    nq = 3 * heads_here * hd
    b_qkv = got[:, at : at + nq].reshape(shards, 3, heads_here, hd)
    b_qkv = b_qkv.transpose(1, 2, 0, 3).reshape(3, heads_here, HDIM)
    b_qkv = lax.dynamic_index_in_dim(b_qkv, i, 1, keepdims=False).reshape(3 * HDIM)
    at += nq
    b_in = got[:, at : at + units // shards].reshape(shards, ub[0], ub[1])
    b_in = half_of(b_in.transpose(1, 0, 2).reshape(units), i, 0)
    at += units // shards
    counts = jnp.sum(got[:, at:], axis=0)
    table = total / (SUBSETS * counts)
    row_scale = jnp.sum(jnp.where(match, table[None, :], 0.0), axis=1)
    carried = cotangent.astype(F32) * row_scale[:, None]
    grad_here = carried.astype(BF16)

    wq = qkv_weight.reshape(feats, 3, heads_here, HDIM)
    wi = fc_in_weight.reshape(feats, 2, units // 2)
    wo = fc_out_weight.T.reshape(feats, 2, units // 2)
    wd = dense_weight.T.reshape(feats, 2, HDIM)

    def halves(which):
        pick = lambda v, ax: lax.dynamic_index_in_dim(v, which, ax, keepdims=False)
        return (
            jnp.concatenate([pick(wq, 2).reshape(feats, 3 * HDIM), pick(wd, 1)], axis=1),
            pick(wi, 1),
            pick(wo, 1),
        )

    x_b = pair_rows(tokens, i)
    mine, theirs = halves(i), halves(1 - i)
    full = []
    for own, other in zip(mine, theirs):
        back = swap(other)
        chunk = jnp.where(i == 0, jnp.concatenate([own, back], 0), jnp.concatenate([back, own], 0))
        full.append(gather_planes(chunk, d, dp))
    w_att, w_in, w_out = full
    w_qkv, w_dense = w_att[:, : 3 * HDIM], w_att[:, 3 * HDIM :]
    grad_b = pair_rows(grad_here, i)

    plane = 2 * rows
    start_row = d * plane
    x = x_b.astype(F32)
    mean = jnp.mean(x, axis=-1, keepdims=True)
    centred = x - mean
    spread = jnp.mean(centred * centred, axis=-1, keepdims=True)
    rstd = lax.rsqrt(spread + EPS)
    xhat = centred * rstd
    h_one = (xhat * gain1 + shift1).astype(BF16)
    h_two = (xhat * gain2 + shift2).astype(BF16)

    here = start_row + jnp.arange(plane, dtype=jnp.int32)
    docs_here, pos_here = locate(here, seq_starts)
    cosine, sine = rotary_tables(pos_here)
    qkv = plain(h_one, w_qkv) + b_qkv
    q = rotate(qkv[:, :HDIM], cosine, sine).astype(BF16)
    k = rotate(qkv[:, HDIM : 2 * HDIM], cosine, sine).astype(BF16)
    v = qkv[:, 2 * HDIM :].astype(BF16)
    reach = min(dp - 1, -(-(SEQ_LEN - 1) // plane))
    packed = jnp.concatenate([k, v], axis=1)
    window = [packed]
    for _ in range(reach):
        window.insert(0, planes(window[0], 1))
    window = jnp.concatenate(window, axis=0)
    span = window.shape[0]
    cols = start_row - reach * plane + jnp.arange(span, dtype=jnp.int32)
    docs_cols, _ = locate(cols, seq_starts)
    allowed = (cols[None, :] <= here[:, None]) & (docs_cols[None, :] == docs_here[:, None])
    key_win, value_win = window[:, :HDIM], window[:, HDIM:]
    masked = jnp.where(allowed, against(q, key_win) * scale, -1e30)
    top = jnp.max(masked, axis=1, keepdims=True)
    expo = jnp.exp(masked - top)
    probs = expo / jnp.sum(expo, axis=1, keepdims=True)
    probs_b = probs.astype(BF16)
    att_b = plain(probs_b, value_win).astype(BF16)

    pre = plain(h_two, w_in) + b_in
    act, gelu_pull = jax.vjp(lambda u: jax.nn.gelu(u, approximate=False), pre)
    act_b = act.astype(BF16)
    d_pre = gelu_pull(plain(grad_b, w_out))[0].astype(BF16)

    d_att = plain(grad_b, w_dense).astype(BF16)
    dprob = against(d_att, value_win)
    delta = jnp.sum(probs * dprob, axis=1, keepdims=True)
    dscore = (probs * (dprob - delta)).astype(BF16)
    dq = plain(dscore, key_win) * scale
    dk_win = inner(dscore, q) * scale
    dv_win = inner(probs_b, d_att)
    grads_win = jnp.concatenate([dk_win, dv_win], axis=1)
    held = None
    for r in range(reach):
        piece = grads_win[r * plane : (r + 1) * plane]
        moved = piece if held is None else piece + held
        held = planes(moved.astype(BF16), -1).astype(F32)
    dkv = grads_win[reach * plane :]
    if held is not None:
        dkv = dkv + held
    dq_raw = rotate(dq, cosine, -sine)
    dk_raw = rotate(dkv[:, :HDIM], cosine, -sine)
    d_qkv = jnp.concatenate([dq_raw, dk_raw, dkv[:, HDIM:]], axis=1).astype(BF16)

    partial_value = against(att_b, w_dense) + against(act_b, w_out)
    share = tp_scatter(partial_value, t, tps)
    share = half_of(share, i, 0) + swap(half_of(share, 1 - i, 0).astype(BF16)).astype(F32)
    part_w = width // tps
    offset = t * part_w
    cut = lambda vec: lax.dynamic_slice_in_dim(vec, offset, part_w, vec.ndim - 1)
    mixed = (cut(tokens).astype(F32) + share + cut(b_dense) + cut(b_out)).astype(BF16)

    g_out = reduce_planes(inner(grad_b, act_b), d, dp)
    g_in = reduce_planes(inner(h_two, d_pre), d, dp)
    g_att = reduce_planes(
        jnp.concatenate([inner(h_one, d_qkv), inner(grad_b, att_b)], axis=1), d, dp
    )
    e_two = against(d_pre, w_in)
    e_one = against(d_qkv, w_qkv)
    u = e_one * gain1 + e_two * gain2
    u_here = tp_scatter(u, t, tps)
    u_here = half_of(u_here, i, 0) + swap(half_of(u_here, 1 - i, 0).astype(BF16)).astype(F32)
    xhat_here = cut(half_of(xhat, i, 0))
    sums = jnp.stack([jnp.sum(u_here, axis=1), jnp.sum(u_here * xhat_here, axis=1)])
    sums = tp_sum(sums, tps) / width
    dx = half_of(rstd, i, 0) * (u_here - sums[0][:, None] - xhat_here * sums[1][:, None])
    tokens_grad = (cut(carried) + dx).astype(BF16)

    def pair_back(grad):
        own = half_of(grad, i, 0)
        got = swap(half_of(grad, 1 - i, 0).astype(BF16)).astype(F32)
        return jnp.where(i == 0, jnp.stack([own, got], 1), jnp.stack([got, own], 1))

    g_att, g_in, g_out = pair_back(g_att), pair_back(g_in), pair_back(g_out)
    qkv_weight_grad = (
        g_att[:, :, : 3 * HDIM].reshape(feats, 2, 3, HDIM).transpose(0, 2, 1, 3).reshape(feats, 3, head_cols)
    )
    dense_weight_grad = g_att[:, :, 3 * HDIM :].reshape(feats, head_cols).T
    fc_in_weight_grad = g_in.reshape(feats, units)
    fc_out_weight_grad = g_out.reshape(feats, units).T

    norms = jnp.stack(
        [
            jnp.sum(e_one * xhat, axis=0),
            jnp.sum(e_one, axis=0),
            jnp.sum(e_two * xhat, axis=0),
            jnp.sum(e_two, axis=0),
            jnp.sum(grad_here.astype(F32), axis=0),
        ]
    )
    norms = norms.reshape(5, shards, feats).transpose(1, 0, 2).reshape(shards, 5 * feats)
    in_b = jnp.where(jnp.arange(2)[:, None] == i, jnp.sum(d_pre.astype(F32), axis=0)[None], 0.0)
    in_b = in_b.reshape(ub[0], shards, ub[1]).transpose(1, 0, 2).reshape(shards, ub[0] * ub[1])
    qkv_b = jnp.sum(d_qkv.astype(F32), axis=0).reshape(3, 1, HDIM)
    qkv_b = jnp.where(jnp.arange(2)[None, :, None] == i, qkv_b, 0.0)
    qkv_b = qkv_b.reshape(3, 2, shards, hd).transpose(2, 0, 1, 3).reshape(shards, nq)
    small = jnp.concatenate([norms, in_b, qkv_b], axis=1)
    small = lax.psum_scatter(small, "fsdp", scatter_dimension=0, tiled=False)
    norm_grads = tp_sum(small[: 4 * feats].reshape(4, feats), tps)
    bias_grad = small[4 * feats : 5 * feats]
    in_bias_grad = small[5 * feats : 5 * feats + ub[0] * ub[1]].reshape(ub)
    qkv_bias_grad = small[5 * feats + ub[0] * ub[1] :].reshape(3, heads_here, hd)
    return (
        mixed,
        tokens_grad,
        qkv_weight_grad,
        qkv_bias_grad,
        dense_weight_grad,
        bias_grad,
        fc_in_weight_grad,
        in_bias_grad,
        fc_out_weight_grad,
        bias_grad,
        norm_grads[0],
        norm_grads[1],
        norm_grads[2],
        norm_grads[3],
    )


def solution(mesh):
    in_specs = (
        P("fsdp", None),
        P("fsdp", None, "tp"),
        P(None, "tp", "fsdp"),
        P("tp", "fsdp"),
        P("fsdp"),
        P("fsdp", "tp"),
        P("tp", "fsdp"),
        P("tp", "fsdp"),
        P("fsdp"),
        P("fsdp"),
        P("fsdp"),
        P("fsdp"),
        P("fsdp"),
        P("fsdp", None),
        P("fsdp"),
        P(),
    )
    out_specs = (
        P("fsdp", "tp"),
        P("fsdp", "tp"),
        P("fsdp", None, "tp"),
        P(None, "tp", "fsdp"),
        P("tp", "fsdp"),
        P("fsdp"),
        P("fsdp", "tp"),
        P("tp", "fsdp"),
        P("tp", "fsdp"),
        P("fsdp"),
        P("fsdp"),
        P("fsdp"),
        P("fsdp"),
        P("fsdp"),
    )
    return jax.shard_map(
        on_device, mesh=mesh, in_specs=in_specs, out_specs=out_specs, check_vma=False
    )
```

time: 2030 us -> 825 us (0.41)
  waiting for transfers between devices: 989 us -> 178 us
  blocking collectives: 742 us -> 138 us
  starting transfers between devices: 20.9 us -> 117 us
  local copies, waits for them, and re-layouts: 49.5 us -> 126 us
  other arithmetic: 47.5 us -> 119 us
    reduce_scatter x5 -> x0, waiting for transfers between devices: 868 us -> none  [the longest x1 287 us: on_device(): lax.psum_scatter(grads[3], 'fsdp', scatter_dimension=1, tiled=True)]
    all_gather x8 -> x0, blocking collectives: 630 us -> none  [the longest x1 387 us: on_device(): lax.all_gather(params[10], 'fsdp', axis=0, tiled=True)]
    ppermute x8 -> x58, waiting for transfers between devices: 18.3 us -> 178 us  [the longest x40 156 us: planes(): return lax.ppermute(value, 'fsdp', pairs)]
    unnamed x1 -> x2, blocking collectives: 37.9 us -> 138 us
    ppermute x8 -> x58, starting transfers between devices: 20.2 us -> 117 us  [the longest x40 100 us: planes(): return lax.ppermute(value, 'fsdp', pairs)]
    psum x1 -> x0, blocking collectives: 74.2 us -> none  [on_device(): counts = lax.psum(local_counts, 'fsdp').astype(f32)]
    psum x1 -> x0, waiting for transfers between devices: 72.6 us -> none  [on_device(): e_one, e_two = lax.psum((e_one, e_two), 'tp')]
    dynamic_slice x0 -> x10, local copies, waits for them, and re-layouts: none -> 34.4 us  [the longest x3 19.1 us: tp_scatter(): keep = lax.dynamic_index_in_dim(view, mine, 2, keepdims=False)]
  transfers between devices with their start and end apart: 19 -> 58, of which waited for: 7 -> 17; matrix products, arithmetic and copies ran while one was open for 12% -> 44% of each run, Pallas kernels for 0% -> 0%
where the time goes in v1:
time: 825 us; the launch traced here: 814 us
  waiting for transfers between devices  178 us (22%)
  blocking collectives  138 us (17%)
  matrix products  132 us (16%)
  local copies, waits for them, and re-layouts  126 us (15%)
  other arithmetic  119 us (14%)
  starting transfers between devices  117 us (14%)
    ppermute x40, waiting for transfers between devices, planes(): return lax.ppermute(value, 'fsdp', pairs)  156 us
    unnamed x2, blocking collectives  138 us
    dot_general x18, matrix products, mm(): lax.dot_general(left, right, (dims, ((), ())), preferred_element_type=F32)  132 us
    ppermute x40, starting transfers between devices, planes(): return lax.ppermute(value, 'fsdp', pairs)  100 us
    unnamed x200, local copies, waits for them, and re-layouts  31 us
    convert_element_type x9, other arithmetic, reduce_planes(): held = planes(value.astype(BF16), sign, k)  28.9 us
    ppermute x10, waiting for transfers between devices, swap(): return lax.ppermute(value, 'fsdp', [(s, s ^ 1) for s in range(count)])  21.1 us
    dynamic_slice x3, local copies, waits for them, and re-layouts, tp_scatter(): keep = lax.dynamic_index_in_dim(view, mine, 2, keepdims=False)  19.1 us
  transfers between devices with their start and end apart: 58, of which 17 were waited for; matrix products, arithmetic and copies ran while one was open for 44% of the time, Pallas kernels for 0%

profile of v1, /device:TPU:0, one launch (start us, length us, event | category | flops | bytes accessed | tf_op | source)
XLA Modules:
  0.0 814.4 jit_solution(11420967097998103635)
XLA Ops:
  20.6 97.4 %all-reduce = f32[16048]{0:T(1024)S(1)} all-reduce(f32[16048]{0:T(1024)S(1)} %dynamic-update-slice), channel_id=2, replica_groups=mesh['fsdp'=8,'tp'=4] {'fsdp'}, use_global_device_ids=true, to_apply=%add | all-reduce | flops 16048 | bytes 128384
  118.3 4.8 convert_reduce_fusion.2
  134.6 4.6 collective-permute-start.2
  142.7 18.2 %collective-permute-done.3 = bf16[512,1024]{0,1:T(8,128)(2,1)S(1)} collective-permute-done((bf16[512,1024]{0,1:T(8,128)(2,1)S(1)}, bf16[512,1024]{0,1:T(8,128)(2,1)S(1)}, u32[]{:S(2)}, u32[]{:S(2)}) %collective-permute-start.3) | collective-permute-done | bytes 1048608 | tf_op jit(solution)/shard_map/ppermute | solution.py:71
  173.7 4.6 collective-permute-start.11
  178.3 5.1 collective-permute-done.19
  184.9 21.0 %collective-permute-done.4 = bf16[512,1024]{0,1:T(8,128)(2,1)S(1)} collective-permute-done((bf16[512,1024]{0,1:T(8,128)(2,1)S(1)}, bf16[512,1024]{0,1:T(8,128)(2,1)S(1)}, u32[]{:S(2)}, u32[]{:S(2)}) %collective-permute-start.4) | collective-permute-done | bytes 1048608 | tf_op jit(solution)/shard_map/ppermute | solution.py:71
  212.5 15.8 %collective-permute-done.12 = bf16[512,1024]{0,1:T(8,128)(2,1)S(1)} collective-permute-done((bf16[512,1024]{0,1:T(8,128)(2,1)S(1)}, bf16[512,1024]{0,1:T(8,128)(2,1)S(1)}, u32[]{:S(2)}, u32[]{:S(2)}) %collective-permute-start.12) | collective-permute-done | bytes 1048608 | tf_op jit(solution)/shard_map/ppermute | solution.py:71
  232.0 5.5 collective-permute-start.15
  237.5 13.2 %collective-permute-done.5 = bf16[512,1024]{0,1:T(8,128)(2,1)S(1)} collective-permute-done((bf16[512,1024]{0,1:T(8,128)(2,1)S(1)}, bf16[512,1024]{0,1:T(8,128)(2,1)S(1)}, u32[]{:S(2)}, u32[]{:S(2)}) %collective-permute-start.5) | collective-permute-done | bytes 1048608 | tf_op jit(solution)/shard_map/ppermute | solution.py:71
  252.3 5.5 fusion.2
  258.6 14.7 %collective-permute-done.20 = bf16[512,1024]{0,1:T(8,128)(2,1)} collective-permute-done((bf16[512,1024]{0,1:T(8,128)(2,1)S(1)}, bf16[512,1024]{0,1:T(8,128)(2,1)}, u32[]{:S(2)}, u32[]{:S(2)}) %collective-permute-start.20) | collective-permute-done | bytes 1048608 | tf_op jit(solution)/shard_map/ppermute | solution.py:71
  274.7 21.2 %collective-permute-done.13 = bf16[512,1024]{0,1:T(8,128)(2,1)} collective-permute-done((bf16[512,1024]{0,1:T(8,128)(2,1)S(1)}, bf16[512,1024]{0,1:T(8,128)(2,1)}, u32[]{:S(2)}, u32[]{:S(2)}) %collective-permute-start.13) | collective-permute-done | bytes 1048608 | tf_op jit(solution)/shard_map/ppermute | solution.py:71
  299.5 6.0 collective-permute-start.16
  305.9 9.1 %fusion.129 = (bf16[1024,768]{0,1:T(8,128)(2,1)S(1)}, f32[1024,768]{0,1:T(8,128)}) fusion(f32[768]{0:T(1024)S(1)} %copy-done.66, bf16[2048,1024]{0,1:T(8,128)(2,1)S(1)} %select_dynamic-update-slice_fusion.6, f32[2048]{0:T(1024)S(1)} %bitcast.185, f32[2048]{0:T(1024)S(1)} %bitcast.182, f32[1024]{0:T(1024)S(1)} %add_rsqrt_fusion, ...), kind=kOutput, calls=%fused_computation.282 | convolution fusion | flops 3254255616 | bytes 12087297 | tf_op jit(solution)/shard_map/dot_general | solution.py:18
  318.5 14.1 %collective-permute-done.14 = bf16[512,1024]{0,1:T(8,128)(2,1)} collective-permute-done((bf16[512,1024]{0,1:T(8,128)(2,1)}, bf16[512,1024]{0,1:T(8,128)(2,1)}, u32[]{:S(2)}, u32[]{:S(2)}) %collective-permute-start.14) | collective-permute-done | bytes 1048608 | tf_op jit(solution)/shard_map/ppermute | solution.py:71
  342.1 20.9 %multiply_convert_fusion.1 = (bf16[1024,1024]{1,0:T(8,128)(2,1)}, f32[1024,1024]{1,0:T(8,128)}, f32[1024,1024]{1,0:T(8,128)}) fusion(f32[1024]{0:T(1024)S(1)} %copy-done.67, bf16[2048,1024]{0,1:T(8,128)(2,1)S(1)} %select_dynamic-update-slice_fusion.3, f32[2048]{0:T(1024)S(1)} %bitcast.190, f32[2048]{0:T(1024)S(1)} %bitcast.187, ...), kind=kOutput, calls=%fused_computation.46 | convolution fusion | flops 4395630592 | bytes 18903040 | tf_op jit(solution)/shard_map/dot_general | solution.py:18
  363.0 7.6 fusion.118
  372.4 5.5 collective-permute-start.49
  381.6 12.0 %convert_reduce_fusion.1 = (f32[1024]{0:T(1024)S(1)}, bf16[1024,1024]{1,0:T(8,128)(2,1)}) fusion(f32[1024,1024]{1,0:T(8,128)} %get-tuple-element.99, bf16[2048,1024]{0,1:T(8,128)(2,1)S(1)} %select_dynamic-update-slice_fusion, bf16[512,2048]{1,0:T(8,128)(2,1)} %collective-permute-done.27, bf16[512,2048]{1,0:T(8,128)(2,1)S(1)} %copy-done.26, pred[]{:T(512)S(6)} %eq.70, ...), kind=kOutput, calls=%fused_computation.42 | convolution fusion | flops 4331666432 | bytes 18882560 | tf_op jit(solution)/shard_map/dot_general | solution.py:18
  393.6 8.2 %fusion.115 = f32[2048,1024]{0,1:T(8,128)S(1)} fusion(bf16[1024,1024]{1,0:T(8,128)(2,1)} %get-tuple-element.156, f32[2048]{0:T(1024)S(1)} %bitcast.191, f32[2048]{0:T(1024)S(1)} %bitcast.188, f32[1024]{0:T(1024)S(1)} %add_rsqrt_fusion, f32[1024]{0:T(1024)S(1)} %broadcast_multiply_fusion, bf16[512,2048]{1,0:T(8,128)(2,1)} %collective-permute-done, ...), kind=kOutput, calls=%fused_computation.271 | convolution fusion | flops 4326424576 | bytes 14704641 | tf_op jit(solution)/shard_map/dot_general | solution.py:18
  405.9 6.7 fusion.131
  419.0 4.8 convolution_convert_fusion
  432.6 5.3 collective-permute-start.43
  437.8 13.5 %collective-permute-done.9 = bf16[1024,512]{0,1:T(8,128)(2,1)S(1)} collective-permute-done((bf16[1024,512]{0,1:T(8,128)(2,1)}, bf16[1024,512]{0,1:T(8,128)(2,1)S(1)}, u32[]{:S(2)}, u32[]{:S(2)}) %collective-permute-start.9) | collective-permute-done | bytes 1048608 | tf_op jit(solution)/shard_map/ppermute | solution.py:71
  465.1 9.5 %multiply_reduce_fusion = (f32[1024]{0:T(1024)S(1)}, f32[1024,3072]{1,0:T(8,128)S(1)}, f32[1024,3072]{1,0:T(8,128)}) fusion(f32[1024]{0:T(1024)S(1)} %fusion.1, f32[1024,3072]{1,0:T(8,128)} %copy-done.14, f32[1024]{0:T(1024)S(1)} %get-tuple-element.152, bf16[1024,256]{1,0:T(8,128)(2,1)S(1)} %copy-done.35, bf16[3072,512]{0,1:T(8,128)(2,1)} %copy-done.17), kind=kOutput, calls=%fused_computation.8 | convolution fusion | flops 1623194624 | bytes 39858176 | tf_op jit(solution)/shard_map/dot_general | solution.py:18
  480.4 5.4 multiply_convert_fusion
  485.8 4.7 convolution_multiply_fusion
  503.3 4.9 collective-permute-start.51
  522.4 6.0 convolution_add_fusion
  528.4 11.9 %reshape_reshape.6 = f32[1024,2,2,512]{3,2,1,0:T(2,128)} reshape(f32[1024,2048]{1,0:T(8,128)} %convolution_add_fusion) | data formatting | bytes 16777216 | tf_op jit(solution)/shard_map/reshape;reshape | solution.py:113
  540.2 6.2 fusion.119
  546.4 9.3 %constant_dynamic-slice_fusion.2 = bf16[1024,2,1,512]{3,2,1,0:T(2,128)(2,1)} fusion(f32[1024,2,2,512]{3,2,1,0:T(2,128)} %reshape_reshape.6, s32[]{:T(128)S(6)} %select_n.283), kind=kLoop, calls=%fused_computation.232 | loop fusion | bytes 4194308 | tf_op jit(solution)/shard_map/jit(dynamic_index_in_dim)/dynamic_slice | solution.py:116
  564.0 8.9 %constant_dynamic-slice_fusion.3 = f32[1024,2,1,512]{3,2,1,0:T(1,128)} fusion(f32[1024,2,2,512]{3,2,1,0:T(2,128)} %reshape_reshape.6, s32[]{:T(128)S(6)} %select_n.282), kind=kLoop, calls=%fused_computation.233 | loop fusion | bytes 8388612 | tf_op jit(solution)/shard_map/jit(dynamic_index_in_dim)/dynamic_slice | solution.py:115
  587.8 5.1 fusion.15
  594.6 13.2 %fusion.121 = (f32[2048]{0:T(1024)S(1)}, f32[2048]{0:T(1024)S(1)}, f32[1024,2048]{1,0:T(8,128)}, f32[2048]{0:T(1024)S(1)}, f32[2048]{0:T(1024)S(1)}) fusion(f32[1024]{0:T(1024)S(1)} %copy-done.46, f32[1024]{0:T(1024)S(1)} %broadcast_multiply_fusion, bf16[512,2048]{1,0:T(8,128)(2,1)S(1)} %copy-done.6, bf16[512,2048]{1,0:T(8,128)(2,1)} %collective-permute-done, ...), kind=kOutput, calls=%fused_computation.277 | convolution fusion | flops 4338999296 | bytes 27320320 | tf_op jit(solution)/shard_map/dot_general | solution.py:18
  608.0 7.7 fusion.117
  615.9 41.1 %all-reduce.1 = f32[8,1728]{1,0:T(8,128)S(1)} all-reduce(f32[8,1728]{1,0:T(8,128)S(1)} %pad_maximum_fusion.6), channel_id=3, replica_groups=mesh['fsdp'=8,'tp'=4] {'fsdp'}, use_global_device_ids=true, to_apply=%region_20.21.clone | all-reduce | flops 13824 | bytes 110592
  657.7 9.3 %copy.102 = f32[1024,2048]{0,1:T(8,128)} copy(f32[1024,2048]{1,0:T(8,128)} %get-tuple-element.110) | data formatting | bytes 16777216 | tf_op jit(solution)/shard_map/add | solution.py:302
  685.9 4.8 constant_dynamic-slice_fusion.1
  700.6 5.4 copy.103
  725.2 8.1 collective-permute-done.48
  738.5 6.0 collective-permute-done.36
  746.6 6.6 collective-permute-start.37
  769.1 4.7 collective-permute-done.37
  773.9 5.1 collective-permute-done.40
  784.3 6.4 collective-permute-done.32
  792.8 6.6 collective-permute-done.41
  (448 shorter events, 268.8 us)
Async XLA Ops:
  4.8 125.8 %collective-permute-start.1 = (bf16[256,1024]{0,1:T(8,128)(2,1)}, bf16[256,1024]{0,1:T(8,128)(2,1)}, u32[]{:S(2)}, u32[]{:S(2)}) collective-permute-start(bf16[256,1024]{0,1:T(8,128)(2,1)} %pad_maximum_fusion.2), channel_id=1, source_target_pairs={{0,4},{4,0},{8,12},{12,8},{16,20},{20,16},{24,28},{28,24},{1,5},{5... | collective-permute-start | bytes 1572872 | tf_op jit(solution)/shard_map/ppermute | solution.py:60
  7.8 161.7 %collective-permute-start = (bf16[512,2048]{1,0:T(8,128)(2,1)S(1)}, bf16[512,2048]{1,0:T(8,128)(2,1)}, u32[]{:S(2)}, u32[]{:S(2)}) collective-permute-start(bf16[512,2048]{1,0:T(8,128)(2,1)S(1)} %copy-done.5), channel_id=1, source_target_pairs={{0,4},{4,0},{8,12},{12,8},{16,20},{20,16},{24,28},{28,24},{1,5},{5... | collective-permute-start | bytes 6291464 | tf_op jit(solution)/shard_map/ppermute | solution.py:60
  10.0 129.2 %collective-permute-start.17 = (bf16[256,1024]{0,1:T(8,128)(2,1)}, bf16[256,1024]{0,1:T(8,128)(2,1)}, u32[]{:S(2)}, u32[]{:S(2)}) collective-permute-start(bf16[256,1024]{0,1:T(8,128)(2,1)} %get-tuple-element.124), channel_id=1, source_target_pairs={{0,4},{4,0},{8,12},{12,8},{16,20},{20,16},{24,28},{28,24},{1,5},{5... | collective-permute-start | bytes 1572872 | tf_op jit(solution)/shard_map/ppermute | solution.py:60
  14.6 148.2 %collective-permute-start.10 = (bf16[256,1024]{0,1:T(8,128)(2,1)}, bf16[256,1024]{0,1:T(8,128)(2,1)}, u32[]{:S(2)}, u32[]{:S(2)}) collective-permute-start(bf16[256,1024]{0,1:T(8,128)(2,1)} %get-tuple-element.126), channel_id=1, source_target_pairs={{0,4},{4,0},{8,12},{12,8},{16,20},{20,16},{24,28},{28,24},{1,5},{5... | collective-permute-start | bytes 1572872 | tf_op jit(solution)/shard_map/ppermute | solution.py:60
  132.9 28.0 %collective-permute-start.3 = (bf16[512,1024]{0,1:T(8,128)(2,1)S(1)}, bf16[512,1024]{0,1:T(8,128)(2,1)S(1)}, u32[]{:S(2)}, u32[]{:S(2)}) collective-permute-start(bf16[512,1024]{0,1:T(8,128)(2,1)S(1)} %get-tuple-element.95), channel_id=1, source_target_pairs={{8,0},{12,4},{16,8},{20,12},{24,16},{28,20},{9,1},{13,5},{17,9},{2... | collective-permute-start | bytes 3145736 | tf_op jit(solution)/shard_map/ppermute | solution.py:71
  134.6 39.1 %collective-permute-start.2 = (bf16[512,1024]{0,1:T(8,128)(2,1)S(1)}, bf16[512,1024]{0,1:T(8,128)(2,1)S(1)}, u32[]{:S(2)}, u32[]{:S(2)}) collective-permute-start(bf16[512,1024]{0,1:T(8,128)(2,1)S(1)} %get-tuple-element.95), channel_id=1, source_target_pairs={{0,8},{4,12},{8,16},{12,20},{16,24},{20,28},{1,9},{5,13},{9,17},{1... | collective-permute-start | bytes 3145736 | tf_op jit(solution)/shard_map/ppermute | solution.py:71
  141.4 42.0 %collective-permute-start.19 = (bf16[512,1024]{0,1:T(8,128)(2,1)S(1)}, bf16[512,1024]{0,1:T(8,128)(2,1)S(1)}, u32[]{:S(2)}, u32[]{:S(2)}) collective-permute-start(bf16[512,1024]{0,1:T(8,128)(2,1)S(1)} %get-tuple-element.97), channel_id=1, source_target_pairs={{8,0},{12,4},{16,8},{20,12},{24,16},{28,20},{9,1},{13,5},{17,9},{2... | collective-permute-start | bytes 3145736 | tf_op jit(solution)/shard_map/ppermute | solution.py:71
  160.9 44.9 %collective-permute-start.4 = (bf16[512,1024]{0,1:T(8,128)(2,1)S(1)}, bf16[512,1024]{0,1:T(8,128)(2,1)S(1)}, u32[]{:S(2)}, u32[]{:S(2)}) collective-permute-start(bf16[512,1024]{0,1:T(8,128)(2,1)S(1)} %collective-permute-done.3), channel_id=1, source_target_pairs={{8,0},{12,4},{16,8},{20,12},{24,16},{28,20},{9,1},{13,5},{17,9},{2... | collective-permute-start | bytes 3145736 | tf_op jit(solution)/shard_map/ppermute | solution.py:71
  162.8 48.4 %collective-permute-start.18 = (bf16[512,1024]{0,1:T(8,128)(2,1)S(1)}, bf16[512,1024]{0,1:T(8,128)(2,1)S(1)}, u32[]{:S(2)}, u32[]{:S(2)}) collective-permute-start(bf16[512,1024]{0,1:T(8,128)(2,1)S(1)} %get-tuple-element.97), channel_id=1, source_target_pairs={{0,8},{4,12},{8,16},{12,20},{16,24},{20,28},{1,9},{5,13},{9,17},{1... | collective-permute-start | bytes 3145736 | tf_op jit(solution)/shard_map/ppermute | solution.py:71
  169.5 58.8 %collective-permute-start.12 = (bf16[512,1024]{0,1:T(8,128)(2,1)S(1)}, bf16[512,1024]{0,1:T(8,128)(2,1)S(1)}, u32[]{:S(2)}, u32[]{:S(2)}) collective-permute-start(bf16[512,1024]{0,1:T(8,128)(2,1)S(1)} %get-tuple-element.101), channel_id=1, source_target_pairs={{8,0},{12,4},{16,8},{20,12},{24,16},{28,20},{9,1},{13,5},{17,9},{2... | collective-permute-start | bytes 3145736 | tf_op jit(solution)/shard_map/ppermute | solution.py:71
  173.7 57.0 %collective-permute-start.11 = (bf16[512,1024]{0,1:T(8,128)(2,1)S(1)}, bf16[512,1024]{0,1:T(8,128)(2,1)S(1)}, u32[]{:S(2)}, u32[]{:S(2)}) collective-permute-start(bf16[512,1024]{0,1:T(8,128)(2,1)S(1)} %get-tuple-element.101), channel_id=1, source_target_pairs={{0,8},{4,12},{8,16},{12,20},{16,24},{20,28},{1,9},{5,13},{9,17},{1... | collective-permute-start | bytes 3145736 | tf_op jit(solution)/shard_map/ppermute | solution.py:71
  183.4 48.6 %collective-permute-start.6 = (bf16[512,1024]{0,1:T(8,128)(2,1)S(1)}, bf16[512,1024]{0,1:T(8,128)(2,1)S(1)}, u32[]{:S(2)}, u32[]{:S(2)}) collective-permute-start(bf16[512,1024]{0,1:T(8,128)(2,1)S(1)} %collective-permute-done.2), channel_id=1, source_target_pairs={{0,8},{4,12},{8,16},{12,20},{16,24},{20,28},{1,9},{5,13},{9,17},{1... | collective-permute-start | bytes 3145736 | tf_op jit(solution)/shard_map/ppermute | solution.py:71
  205.8 44.9 %collective-permute-start.5 = (bf16[512,1024]{0,1:T(8,128)(2,1)S(1)}, bf16[512,1024]{0,1:T(8,128)(2,1)S(1)}, u32[]{:S(2)}, u32[]{:S(2)}) collective-permute-start(bf16[512,1024]{0,1:T(8,128)(2,1)S(1)} %collective-permute-done.4), channel_id=1, source_target_pairs={{8,0},{12,4},{16,8},{20,12},{24,16},{28,20},{9,1},{13,5},{17,9},{2... | collective-permute-start | bytes 3145736 | tf_op jit(solution)/shard_map/ppermute | solution.py:71
  211.2 62.1 %collective-permute-start.20 = (bf16[512,1024]{0,1:T(8,128)(2,1)S(1)}, bf16[512,1024]{0,1:T(8,128)(2,1)}, u32[]{:S(2)}, u32[]{:S(2)}) collective-permute-start(bf16[512,1024]{0,1:T(8,128)(2,1)S(1)} %collective-permute-done.19), channel_id=1, source_target_pairs={{8,0},{12,4},{16,8},{20,12},{24,16},{28,20},{9,1},{13,5},{17,9},{2... | collective-permute-start | bytes 3145736 | tf_op jit(solution)/shard_map/ppermute | solution.py:71
  228.3 45.1 %collective-permute-start.22 = (bf16[512,1024]{0,1:T(8,128)(2,1)S(1)}, bf16[512,1024]{0,1:T(8,128)(2,1)}, u32[]{:S(2)}, u32[]{:S(2)}) collective-permute-start(bf16[512,1024]{0,1:T(8,128)(2,1)S(1)} %collective-permute-done.18), channel_id=1, source_target_pairs={{0,8},{4,12},{8,16},{12,20},{16,24},{20,28},{1,9},{5,13},{9,17},{1... | collective-permute-start | bytes 3145736 | tf_op jit(solution)/shard_map/ppermute | solution.py:71
  230.7 65.1 %collective-permute-start.13 = (bf16[512,1024]{0,1:T(8,128)(2,1)S(1)}, bf16[512,1024]{0,1:T(8,128)(2,1)}, u32[]{:S(2)}, u32[]{:S(2)}) collective-permute-start(bf16[512,1024]{0,1:T(8,128)(2,1)S(1)} %collective-permute-done.12), channel_id=1, source_target_pairs={{8,0},{12,4},{16,8},{20,12},{24,16},{28,20},{9,1},{13,5},{17,9},{2... | collective-permute-start | bytes 3145736 | tf_op jit(solution)/shard_map/ppermute | solution.py:71
  232.0 66.1 %collective-permute-start.15 = (bf16[512,1024]{0,1:T(8,128)(2,1)S(1)}, bf16[512,1024]{0,1:T(8,128)(2,1)}, u32[]{:S(2)}, u32[]{:S(2)}) collective-permute-start(bf16[512,1024]{0,1:T(8,128)(2,1)S(1)} %collective-permute-done.11), channel_id=1, source_target_pairs={{0,8},{4,12},{8,16},{12,20},{16,24},{20,28},{1,9},{5,13},{9,17},{1... | collective-permute-start | bytes 3145736 | tf_op jit(solution)/shard_map/ppermute | solution.py:71
  250.8 48.7 %collective-permute-start.7 = (bf16[512,1024]{0,1:T(8,128)(2,1)S(1)}, bf16[512,1024]{0,1:T(8,128)(2,1)S(1)}, u32[]{:S(2)}, u32[]{:S(2)}) collective-permute-start(bf16[512,1024]{0,1:T(8,128)(2,1)S(1)} %collective-permute-done.6), channel_id=1, source_target_pairs={{0,8},{4,12},{8,16},{12,20},{16,24},{20,28},{1,9},{5,13},{9,17},{1... | collective-permute-start | bytes 3145736 | tf_op jit(solution)/shard_map/ppermute | solution.py:71
  273.3 89.7 %collective-permute-start.27 = (bf16[512,2048]{1,0:T(8,128)(2,1)S(1)}, bf16[512,2048]{1,0:T(8,128)(2,1)}, u32[]{:S(2)}, u32[]{:S(2)}) collective-permute-start(bf16[512,2048]{1,0:T(8,128)(2,1)S(1)} %copy-done.26), channel_id=1, source_target_pairs={{0,4},{4,0},{8,12},{12,8},{16,20},{20,16},{24,28},{28,24},{1,5},{5... | collective-permute-start | bytes 6291464 | tf_op jit(solution)/shard_map/ppermute | solution.py:60
  273.4 104.6 %collective-permute-start.21 = (bf16[512,1024]{0,1:T(8,128)(2,1)}, bf16[512,1024]{0,1:T(8,128)(2,1)}, u32[]{:S(2)}, u32[]{:S(2)}) collective-permute-start(bf16[512,1024]{0,1:T(8,128)(2,1)} %collective-permute-done.20), channel_id=1, source_target_pairs={{8,0},{12,4},{16,8},{20,12},{24,16},{28,20},{9,1},{13,5},{17,9},{2... | collective-permute-start | bytes 3145736 | tf_op jit(solution)/shard_map/ppermute | solution.py:71
  295.8 85.4 %collective-permute-start.23 = (bf16[512,1024]{0,1:T(8,128)(2,1)}, bf16[512,1024]{0,1:T(8,128)(2,1)}, u32[]{:S(2)}, u32[]{:S(2)}) collective-permute-start(bf16[512,1024]{0,1:T(8,128)(2,1)} %collective-permute-done.22), channel_id=1, source_target_pairs={{0,8},{4,12},{8,16},{12,20},{16,24},{20,28},{1,9},{5,13},{9,17},{1... | collective-permute-start | bytes 3145736 | tf_op jit(solution)/shard_map/ppermute | solution.py:71
  298.2 34.5 %collective-permute-start.14 = (bf16[512,1024]{0,1:T(8,128)(2,1)}, bf16[512,1024]{0,1:T(8,128)(2,1)}, u32[]{:S(2)}, u32[]{:S(2)}) collective-permute-start(bf16[512,1024]{0,1:T(8,128)(2,1)} %collective-permute-done.13), channel_id=1, source_target_pairs={{8,0},{12,4},{16,8},{20,12},{24,16},{28,20},{9,1},{13,5},{17,9},{2... | collective-permute-start | bytes 3145736 | tf_op jit(solution)/shard_map/ppermute | solution.py:71
  299.5 42.2 %collective-permute-start.16 = (bf16[512,1024]{0,1:T(8,128)(2,1)}, bf16[512,1024]{0,1:T(8,128)(2,1)}, u32[]{:S(2)}, u32[]{:S(2)}) collective-permute-start(bf16[512,1024]{0,1:T(8,128)(2,1)} %collective-permute-done.15), channel_id=1, source_target_pairs={{0,8},{4,12},{8,16},{12,20},{16,24},{20,28},{1,9},{5,13},{9,17},{1... | collective-permute-start | bytes 3145736 | tf_op jit(solution)/shard_map/ppermute | solution.py:71
  332.6 85.0 %collective-permute-start.8 = (bf16[1024,512]{0,1:T(8,128)(2,1)}, bf16[1024,512]{0,1:T(8,128)(2,1)}, u32[]{:S(2)}, u32[]{:S(2)}) collective-permute-start(bf16[1024,512]{0,1:T(8,128)(2,1)} %pad_maximum_fusion.1), channel_id=1, source_target_pairs={{0,8},{4,12},{8,16},{12,20},{16,24},{20,28},{1,9},{5,13},{9,17},{1... | collective-permute-start | bytes 3145736 | tf_op jit(solution)/shard_map/ppermute | solution.py:71
  372.4 51.3 %collective-permute-start.49 = (bf16[512,1024]{0,1:T(8,128)(2,1)}, bf16[512,1024]{0,1:T(8,128)(2,1)}, u32[]{:S(2)}, u32[]{:S(2)}) collective-permute-start(bf16[512,1024]{0,1:T(8,128)(2,1)} %get-tuple-element.104), channel_id=1, source_target_pairs={{0,8},{4,12},{1,9},{5,13},{2,10},{6,14},{3,11},{7,15}} | collective-permute-start | bytes 3145736 | tf_op jit(solution)/shard_map/ppermute | solution.py:71
  403.5 25.8 %collective-permute-start.42 = (bf16[512,1024]{0,1:T(8,128)(2,1)}, bf16[512,1024]{0,1:T(8,128)(2,1)}, u32[]{:S(2)}, u32[]{:S(2)}) collective-permute-start(bf16[512,1024]{0,1:T(8,128)(2,1)} %get-tuple-element.108), channel_id=1, source_target_pairs={{0,8},{4,12},{1,9},{5,13},{2,10},{6,14},{3,11},{7,15}} | collective-permute-start | bytes 3145736 | tf_op jit(solution)/shard_map/ppermute | solution.py:71
  414.3 81.6 %collective-permute-start.52 = (bf16[512,1024]{0,1:T(8,128)(2,1)}, bf16[512,1024]{0,1:T(8,128)(2,1)}, u32[]{:S(2)}, u32[]{:S(2)}) collective-permute-start(bf16[512,1024]{0,1:T(8,128)(2,1)} %get-tuple-element.105), channel_id=1, source_target_pairs={{24,16},{28,20},{25,17},{29,21},{26,18},{30,22},{27,19},{31,23}} | collective-permute-start | bytes 3145736 | tf_op jit(solution)/shard_map/ppermute | solution.py:71
  416.0 96.8 %collective-permute-start.45 = (bf16[512,1024]{0,1:T(8,128)(2,1)}, bf16[512,1024]{0,1:T(8,128)(2,1)}, u32[]{:S(2)}, u32[]{:S(2)}) collective-permute-start(bf16[512,1024]{0,1:T(8,128)(2,1)} %get-tuple-element.109), channel_id=1, source_target_pairs={{24,16},{28,20},{25,17},{29,21},{26,18},{30,22},{27,19},{31,23}} | collective-permute-start | bytes 3145736 | tf_op jit(solution)/shard_map/ppermute | solution.py:71
  417.6 33.8 %collective-permute-start.9 = (bf16[1024,512]{0,1:T(8,128)(2,1)}, bf16[1024,512]{0,1:T(8,128)(2,1)S(1)}, u32[]{:S(2)}, u32[]{:S(2)}) collective-permute-start(bf16[1024,512]{0,1:T(8,128)(2,1)} %collective-permute-done.8), channel_id=1, source_target_pairs={{0,8},{4,12},{8,16},{12,20},{16,24},{20,28},{1,9},{5,13},{9,17},{1... | collective-permute-start | bytes 3145736 | tf_op jit(solution)/shard_map/ppermute | solution.py:71
  427.0 68.8 %collective-permute-start.50 = (bf16[512,1024]{0,1:T(8,128)(2,1)}, bf16[512,1024]{0,1:T(8,128)(2,1)}, u32[]{:S(2)}, u32[]{:S(2)}) collective-permute-start(bf16[512,1024]{0,1:T(8,128)(2,1)} %add_convert_fusion.6), channel_id=1, source_target_pairs={{0,8},{4,12},{8,16},{12,20},{1,9},{5,13},{9,17},{13,21},{2,10},{6,... | collective-permute-start | bytes 3145736 | tf_op jit(solution)/shard_map/ppermute | solution.py:71
  432.6 80.2 %collective-permute-start.43 = (bf16[512,1024]{0,1:T(8,128)(2,1)}, bf16[512,1024]{0,1:T(8,128)(2,1)}, u32[]{:S(2)}, u32[]{:S(2)}) collective-permute-start(bf16[512,1024]{0,1:T(8,128)(2,1)} %add_convert_fusion.10), channel_id=1, source_target_pairs={{0,8},{4,12},{8,16},{12,20},{1,9},{5,13},{9,17},{13,21},{2,10},{6,... | collective-permute-start | bytes 3145736 | tf_op jit(solution)/shard_map/ppermute | solution.py:71
  491.7 64.0 %collective-permute-start.28 = (bf16[1024,512]{0,1:T(8,128)(2,1)}, bf16[1024,512]{0,1:T(8,128)(2,1)}, u32[]{:S(2)}, u32[]{:S(2)}) collective-permute-start(bf16[1024,512]{0,1:T(8,128)(2,1)} %fusion.44), channel_id=1, source_target_pairs={{8,0},{12,4},{16,8},{20,12},{24,16},{28,20},{9,1},{13,5},{17,9},{2... | collective-permute-start | bytes 3145736 | tf_op jit(solution)/shard_map/ppermute | solution.py:71
  501.6 71.3 %collective-permute-start.53 = (bf16[512,1024]{0,1:T(8,128)(2,1)}, bf16[512,1024]{0,1:T(8,128)(2,1)}, u32[]{:S(2)}, u32[]{:S(2)}) collective-permute-start(bf16[512,1024]{0,1:T(8,128)(2,1)} %get-tuple-element.103), channel_id=1, source_target_pairs={{16,8},{20,12},{24,16},{28,20},{17,9},{21,13},{25,17},{29,21},{18,... | collective-permute-start | bytes 3145736 | tf_op jit(solution)/shard_map/ppermute | solution.py:71
  503.3 175.2 %collective-permute-start.51 = (bf16[512,1024]{0,1:T(8,128)(2,1)}, bf16[512,1024]{0,1:T(8,128)(2,1)}, u32[]{:S(2)}, u32[]{:S(2)}) collective-permute-start(bf16[512,1024]{0,1:T(8,128)(2,1)} %get-tuple-element.102), channel_id=1, source_target_pairs={{0,8},{4,12},{8,16},{12,20},{16,24},{20,28},{1,9},{5,13},{9,17},{1... | collective-permute-start | bytes 3145736 | tf_op jit(solution)/shard_map/ppermute | solution.py:71
  516.5 59.8 %collective-permute-start.46 = (bf16[512,1024]{0,1:T(8,128)(2,1)}, bf16[512,1024]{0,1:T(8,128)(2,1)}, u32[]{:S(2)}, u32[]{:S(2)}) collective-permute-start(bf16[512,1024]{0,1:T(8,128)(2,1)} %get-tuple-element.107), channel_id=1, source_target_pairs={{16,8},{20,12},{24,16},{28,20},{17,9},{21,13},{25,17},{29,21},{18,... | collective-permute-start | bytes 3145736 | tf_op jit(solution)/shard_map/ppermute | solution.py:71
  518.1 172.7 %collective-permute-start.44 = (bf16[512,1024]{0,1:T(8,128)(2,1)}, bf16[512,1024]{0,1:T(8,128)(2,1)}, u32[]{:S(2)}, u32[]{:S(2)}) collective-permute-start(bf16[512,1024]{0,1:T(8,128)(2,1)} %get-tuple-element.106), channel_id=1, source_target_pairs={{0,8},{4,12},{8,16},{12,20},{16,24},{20,28},{1,9},{5,13},{9,17},{1... | collective-permute-start | bytes 3145736 | tf_op jit(solution)/shard_map/ppermute | solution.py:71
  572.9 135.0 %collective-permute-start.24 = (bf16[1024,2,512]{2,0,1:T(8,128)(2,1)}, bf16[1024,2,512]{2,0,1:T(8,128)(2,1)}, u32[]{:S(2)}, u32[]{:S(2)}) collective-permute-start(bf16[1024,2,512]{2,0,1:T(8,128)(2,1)} %bitcast.160), channel_id=1, source_target_pairs={{0,1},{1,0},{2,3},{3,2},{4,5},{5,4},{6,7},{7,6},{8,9},{9,8},{10,11... | collective-permute-start | bytes 6291464 | tf_op jit(solution)/shard_map/ppermute | solution.py:117
  576.3 102.2 %collective-permute-start.54 = (bf16[512,1024]{0,1:T(8,128)(2,1)}, bf16[512,1024]{0,1:T(8,128)(2,1)}, u32[]{:S(2)}, u32[]{:S(2)}) collective-permute-start(bf16[512,1024]{0,1:T(8,128)(2,1)} %add_convert_fusion.3), channel_id=1, source_target_pairs={{8,0},{12,4},{16,8},{20,12},{24,16},{28,20},{9,1},{13,5},{17,9},{2... | collective-permute-start | bytes 3145736 | tf_op jit(solution)/shard_map/ppermute | solution.py:71
  581.1 111.3 %collective-permute-start.47 = (bf16[512,1024]{0,1:T(8,128)(2,1)}, bf16[512,1024]{0,1:T(8,128)(2,1)}, u32[]{:S(2)}, u32[]{:S(2)}) collective-permute-start(bf16[512,1024]{0,1:T(8,128)(2,1)} %add_convert_fusion.7), channel_id=1, source_target_pairs={{8,0},{12,4},{16,8},{20,12},{24,16},{28,20},{9,1},{13,5},{17,9},{2... | collective-permute-start | bytes 3145736 | tf_op jit(solution)/shard_map/ppermute | solution.py:71
  678.4 33.4 %collective-permute-start.56 = (f32[4,256]{1,0:T(4,128)S(1)}, f32[4,256]{1,0:T(4,128)S(1)}, u32[]{:S(2)}, u32[]{:S(2)}) collective-permute-start(f32[4,256]{1,0:T(4,128)S(1)} %reshape.279), channel_id=1, source_target_pairs={{0,1},{1,0},{2,3},{3,2},{4,5},{5,4},{6,7},{7,6},{8,9},{9,8},{10,11... | collective-permute-start | bytes 12296 | tf_op jit(solution)/shard_map/ppermute | solution.py:126
  678.4 39.5 %collective-permute-start.35 = (bf16[512,1024]{0,1:T(8,128)(2,1)}, bf16[512,1024]{0,1:T(8,128)(2,1)}, u32[]{:S(2)}, u32[]{:S(2)}) collective-permute-start(bf16[512,1024]{0,1:T(8,128)(2,1)} %get-tuple-element.117), channel_id=1, source_target_pairs={{0,8},{4,12},{1,9},{5,13},{2,10},{6,14},{3,11},{7,15}} | collective-permute-start | bytes 3145736 | tf_op jit(solution)/shard_map/ppermute | solution.py:71
  690.8 28.7 %collective-permute-start.38 = (bf16[512,1024]{0,1:T(8,128)(2,1)}, bf16[512,1024]{0,1:T(8,128)(2,1)}, u32[]{:S(2)}, u32[]{:S(2)}) collective-permute-start(bf16[512,1024]{0,1:T(8,128)(2,1)} %get-tuple-element.118), channel_id=1, source_target_pairs={{24,16},{28,20},{25,17},{29,21},{26,18},{30,22},{27,19},{31,23}} | collective-permute-start | bytes 3145736 | tf_op jit(solution)/shard_map/ppermute | solution.py:71
  692.4 40.9 %collective-permute-start.30 = (bf16[1024,2,512]{2,0,1:T(8,128)(2,1)}, bf16[1024,2,512]{2,0,1:T(8,128)(2,1)}, u32[]{:S(2)}, u32[]{:S(2)}) collective-permute-start(bf16[1024,2,512]{2,0,1:T(8,128)(2,1)} %bitcast.123), channel_id=1, source_target_pairs={{0,1},{1,0},{2,3},{3,2},{4,5},{5,4},{6,7},{7,6},{8,9},{9,8},{10,11... | collective-permute-start | bytes 6291464 | tf_op jit(solution)/shard_map/ppermute | solution.py:117
  718.0 44.3 %collective-permute-start.25 = (bf16[1024,1,512]{2,0,1:T(8,128)(2,1)}, bf16[1024,1,512]{2,0,1:T(8,128)(2,1)}, u32[]{:S(2)}, u32[]{:S(2)}) collective-permute-start(bf16[1024,1,512]{2,0,1:T(8,128)(2,1)} %dynamic-slice_convert_fusion.5), channel_id=1, source_target_pairs={{0,2},{1,3},{2,0},{3,1},{4,6},{5,7},{6,4},{7,5},{8,10},{9,11},{10,... | collective-permute-start | bytes 3145736 | tf_op jit(solution)/shard_map/ppermute | solution.py:117
  736.9 28.6 %collective-permute-start.31 = (bf16[1024,1,512]{2,0,1:T(8,128)(2,1)}, bf16[1024,1,512]{2,0,1:T(8,128)(2,1)}, u32[]{:S(2)}, u32[]{:S(2)}) collective-permute-start(bf16[1024,1,512]{2,0,1:T(8,128)(2,1)} %dynamic-slice_convert_fusion.4), channel_id=1, source_target_pairs={{0,2},{1,3},{2,0},{3,1},{4,6},{5,7},{6,4},{7,5},{8,10},{9,11},{10,... | collective-permute-start | bytes 3145736 | tf_op jit(solution)/shard_map/ppermute | solution.py:117
  746.6 27.3 %collective-permute-start.37 = (bf16[512,1024]{0,1:T(8,128)(2,1)}, bf16[512,1024]{0,1:T(8,128)(2,1)}, u32[]{:S(2)}, u32[]{:S(2)}) collective-permute-start(bf16[512,1024]{0,1:T(8,128)(2,1)} %get-tuple-element.113), channel_id=1, source_target_pairs={{0,8},{4,12},{8,16},{12,20},{16,24},{20,28},{1,9},{5,13},{9,17},{1... | collective-permute-start | bytes 3145736 | tf_op jit(solution)/shard_map/ppermute | solution.py:71
  753.2 25.7 %collective-permute-start.40 = (bf16[512,1024]{0,1:T(8,128)(2,1)}, bf16[512,1024]{0,1:T(8,128)(2,1)}, u32[]{:S(2)}, u32[]{:S(2)}) collective-permute-start(bf16[512,1024]{0,1:T(8,128)(2,1)} %get-tuple-element.114), channel_id=1, source_target_pairs={{8,0},{12,4},{16,8},{20,12},{24,16},{28,20},{9,1},{13,5},{17,9},{2... | collective-permute-start | bytes 3145736 | tf_op jit(solution)/shard_map/ppermute | solution.py:71
  767.9 22.9 %collective-permute-start.32 = (bf16[512,512]{1,0:T(8,128)(2,1)S(1)}, bf16[512,512]{1,0:T(8,128)(2,1)S(1)}, u32[]{:S(2)}, u32[]{:S(2)}) collective-permute-start(bf16[512,512]{1,0:T(8,128)(2,1)S(1)} %fusion.70), channel_id=1, source_target_pairs={{0,4},{4,0},{8,12},{12,8},{16,20},{20,16},{24,28},{28,24},{1,5},{5... | collective-permute-start | bytes 1572872 | tf_op jit(solution)/shard_map/ppermute | solution.py:60
  (99 other events, 1888.1 us)

commit v2 on v1

--- a/solution.py
+++ b/solution.py
@@ -1,8 +1,11 @@
+import functools
 import math
 
 import jax
 import jax.numpy as jnp
 from jax import lax
+from jax.experimental import pallas as pl
+from jax.experimental.pallas import tpu as pltpu
 from jax.sharding import PartitionSpec as P
 
 HDIM = 256
@@ -12,6 +15,9 @@
 EPS = 1e-05
 F32 = jnp.float32
 BF16 = jnp.bfloat16
+MESH = pl.DeviceIdType.MESH
+ANY = pl.BlockSpec(memory_space=pl.ANY)
+VMEM = pl.BlockSpec(memory_space=pltpu.VMEM)
 
 
 def mm(left, right, dims):
@@ -36,15 +42,6 @@
     freq = 1.0 / 10000.0 ** (steps * 2.0 / ROT)
     angle = positions[:, None] * freq[None, :]
     return jnp.cos(angle), jnp.sin(angle)
-
-
-def rotate(values, cosine, sine):
-    half = ROT // 2
-    first = values[..., :half]
-    second = values[..., half:ROT]
-    return jnp.concatenate(
-        [first * cosine - second * sine, second * cosine + first * sine, values[..., ROT:]], axis=-1
-    )
 
 
 def locate(indices, starts):
@@ -69,19 +66,6 @@
             if reach is None or 0 <= s + 2 * reach < count:
                 pairs.append((s, d))
     return lax.ppermute(value, "fsdp", pairs)
-
-
-def gather_planes(chunk, d, dp):
-    ups, downs = [chunk], [chunk]
-    for _ in range(dp - 1):
-        ups.append(planes(ups[-1], 1))
-        downs.append(planes(downs[-1], -1))
-    rows = chunk.shape[0]
-    full = jnp.zeros((dp * rows, chunk.shape[1]), chunk.dtype)
-    for s in range(dp):
-        piece = chunk if s == 0 else jnp.where(d >= s, ups[s], downs[dp - s])
-        full = lax.dynamic_update_slice_in_dim(full, piece, lax.rem(d - s + dp, dp) * rows, 0)
-    return full
 
 
 def reduce_planes(parts, d, dp):
@@ -133,9 +117,393 @@
     return lax.dynamic_slice_in_dim(value, which * size, size, axis)
 
 
-def pair_rows(value, i):
-    got = swap(value)
-    return jnp.where(i == 0, jnp.concatenate([value, got], 0), jnp.concatenate([got, value], 0))
+def exchange_kernel(axis, spread, v_ref, o_ref, ssem, rsem):
+    count = o_ref.shape[0]
+    me = lax.axis_index(axis)
+
+    def peer(step):
+        return lax.rem(me + step, count)
+
+    barrier = pltpu.get_barrier_semaphore()
+    for step in range(1, count):
+        pl.semaphore_signal(barrier, 1, device_id={axis: peer(step)}, device_id_type=MESH)
+    pl.semaphore_wait(barrier, count - 1)
+
+    def copy(step):
+        return pltpu.make_async_remote_copy(
+            src_ref=v_ref.at[peer(step)] if spread else v_ref,
+            dst_ref=o_ref.at[me],
+            send_sem=ssem.at[step],
+            recv_sem=rsem.at[step],
+            device_id={axis: peer(step)},
+            device_id_type=MESH,
+        )
+
+    for step in range(1, count):
+        copy(step).start()
+    o_ref[me] = v_ref[me] if spread else v_ref[...]
+    for step in range(1, count):
+        copy(step).wait()
+
+
+def exchange(value, axis, spread, cid):
+    count = lax.axis_size(axis)
+    block = value.shape[1:] if spread else value.shape
+    return pl.pallas_call(
+        functools.partial(exchange_kernel, axis, spread),
+        out_shape=jax.ShapeDtypeStruct((count,) + block, value.dtype),
+        in_specs=[VMEM],
+        out_specs=VMEM,
+        scratch_shapes=[pltpu.SemaphoreType.DMA((count,)), pltpu.SemaphoreType.DMA((count,))],
+        compiler_params=pltpu.CompilerParams(collective_id=cid, has_side_effects=True),
+        name="exchange",
+    )(value)
+
+
+GROUPS = 3
+
+
+def attend_kernel(
+    dims,
+    tok, gh, w2, vecs, bq, tabs, first,
+    x_o, g_o, wa_o, wi_o, wo_o, att_o, dqkv_o,
+    xs, h1s, was, gs, win, qs, das, acc, down,
+    rcv, lsem, tsem, psem, zsem, zrec, ksem, dsem,
+):
+    R, D, feats, dp, reach = dims
+    f = lax.axis_index("fsdp")
+    t = lax.axis_index("tp")
+    d, i = f // 2, lax.rem(f, 2)
+    core = lax.rem(t, 2)
+    plane = 2 * R
+    qb = min(256, plane)
+    nb = plane // qb
+    mate = (f + 1 - 2 * i, t)
+    near = (f, t + 1 - 2 * core)
+    dirs = ((f + 2, t), (f - 2, t))
+    has = (d + 1 < dp, d >= 1)
+    outs = (wa_o, wi_o, wo_o)
+    gw = w2.shape[2] // GROUPS
+
+    barrier = pltpu.get_barrier_semaphore()
+    for who in (mate, near):
+        pl.semaphore_signal(barrier, 1, device_id=who, device_id_type=MESH)
+    for k in range(2):
+        @pl.when(has[k])
+        def _():
+            pl.semaphore_signal(barrier, 1, device_id=dirs[k], device_id_type=MESH)
+    pl.semaphore_wait(barrier, 2 + has[0].astype(jnp.int32) + has[1].astype(jnp.int32))
+
+    def rc(src, dst, ssem, rsem, who):
+        return pltpu.make_async_remote_copy(
+            src_ref=src, dst_ref=dst, send_sem=ssem, recv_sem=rsem, device_id=who, device_id_type=MESH
+        )
+
+    def slot(g, s):
+        return outs[g].at[pl.ds(s * feats, feats), :]
+
+    def part(half, g):
+        return w2.at[half, :, pl.ds(g * gw, gw)]
+
+    def pair_copy(g):
+        return rc(part(1 - i, g), slot(g, f), psem.at[0, g], psem.at[1, g], mate)
+
+    def own_copy(g):
+        return pltpu.make_async_copy(part(i, g), slot(g, f), lsem.at[g])
+
+    def z_own(g, way):
+        return rc(part(i, g), slot(g, f), zsem.at[g, 0, way, 0], zrec.at[g, f], dirs[way])
+
+    def z_mate(g, way):
+        s = f + 1 - 2 * i
+        return rc(slot(g, s), slot(g, s), zsem.at[g, 0, way, 1], zrec.at[g, s], dirs[way])
+
+    def z_fwd(g, k, way, j):
+        s = (d - k) * 2 + j if way == 0 else (d + k) * 2 + j
+        return rc(slot(g, s), slot(g, s), zsem.at[g, k, way, j], zrec.at[g, s], dirs[way])
+
+    def send_own(g):
+        for way in range(2):
+            @pl.when(has[way])
+            def _():
+                z_own(g, way).start()
+
+    def send_mate(g):
+        pair_copy(g).wait_recv()
+        for way in range(2):
+            @pl.when(has[way])
+            def _():
+                z_mate(g, way).start()
+
+    def from_dist(k, way):
+        return d >= k if way == 0 else d + k < dp
+
+    def arrive(g, k):
+        for way in range(2):
+            @pl.when(from_dist(k, way))
+            def _():
+                for j in range(2):
+                    z_fwd(g, k, way, j).wait_recv()
+
+                    @pl.when(has[way])
+                    def _():
+                        z_fwd(g, k, way, j).start()
+
+    def finish(g):
+        own_copy(g).wait()
+        pair_copy(g).wait_send()
+        for way in range(2):
+            @pl.when(has[way])
+            def _():
+                z_own(g, way).wait_send()
+                z_mate(g, way).wait_send()
+            for k in range(1, dp - 1):
+                @pl.when(from_dist(k, way) & has[way])
+                def _():
+                    for j in range(2):
+                        z_fwd(g, k, way, j).wait_send()
+
+    hr = R // 2
+
+    def rows_x(a, ref, out):
+        return rc(
+            ref.at[pl.ds(core * hr, hr), :], out.at[pl.ds(i * R + core * hr, hr), :],
+            tsem.at[a, 0], tsem.at[a, 1], mate,
+        )
+
+    def rows_c(a, out):
+        at = out.at[pl.ds((1 - i) * R + core * hr, hr), :]
+        return rc(at, at, tsem.at[a, 2], tsem.at[a, 3], near)
+
+    def rows_own(a, ref, out):
+        return pltpu.make_async_copy(ref, out.at[pl.ds(i * R, R), :], lsem.at[GROUPS + a])
+
+    pair_copy(0).start()
+    send_own(0)
+    rows_x(0, tok, x_o).start()
+    own_copy(0).start()
+    rows_own(0, tok, x_o).start()
+    rows_own(1, gh, g_o).start()
+    send_mate(0)
+    rows_x(1, gh, g_o).start()
+    pair_copy(1).start()
+    pair_copy(2).start()
+    own_copy(1).start()
+    own_copy(2).start()
+    rows_x(0, tok, x_o).wait_recv()
+    rows_c(0, x_o).start()
+    send_own(1)
+    rows_c(0, x_o).wait_recv()
+    rows_own(0, tok, x_o).wait()
+    load_x = pltpu.make_async_copy(x_o, xs, lsem.at[5])
+    load_x.start()
+    arrive(0, 1)
+    load_x.wait()
+
+    def norm_block(b, _):
+        at = pl.ds(pl.multiple_of(b * qb, qb), qb)
+        x = xs[at, :].astype(F32)
+        mean = jnp.mean(x, axis=-1, keepdims=True)
+        c = x - mean
+        var = jnp.mean(c * c, axis=-1, keepdims=True)
+        h1s[at, :] = (c * lax.rsqrt(var + EPS) * vecs[0:1, :] + vecs[1:2, :]).astype(BF16)
+        return 0
+
+    lax.fori_loop(0, nb // 2, norm_block, 0)
+    for k in range(2, dp):
+        arrive(0, k)
+        if k == 2:
+            send_mate(1)
+    lax.fori_loop(nb // 2, nb, norm_block, 0)
+    own_copy(0).wait()
+    load_w = pltpu.make_async_copy(wa_o, was, lsem.at[5])
+    load_w.start()
+    rows_x(1, gh, g_o).wait_recv()
+    rows_c(1, g_o).start()
+    send_own(2)
+    send_mate(2)
+    arrive(1, 1)
+    rows_c(1, g_o).wait_recv()
+    rows_own(1, gh, g_o).wait()
+    load_g = pltpu.make_async_copy(g_o, gs, lsem.at[6])
+    load_g.start()
+    load_w.wait()
+    load_g.wait()
+
+    def turn(u, at, sign):
+        lo, hi = u[:, :128], u[:, 128:]
+        a = pltpu.roll(lo, ROT // 2, 1) * tabs[1, at, :] + pltpu.roll(lo, 128 - ROT // 2, 1) * tabs[2, at, :]
+        lo = lo * tabs[0, at, :] + (a if sign > 0 else -a)
+        return jnp.concatenate([lo, hi], axis=1)
+
+    scale = 1.0 / math.sqrt(HDIM)
+
+    def proj_block(b, _):
+        at = pl.ds(pl.multiple_of(b * qb, qb), qb)
+        y = plain(h1s[at, :], was[:, : 3 * HDIM]) + bq[...]
+        qs[at, :] = (turn(y[:, :HDIM], at, 1).astype(BF16).astype(F32) * scale).astype(BF16)
+        win[reach, at, :HDIM] = turn(y[:, HDIM : 2 * HDIM], at, 1).astype(BF16)
+        win[reach, at, HDIM:] = y[:, 2 * HDIM :].astype(BF16)
+        das[at, :] = plain(gs[at, :], was[:, 3 * HDIM :]).astype(BF16)
+        return 0
+
+    lax.fori_loop(0, nb, proj_block, 0)
+
+    def kv_copy(k):
+        return rc(win.at[reach - k], win.at[reach - k - 1], ksem.at[0, k], ksem.at[1, k + 1], dirs[0])
+
+    def kv_recv(k):
+        return rc(win.at[reach - k], win.at[reach - k], ksem.at[0, k - 1], ksem.at[1, k], dirs[0])
+
+    @pl.when(has[0])
+    def _():
+        kv_copy(0).start()
+
+    arrive(2, 1)
+    arrive(1, 2)
+    for k in range(1, reach + 1):
+        @pl.when(d >= k)
+        def _():
+            kv_recv(k).wait_recv()
+            if k < reach:
+                @pl.when(has[0])
+                def _():
+                    kv_copy(k).start()
+
+        @pl.when(d < k)
+        def _():
+            win[reach - k] = jnp.zeros((plane, 2 * HDIM), BF16)
+
+    acc[...] = jnp.zeros_like(acc)
+    span = SEQ_LEN + qb
+    base = reach * plane - SEQ_LEN
+
+    def attend_block(b, _):
+        at = pl.ds(pl.multiple_of(b * qb, qb), qb)
+        keys_at = pl.ds(pl.multiple_of(base + b * qb, qb), span)
+        flat = win.reshape((reach + 1) * plane, 2 * HDIM)
+        keys = flat[keys_at, :HDIM]
+        vals = flat[keys_at, HDIM:]
+        q = qs[at, :]
+        s = against(q, keys)
+        c = base + b * qb + lax.broadcasted_iota(jnp.int32, (qb, span), 1)
+        r = reach * plane + b * qb + lax.broadcasted_iota(jnp.int32, (qb, span), 0)
+        s = jnp.where((c >= first[at, :]) & (c <= r), s, -1e30)
+        e = jnp.exp(s - jnp.max(s, axis=1, keepdims=True))
+        p = e * (1.0 / jnp.sum(e, axis=1, keepdims=True))
+        pb = p.astype(BF16)
+        att_o[at, :] = plain(pb, vals).astype(BF16)
+        da = das[at, :]
+        dpr = against(da, vals)
+        delta = jnp.sum(p * dpr, axis=1, keepdims=True)
+        ds = (p * (dpr - delta)).astype(BF16)
+        dq = plain(ds, keys) * scale
+        dqkv_o[at, :HDIM] = turn(dq, at, -1).astype(BF16)
+        acc[keys_at, :HDIM] += inner(ds, q)
+        acc[keys_at, HDIM:] += inner(pb, da)
+        return 0
+
+    lax.fori_loop(0, nb // 2, attend_block, 0)
+    arrive(2, 2)
+    for k in range(3, dp):
+        arrive(1, k)
+    lax.fori_loop(nb // 2, nb, attend_block, 0)
+
+    def down_copy(r):
+        return rc(down.at[r], rcv.at[r], dsem.at[0, r], dsem.at[1, r], dirs[1])
+
+    for r in range(reach + 1):
+        at = pl.ds(r * plane, plane)
+        if r > 0:
+            @pl.when(has[0])
+            def _():
+                down_copy(r - 1).wait_recv()
+                acc[at, :] += rcv[r - 1].astype(F32)
+        if r < reach:
+            down[r] = acc[at, :].astype(BF16)
+
+            @pl.when(has[1])
+            def _():
+                down_copy(r).start()
+        else:
+            def tail_block(b, _):
+                here = pl.ds(pl.multiple_of(b * qb, qb), qb)
+                a = acc[pl.ds(pl.multiple_of(reach * plane + b * qb, qb), qb), :]
+                dqkv_o[here, HDIM : 2 * HDIM] = turn(a[:, :HDIM], here, -1).astype(BF16)
+                dqkv_o[here, 2 * HDIM :] = a[:, HDIM:].astype(BF16)
+                return 0
+
+            lax.fori_loop(0, nb, tail_block, 0)
+        if r == 0:
+            for k in range(3, dp):
+                arrive(2, k)
+
+    for r in range(reach):
+        @pl.when(has[1])
+        def _():
+            down_copy(r).wait_send()
+    for k in range(reach):
+        @pl.when((d >= k) & has[0])
+        def _():
+            kv_copy(k).wait_send()
+    for g in range(GROUPS):
+        if g == 0:
+            pair_copy(g).wait_send()
+            for way in range(2):
+                @pl.when(has[way])
+                def _():
+                    z_own(g, way).wait_send()
+                    z_mate(g, way).wait_send()
+                for k in range(1, dp - 1):
+                    @pl.when(from_dist(k, way) & has[way])
+                    def _():
+                        for j in range(2):
+                            z_fwd(g, k, way, j).wait_send()
+        else:
+            finish(g)
+    for a, (ref, out) in enumerate(((tok, x_o), (gh, g_o))):
+        rows_x(a, ref, out).wait_send()
+        rows_c(a, out).wait_send()
+
+
+def attend(tok, gh, w2, vecs, bq, tabs, first, dims):
+    R, D, feats, dp, reach = dims
+    plane = 2 * R
+    gw = w2.shape[2] // GROUPS
+    sds = jax.ShapeDtypeStruct
+    return pl.pallas_call(
+        functools.partial(attend_kernel, dims),
+        out_shape=[
+            sds((plane, D), BF16), sds((plane, D), BF16),
+            sds((D, gw), BF16), sds((D, gw), BF16), sds((D, gw), BF16),
+            sds((plane, HDIM), BF16), sds((plane, 3 * HDIM), BF16),
+        ],
+        in_specs=[ANY, ANY, ANY, VMEM, VMEM, VMEM, VMEM],
+        out_specs=[ANY] * 5 + [VMEM] * 2,
+        scratch_shapes=[
+            pltpu.VMEM((plane, D), BF16),
+            pltpu.VMEM((plane, D), BF16),
+            pltpu.VMEM((D, gw), BF16),
+            pltpu.VMEM((plane, D), BF16),
+            pltpu.VMEM((reach + 1, plane, 2 * HDIM), BF16),
+            pltpu.VMEM((plane, HDIM), BF16),
+            pltpu.VMEM((plane, HDIM), BF16),
+            pltpu.VMEM(((reach + 1) * plane, 2 * HDIM), F32),
+            pltpu.VMEM((reach, plane, 2 * HDIM), BF16),
+            pltpu.VMEM((reach, plane, 2 * HDIM), BF16),
+            pltpu.SemaphoreType.DMA((8,)),
+            pltpu.SemaphoreType.DMA((2, 4)),
+            pltpu.SemaphoreType.DMA((2, GROUPS)),
+            pltpu.SemaphoreType.DMA((GROUPS, dp, 2, 2)),
+            pltpu.SemaphoreType.DMA((GROUPS, 2 * dp)),
+            pltpu.SemaphoreType.DMA((2, reach + 1)),
+            pltpu.SemaphoreType.DMA((2, reach)),
+        ],
+        compiler_params=pltpu.CompilerParams(
+            collective_id=4, has_side_effects=True, vmem_limit_bytes=62 << 20
+        ),
+        name="attend",
+    )(tok, gh, w2, vecs, bq, tabs, first)
 
 
 def on_device(
@@ -180,7 +548,10 @@
         [v.astype(F32) for v in vecs]
         + [qkv_bias.astype(F32).reshape(-1), fc_in_bias.astype(F32).reshape(-1), counts]
     )
-    got = lax.all_gather(pack, "fsdp", axis=0, tiled=False)
+    size = pack.shape[0]
+    lanes = -(-size // 1024) * 128
+    got = exchange(jnp.pad(pack, (0, 8 * lanes - size)).reshape(8, lanes), "fsdp", False, 1)
+    got = got.reshape(shards, 8 * lanes)
     gain1, shift1, gain2, shift2, b_dense, b_out = [
         got[:, k * feats : (k + 1) * feats].reshape(width) for k in range(6)
     ]
@@ -193,38 +564,44 @@
     b_in = got[:, at : at + units // shards].reshape(shards, ub[0], ub[1])
     b_in = half_of(b_in.transpose(1, 0, 2).reshape(units), i, 0)
     at += units // shards
-    counts = jnp.sum(got[:, at:], axis=0)
+    counts = jnp.sum(got[:, at : at + SUBSETS], axis=0)
     table = total / (SUBSETS * counts)
     row_scale = jnp.sum(jnp.where(match, table[None, :], 0.0), axis=1)
     carried = cotangent.astype(F32) * row_scale[:, None]
     grad_here = carried.astype(BF16)
 
-    wq = qkv_weight.reshape(feats, 3, heads_here, HDIM)
-    wi = fc_in_weight.reshape(feats, 2, units // 2)
-    wo = fc_out_weight.T.reshape(feats, 2, units // 2)
-    wd = dense_weight.T.reshape(feats, 2, HDIM)
-
-    def halves(which):
-        pick = lambda v, ax: lax.dynamic_index_in_dim(v, which, ax, keepdims=False)
-        return (
-            jnp.concatenate([pick(wq, 2).reshape(feats, 3 * HDIM), pick(wd, 1)], axis=1),
-            pick(wi, 1),
-            pick(wo, 1),
-        )
-
-    x_b = pair_rows(tokens, i)
-    mine, theirs = halves(i), halves(1 - i)
-    full = []
-    for own, other in zip(mine, theirs):
-        back = swap(other)
-        chunk = jnp.where(i == 0, jnp.concatenate([own, back], 0), jnp.concatenate([back, own], 0))
-        full.append(gather_planes(chunk, d, dp))
-    w_att, w_in, w_out = full
-    w_qkv, w_dense = w_att[:, : 3 * HDIM], w_att[:, 3 * HDIM :]
-    grad_b = pair_rows(grad_here, i)
-
+    w2 = jnp.concatenate(
+        [
+            qkv_weight.reshape(feats, 3, heads_here, HDIM).transpose(2, 0, 1, 3).reshape(2, feats, 3 * HDIM),
+            dense_weight.reshape(heads_here, HDIM, feats).transpose(0, 2, 1),
+            fc_in_weight.reshape(feats, 2, units // 2).transpose(1, 0, 2),
+            fc_out_weight.reshape(2, units // 2, feats).transpose(0, 2, 1),
+        ],
+        axis=2,
+    )
     plane = 2 * rows
     start_row = d * plane
+    reach = min(dp - 1, -(-(SEQ_LEN - 1) // plane))
+    here = start_row + jnp.arange(plane, dtype=jnp.int32)
+    docs_here, pos_here = locate(here, seq_starts)
+    first = (here - pos_here.astype(jnp.int32)) - (start_row - reach * plane)
+    cosine, sine = rotary_tables(pos_here)
+    ones = jnp.ones((plane, 128 - ROT), F32)
+    none = jnp.zeros((plane, 128 - ROT), F32)
+    zero = jnp.zeros_like(sine)
+    tabs = jnp.stack(
+        [
+            jnp.concatenate([cosine, cosine, ones], 1),
+            jnp.concatenate([zero, sine, none], 1),
+            jnp.concatenate([-sine, zero, none], 1),
+        ]
+    )
+    vecs = jnp.stack([gain1, shift1, gain2, shift2] + [jnp.zeros_like(gain1)] * 4)
+    x_b, grad_b, w_att, w_in, w_out, att_b, d_qkv = attend(
+        tokens, grad_here, w2, vecs, b_qkv.reshape(1, -1), tabs, first[:, None],
+        (rows, width, feats, dp, reach),
+    )
+    w_qkv, w_dense = w_att[:, : 3 * HDIM], w_att[:, 3 * HDIM :]
     x = x_b.astype(F32)
     mean = jnp.mean(x, axis=-1, keepdims=True)
     centred = x - mean
@@ -234,55 +611,10 @@
     h_one = (xhat * gain1 + shift1).astype(BF16)
     h_two = (xhat * gain2 + shift2).astype(BF16)
 
-    here = start_row + jnp.arange(plane, dtype=jnp.int32)
-    docs_here, pos_here = locate(here, seq_starts)
-    cosine, sine = rotary_tables(pos_here)
-    qkv = plain(h_one, w_qkv) + b_qkv
-    q = rotate(qkv[:, :HDIM], cosine, sine).astype(BF16)
-    k = rotate(qkv[:, HDIM : 2 * HDIM], cosine, sine).astype(BF16)
-    v = qkv[:, 2 * HDIM :].astype(BF16)
-    reach = min(dp - 1, -(-(SEQ_LEN - 1) // plane))
-    packed = jnp.concatenate([k, v], axis=1)
-    window = [packed]
-    for _ in range(reach):
-        window.insert(0, planes(window[0], 1))
-    window = jnp.concatenate(window, axis=0)
-    span = window.shape[0]
-    cols = start_row - reach * plane + jnp.arange(span, dtype=jnp.int32)
-    docs_cols, _ = locate(cols, seq_starts)
-    allowed = (cols[None, :] <= here[:, None]) & (docs_cols[None, :] == docs_here[:, None])
-    key_win, value_win = window[:, :HDIM], window[:, HDIM:]
-    masked = jnp.where(allowed, against(q, key_win) * scale, -1e30)
-    top = jnp.max(masked, axis=1, keepdims=True)
-    expo = jnp.exp(masked - top)
-    probs = expo / jnp.sum(expo, axis=1, keepdims=True)
-    probs_b = probs.astype(BF16)
-    att_b = plain(probs_b, value_win).astype(BF16)
-
     pre = plain(h_two, w_in) + b_in
     act, gelu_pull = jax.vjp(lambda u: jax.nn.gelu(u, approximate=False), pre)
     act_b = act.astype(BF16)
     d_pre = gelu_pull(plain(grad_b, w_out))[0].astype(BF16)
-
-    d_att = plain(grad_b, w_dense).astype(BF16)
-    dprob = against(d_att, value_win)
-    delta = jnp.sum(probs * dprob, axis=1, keepdims=True)
-    dscore = (probs * (dprob - delta)).astype(BF16)
-    dq = plain(dscore, key_win) * scale
-    dk_win = inner(dscore, q) * scale
-    dv_win = inner(probs_b, d_att)
-    grads_win = jnp.concatenate([dk_win, dv_win], axis=1)
-    held = None
-    for r in range(reach):
-        piece = grads_win[r * plane : (r + 1) * plane]
-        moved = piece if held is None else piece + held
-        held = planes(moved.astype(BF16), -1).astype(F32)
-    dkv = grads_win[reach * plane :]
-    if held is not None:
-        dkv = dkv + held
-    dq_raw = rotate(dq, cosine, -sine)
-    dk_raw = rotate(dkv[:, :HDIM], cosine, -sine)
-    d_qkv = jnp.concatenate([dq_raw, dk_raw, dkv[:, HDIM:]], axis=1).astype(BF16)
 
     partial_value = against(att_b, w_dense) + against(act_b, w_out)
     share = tp_scatter(partial_value, t, tps)
@@ -337,11 +669,16 @@
     qkv_b = jnp.where(jnp.arange(2)[None, :, None] == i, qkv_b, 0.0)
     qkv_b = qkv_b.reshape(3, 2, shards, hd).transpose(2, 0, 1, 3).reshape(shards, nq)
     small = jnp.concatenate([norms, in_b, qkv_b], axis=1)
-    small = lax.psum_scatter(small, "fsdp", scatter_dimension=0, tiled=False)
-    norm_grads = tp_sum(small[: 4 * feats].reshape(4, feats), tps)
+    size = small.shape[1]
+    lanes = -(-size // 1024) * 128
+    small = jnp.pad(small, ((0, 0), (0, 8 * lanes - size))).reshape(shards, 8, lanes)
+    small = jnp.sum(exchange(small, "fsdp", True, 2), axis=0).reshape(8 * lanes)
+    norm_grads = small[: 4 * feats].reshape(8, feats // 2)
+    norm_grads = jnp.sum(exchange(norm_grads, "tp", False, 3), axis=0).reshape(4, feats)
     bias_grad = small[4 * feats : 5 * feats]
     in_bias_grad = small[5 * feats : 5 * feats + ub[0] * ub[1]].reshape(ub)
-    qkv_bias_grad = small[5 * feats + ub[0] * ub[1] :].reshape(3, heads_here, hd)
+    at = 5 * feats + ub[0] * ub[1]
+    qkv_bias_grad = small[at : at + nq].reshape(3, heads_here, hd)
     return (
         mixed,
         tokens_grad,

time: 825 us -> 807 us (0.978)
  Pallas kernels: 0 us -> 334 us
  blocking collectives: 138 us -> 0 us
  waiting for transfers between devices: 178 us -> 95.9 us
  matrix products: 132 us -> 83 us
  other arithmetic: 119 us -> 76.6 us
  starting transfers between devices: 117 us -> 98.8 us
  local copies, waits for them, and re-layouts: 126 us -> 108 us
    pallas_call x0 -> x4, Pallas kernels: none -> 334 us  [the longest x1 301 us: attend(): pl.pallas_call(functools.partial(attend_kernel, dims), out_shape=[sds((pl...]
    unnamed x2 -> x0, blocking collectives: 138 us -> none
    ppermute x40 -> x18, waiting for transfers between devices: 156 us -> 64.3 us  [planes(): return lax.ppermute(value, 'fsdp', pairs)]
    dot_general x18 -> x10, matrix products: 132 us -> 83 us  [mm(): lax.dot_general(left, right, (dims, ((), ())), preferred_element_type=F32)]
    dynamic_update_slice x12 -> x0, other arithmetic: 13.3 us -> none  [gather_planes(): lax.dynamic_update_slice_in_dim(full, piece, lax.rem(d - s + dp, dp) * ro...]
    unnamed x200 -> x94, local copies, waits for them, and re-layouts: 31 us -> 19.9 us
    ppermute x40 -> x18, starting transfers between devices: 100 us -> 89.1 us  [planes(): return lax.ppermute(value, 'fsdp', pairs)]
    ppermute x10 -> x5, waiting for transfers between devices: 21.1 us -> 31.6 us  [swap(): return lax.ppermute(value, 'fsdp', [(s, s ^ 1) for s in range(count)])]
  transfers between devices with their start and end apart: 58 -> 29, of which waited for: 17 -> 10; matrix products, arithmetic and copies ran while one was open for 44% -> 20% of each run, Pallas kernels for 0% -> 3%
where the time goes in v2:
time: 807 us; the launch traced here: 798 us
  Pallas kernels  334 us (41%)
  local copies, waits for them, and re-layouts  108 us (13%)
  starting transfers between devices  98.8 us (12%)
  waiting for transfers between devices  95.9 us (12%)
  matrix products  83 us (10%)
  other arithmetic  76.6 us (9%)
    pallas_call x1, Pallas kernels, attend(): pl.pallas_call(functools.partial(attend_kernel, dims), out_shape=[sds((pl...  301 us
    ppermute x18, starting transfers between devices, planes(): return lax.ppermute(value, 'fsdp', pairs)  89.1 us
    dot_general x10, matrix products, mm(): lax.dot_general(left, right, (dims, ((), ())), preferred_element_type=F32)  83 us
    ppermute x18, waiting for transfers between devices, planes(): return lax.ppermute(value, 'fsdp', pairs)  64.3 us
    pallas_call x3, Pallas kernels, exchange(): pl.pallas_call(functools.partial(exchange_kernel, axis, spread), out_shap...  32.7 us
    ppermute x5, waiting for transfers between devices, swap(): return lax.ppermute(value, 'fsdp', [(s, s ^ 1) for s in range(count)])  31.6 us
    convert_element_type x9, other arithmetic, reduce_planes(): held = planes(value.astype(BF16), sign, k)  27.7 us
    unnamed x94, local copies, waits for them, and re-layouts  19.9 us
  transfers between devices with their start and end apart: 29, of which 10 were waited for; matrix products, arithmetic and copies ran while one was open for 20% of the time, Pallas kernels for 3%

profile of v2, /device:TPU:0, one launch (start us, length us, event | category | flops | bytes accessed | tf_op | source)
XLA Modules:
  0.0 798.2 jit_solution(222921655486999172)
XLA Ops:
  3.1 4.1 concatenate.22
  7.8 10.0 %exchange.3 = f32[8,8,256]{2,1,0:T(8,128)} custom-call(f32[8,256]{1,0:T(8,128)} %reshape.279.v_ref), custom_call_target="tpu_custom_call" | custom-call | tf_op jit(solution)/shard_map/exchange/pallas_call | solution.py:152
  29.3 4.8 convert_reduce_fusion.2
  42.8 301.3 %attend.1 = (bf16[1024,2048]{1,0:T(8,128)(2,1)}, bf16[1024,2048]{1,0:T(8,128)(2,1)}, bf16[2048,1024]{1,0:T(8,128)(2,1)}, bf16[2048,1024]{1,0:T(8,128)(2,1)}, bf1...) custom-call(bf16[512,2048]{1,0:T(8,128)(2,1)} %tok.1, ...), custom_call_target="tpu_custom_call" | custom-call | tf_op jit(solution)/shard_map/attend/pallas_call | solution.py:474
  349.1 8.0 %fusion.48 = f32[1024,1024]{1,0:T(8,128)S(1)} fusion(bf16[2048,1024]{1,0:T(8,128)(2,1)} %get-tuple-element.24, bf16[1024,2048]{1,0:T(8,128)(2,1)} %get-tuple-element.23, f32[2048]{0:T(1024)S(1)} %bitcast.207, f32[2048]{0:T(1024)S(1)} %bitcast.209, f32[1024]{0:T(1024)S(1)} %add_rsqrt_fusion, f32[1024]{0:T(1024)S(1)} %broadcast_multiply_fusion), kind=kOutput, calls=%fused_computation.182 | convolution fusion | flops 4307550208 | bytes 12607488 | tf_op jit(solution)/shard_map/dot_general | solution.py:24
  357.2 15.8 %convert_reduce_fusion.1 = (f32[1024]{0:T(1024)S(1)}, bf16[1024,1024]{1,0:T(8,128)(2,1)}, f32[1024,1024]{1,0:T(8,128)S(1)}) fusion(f32[1024,1024]{1,0:T(8,128)S(1)} %fusion.48, f32[1024]{0:T(1024)S(1)} %dynamic_slice.141, bf16[1024,2048]{1,0:T(8,128)(2,1)S(1)} %copy-done.26, bf16[2048,1024]{1,0:T(8,128)(2,1)S(1)} %copy-done.27), kind=kOutput, calls=%fused_computation.31 | convolution fusion | flops 4373609472 | bytes 18882560 | tf_op jit(solution)/shard_map/dot_general | solution.py:24
  374.1 4.6 fusion.54
  378.7 6.0 convolution_add_fusion
  384.7 11.7 %reshape_reshape.10 = f32[1024,2,2,512]{3,2,1,0:T(2,128)} reshape(f32[1024,2048]{1,0:T(8,128)} %convolution_add_fusion) | data formatting | bytes 16777216 | tf_op jit(solution)/shard_map/reshape;reshape | solution.py:97
  396.4 9.1 %constant_dynamic-slice_fusion.2 = bf16[1024,2,1,512]{3,2,1,0:T(2,128)(2,1)} fusion(f32[1024,2,2,512]{3,2,1,0:T(2,128)} %reshape_reshape.10, s32[]{:T(128)S(6)} %select_n.153), kind=kLoop, calls=%fused_computation.144 | loop fusion | bytes 4194308 | tf_op jit(solution)/shard_map/jit(dynamic_index_in_dim)/dynamic_slice | solution.py:100
  405.5 4.3 copy.140
  409.9 5.8 fusion.14
  415.7 14.0 %fusion.49 = (f32[2048]{0:T(1024)S(1)}, f32[2048]{0:T(1024)S(1)}, f32[1024,2048]{1,0:T(8,128)}, f32[2048]{0:T(1024)S(1)}, f32[2048]{0:T(1024)S(1)}, /*index=5*/f32[1024,2048]{1,0:T(8,128)}) fusion(f32[1024]{0:T(1024)S(1)} %add_rsqrt_fusion, f32[1024]{0:T(1024)S(1)} %broadcast_multiply_fusion, bf16[1024,2048]{1,0:T(8,128)(2,1)S(1)} %copy-done.2, ...), kind=kOutput, calls=%fused_computation.183 | convolution fusion | flops 4320124928 | bytes 35708928 | tf_op jit(solution)/shard_map/dot_general | solution.py:24
  429.7 9.3 %copy.111 = f32[1024,2048]{0,1:T(8,128)} copy(f32[1024,2048]{1,0:T(8,128)} %get-tuple-element.117) | data formatting | bytes 16777216 | tf_op jit(solution)/shard_map/add | solution.py:634
  444.6 3.5 fusion.55
  448.1 9.2 %fusion.4 = f32[2048,768]{0,1:T(8,128)} fusion(bf16[1024,768]{1,0:T(8,128)(2,1)} %get-tuple-element.26, bf16[1024,2048]{1,0:T(8,128)(2,1)} %get-tuple-element.23, f32[2048]{0:T(1024)S(1)} %bitcast.214, f32[2048]{0:T(1024)S(1)} %bitcast.213, f32[1024]{0:T(1024)S(1)} %add_rsqrt_fusion, f32[1024]{0:T(1024)S(1)} %broadcast_multiply_fusion), kind=kOutput, calls=%fused_computation.27 | convolution fusion | flops 3233808384 | bytes 12083200 | tf_op jit(solution)/shard_map/dot_general | solution.py:24
  457.3 3.6 fusion.29
  460.9 37.7 %collective-permute-start.8 = (bf16[512,1024]{0,1:T(8,128)(2,1)}, bf16[512,1024]{0,1:T(8,128)(2,1)}, u32[]{:S(2)}, u32[]{:S(2)}) collective-permute-start(bf16[512,1024]{0,1:T(8,128)(2,1)} %get-tuple-element.124), channel_id=1, source_target_pairs={{0,8},{4,12},{1,9},{5,13},{2,10},{6,14},{3,11},{7,15}} | collective-permute-start | bytes 3145736 | tf_op jit(solution)/shard_map/ppermute | solution.py:68
  500.3 5.5 fusion.47
  505.8 3.3 copy-done
  514.7 10.7 %fusion.56 = f32[2048,1024]{0,1:T(8,128)} fusion(bf16[1024,2048]{1,0:T(8,128)(2,1)} %get-tuple-element.27, bf16[1024,1024]{1,0:T(8,128)(2,1)} %copy-done.11), kind=kOutput, calls=%fused_computation.188 | convolution fusion | flops 4294967296 | bytes 14680064 | tf_op jit(solution)/shard_map/dot_general | solution.py:24
  527.0 17.7 %exchange.4 = f32[8,8,256]{2,1,0:T(8,128)} custom-call(f32[8,8,256]{2,1,0:T(8,128)} %bitcast.186), custom_call_target="tpu_custom_call" | custom-call | tf_op jit(solution)/shard_map/exchange/pallas_call | solution.py:152
  545.6 4.7 constant_dynamic-slice_fusion.1
  550.3 3.9 dynamic-slice_convert_fusion.1
  554.6 5.4 copy.112
  561.9 5.0 exchange.5
  568.2 5.9 collective-permute-start.22
  574.1 9.0 %constant_dynamic-slice_fusion.3 = f32[1024,2,1,512]{3,2,1,0:T(1,128)} fusion(f32[1024,2,2,512]{3,2,1,0:T(2,128)} %reshape_reshape.10, s32[]{:T(128)S(6)} %select_n.152), kind=kLoop, calls=%fused_computation.145 | loop fusion | bytes 8388612 | tf_op jit(solution)/shard_map/jit(dynamic_index_in_dim)/dynamic_slice | solution.py:99
  583.9 5.0 fusion.27
  590.9 3.3 add_convert_fusion.11
  596.1 4.4 collective-permute-start.9
  607.0 3.7 collective-permute-start.16
  610.6 6.1 collective-permute-start.23
  616.7 4.2 bitcast_add_fusion
  630.1 3.7 fusion.24
  633.9 13.0 %collective-permute-done.16 = bf16[512,1024]{0,1:T(8,128)(2,1)} collective-permute-done((bf16[512,1024]{0,1:T(8,128)(2,1)}, bf16[512,1024]{0,1:T(8,128)(2,1)}, u32[]{:S(2)}, u32[]{:S(2)}) %collective-permute-start.16) | collective-permute-done | bytes 1048608 | tf_op jit(solution)/shard_map/ppermute | solution.py:68
  651.2 5.1 collective-permute-start.10
  656.3 13.1 %collective-permute-done.23 = bf16[512,1024]{0,1:T(8,128)(2,1)} collective-permute-done((bf16[512,1024]{0,1:T(8,128)(2,1)}, bf16[512,1024]{0,1:T(8,128)(2,1)}, u32[]{:S(2)}, u32[]{:S(2)}) %collective-permute-start.23) | collective-permute-done | bytes 1048608 | tf_op jit(solution)/shard_map/ppermute | solution.py:68
  670.2 3.7 add_convert_fusion.6
  673.9 5.9 collective-permute-start.17
  683.9 6.8 collective-permute-start.24
  697.9 19.9 %collective-permute-done.5 = bf16[512,512]{1,0:T(8,128)(2,1)S(1)} collective-permute-done((bf16[512,512]{1,0:T(8,128)(2,1)S(1)}, bf16[512,512]{1,0:T(8,128)(2,1)S(1)}, u32[]{:S(2)}, u32[]{:S(2)}) %collective-permute-start.5) | collective-permute-done | bytes 524320 | tf_op jit(solution)/shard_map/ppermute | solution.py:57
  721.1 3.6 collective-permute-done.14
  732.3 3.7 copy.114
  735.9 3.3 reshape.293
  742.4 17.0 %collective-permute-done.20 = bf16[512,1024]{0,1:T(8,128)(2,1)} collective-permute-done((bf16[512,1024]{0,1:T(8,128)(2,1)}, bf16[512,1024]{0,1:T(8,128)(2,1)}, u32[]{:S(2)}, u32[]{:S(2)}) %collective-permute-start.20) | collective-permute-done | bytes 1048608 | tf_op jit(solution)/shard_map/ppermute | solution.py:68
  763.7 15.8 %collective-permute-done.27 = bf16[512,1024]{0,1:T(8,128)(2,1)} collective-permute-done((bf16[512,1024]{0,1:T(8,128)(2,1)}, bf16[512,1024]{0,1:T(8,128)(2,1)}, u32[]{:S(2)}, u32[]{:S(2)}) %collective-permute-start.27) | collective-permute-done | bytes 1048608 | tf_op jit(solution)/shard_map/ppermute | solution.py:68
  786.7 8.1 %collective-permute-done.28 = bf16[256,1024]{0,1:T(8,128)(2,1)} collective-permute-done((bf16[256,1024]{0,1:T(8,128)(2,1)}, bf16[256,1024]{0,1:T(8,128)(2,1)}, u32[]{:S(2)}, u32[]{:S(2)}) %collective-permute-start.28) | collective-permute-done | bytes 524320 | tf_op jit(solution)/shard_map/ppermute | solution.py:57
  (257 shorter events, 112.9 us)
Async XLA Ops:
  0.6 23.1 %copy-start.20 = (bf16[512,256]{1,0:T(8,128)(2,1)S(1)}, bf16[512,256]{1,0:T(8,128)(2,1)}, u32[]{:S(2)}) copy-start(bf16[512,256]{1,0:T(8,128)(2,1)} %param.19) | copy-start | bytes 786436
  409.9 193.3 %collective-permute-start = (bf16[1024,2,512]{2,0,1:T(8,128)(2,1)}, bf16[1024,2,512]{2,0,1:T(8,128)(2,1)}, u32[]{:S(2)}, u32[]{:S(2)}) collective-permute-start(bf16[1024,2,512]{2,0,1:T(8,128)(2,1)} %bitcast.156), channel_id=1, source_target_pairs={{0,1},{1,0},{2,3},{3,2},{4,5},{5,4},{6,7},{7,6},{8,9},{9,8},{10,11... | collective-permute-start | bytes 6291464 | tf_op jit(solution)/shard_map/ppermute | solution.py:101
  444.1 166.6 %collective-permute-start.3 = (bf16[1024,2,512]{2,0,1:T(8,128)(2,1)}, bf16[1024,2,512]{2,0,1:T(8,128)(2,1)}, u32[]{:S(2)}, u32[]{:S(2)}) collective-permute-start(bf16[1024,2,512]{2,0,1:T(8,128)(2,1)} %bitcast.174), channel_id=1, source_target_pairs={{0,1},{1,0},{2,3},{3,2},{4,5},{5,4},{6,7},{7,6},{8,9},{9,8},{10,11... | collective-permute-start | bytes 6291464 | tf_op jit(solution)/shard_map/ppermute | solution.py:101
  457.3 43.0 %copy-start.3 = (bf16[1024,2048]{1,0:T(8,128)(2,1)S(1)}, bf16[1024,2048]{1,0:T(8,128)(2,1)}, u32[]{:S(2)}) copy-start(bf16[1024,2048]{1,0:T(8,128)(2,1)} %get-tuple-element.23) | copy-start | bytes 12582916
  457.3 43.0 %copy-start.28 = (bf16[1024,1024]{1,0:T(8,128)(2,1)S(1)}, bf16[1024,1024]{1,0:T(8,128)(2,1)}, u32[]{:S(2)}) copy-start(bf16[1024,1024]{1,0:T(8,128)(2,1)} %get-tuple-element.107) | copy-start | bytes 6291460
  460.9 107.2 %collective-permute-start.8 = (bf16[512,1024]{0,1:T(8,128)(2,1)}, bf16[512,1024]{0,1:T(8,128)(2,1)}, u32[]{:S(2)}, u32[]{:S(2)}) collective-permute-start(bf16[512,1024]{0,1:T(8,128)(2,1)} %get-tuple-element.124), channel_id=1, source_target_pairs={{0,8},{4,12},{1,9},{5,13},{2,10},{6,14},{3,11},{7,15}} | collective-permute-start | bytes 3145736 | tf_op jit(solution)/shard_map/ppermute | solution.py:68
  498.6 84.4 %collective-permute-start.11 = (bf16[512,1024]{0,1:T(8,128)(2,1)}, bf16[512,1024]{0,1:T(8,128)(2,1)}, u32[]{:S(2)}, u32[]{:S(2)}) collective-permute-start(bf16[512,1024]{0,1:T(8,128)(2,1)} %get-tuple-element.125), channel_id=1, source_target_pairs={{24,16},{28,20},{25,17},{29,21},{26,18},{30,22},{27,19},{31,23}} | collective-permute-start | bytes 3145736 | tf_op jit(solution)/shard_map/ppermute | solution.py:68
  510.4 78.6 %collective-permute-start.15 = (bf16[512,1024]{0,1:T(8,128)(2,1)}, bf16[512,1024]{0,1:T(8,128)(2,1)}, u32[]{:S(2)}, u32[]{:S(2)}) collective-permute-start(bf16[512,1024]{0,1:T(8,128)(2,1)} %get-tuple-element.115), channel_id=1, source_target_pairs={{0,8},{4,12},{1,9},{5,13},{2,10},{6,14},{3,11},{7,15}} | collective-permute-start | bytes 3145736 | tf_op jit(solution)/shard_map/ppermute | solution.py:68
  545.6 8.8 %copy-start.21 = (f32[8,256]{1,0:T(8,128)}, f32[8,256]{1,0:T(8,128)S(1)}, u32[]{:S(2)}) copy-start(f32[8,256]{1,0:T(8,128)S(1)} %reduce_sum.181) | copy-start | bytes 24580
  545.6 251.8 %copy-start.24 = (f32[1,256]{1,0:T(1,128)}, f32[1,256]{1,0:T(1,128)S(1)}, u32[]{:S(2)}) copy-start(f32[1,256]{1,0:T(1,128)S(1)} %get-tuple-element.142) | copy-start | bytes 3076
  568.2 27.9 %collective-permute-start.22 = (bf16[512,1024]{0,1:T(8,128)(2,1)}, bf16[512,1024]{0,1:T(8,128)(2,1)}, u32[]{:S(2)}, u32[]{:S(2)}) collective-permute-start(bf16[512,1024]{0,1:T(8,128)(2,1)} %get-tuple-element.111), channel_id=1, source_target_pairs={{0,8},{4,12},{1,9},{5,13},{2,10},{6,14},{3,11},{7,15}} | collective-permute-start | bytes 3145736 | tf_op jit(solution)/shard_map/ppermute | solution.py:68
  583.1 17.5 %slice-start.4 = ((s8[8388608]{0:T(1024)(128)(4,1)}), s8[4194304]{0:T(1024)(128)(4,1)S(1)}, s32[]{:S(2)}) async-start(s8[8388608]{0:T(1024)(128)(4,1)} %bitcast.165), calls=%async_computation.4 | async-start | bytes 8388608
  583.1 17.5 %slice-start.5 = ((s8[8388608]{0:T(1024)(128)(4,1)}), s8[4194304]{0:T(1024)(128)(4,1)S(1)}, s32[]{:S(2)}) async-start(s8[8388608]{0:T(1024)(128)(4,1)} %bitcast.165), calls=%async_computation.5 | async-start | bytes 8388608
  583.1 23.9 %collective-permute-start.18 = (bf16[512,1024]{0,1:T(8,128)(2,1)S(1)}, bf16[512,1024]{0,1:T(8,128)(2,1)S(1)}, u32[]{:S(2)}, u32[]{:S(2)}) collective-permute-start(bf16[512,1024]{0,1:T(8,128)(2,1)S(1)} %get-tuple-element.116), channel_id=1, source_target_pairs={{24,16},{28,20},{25,17},{29,21},{26,18},{30,22},{27,19},{31,23}} | collective-permute-start | bytes 3145736 | tf_op jit(solution)/shard_map/ppermute | solution.py:68
  589.0 15.1 %copy-start.5 = (f32[1024,2,1,512]{3,2,1,0:T(1,128)S(1)}, f32[1024,2,1,512]{3,2,1,0:T(1,128)}, u32[]{:S(2)}) copy-start(f32[1024,2,1,512]{3,2,1,0:T(1,128)} %constant_dynamic-slice_fusion.3) | copy-start | bytes 12582916
  589.0 62.3 %collective-permute-start.25 = (bf16[512,1024]{0,1:T(8,128)(2,1)S(1)}, bf16[512,1024]{0,1:T(8,128)(2,1)}, u32[]{:S(2)}, u32[]{:S(2)}) collective-permute-start(bf16[512,1024]{0,1:T(8,128)(2,1)S(1)} %copy-done.13), channel_id=1, source_target_pairs={{24,16},{28,20},{25,17},{29,21},{26,18},{30,22},{27,19},{31,23}} | collective-permute-start | bytes 3145736 | tf_op jit(solution)/shard_map/ppermute | solution.py:68
  596.1 28.3 %collective-permute-start.9 = (bf16[512,1024]{0,1:T(8,128)(2,1)}, bf16[512,1024]{0,1:T(8,128)(2,1)S(1)}, u32[]{:S(2)}, u32[]{:S(2)}) collective-permute-start(bf16[512,1024]{0,1:T(8,128)(2,1)} %get-tuple-element.122), channel_id=1, source_target_pairs={{0,8},{4,12},{8,16},{12,20},{1,9},{5,13},{9,17},{13,21},{2,10},{6,... | collective-permute-start | bytes 3145736 | tf_op jit(solution)/shard_map/ppermute | solution.py:68
  603.2 13.6 %copy-start.4 = (f32[1024,2,1,512]{3,0,1,2:T(8,128)S(1)}, f32[1024,2,1,512]{3,0,1,2:T(8,128)}, u32[]{:S(2)}) copy-start(f32[1024,2,1,512]{3,0,1,2:T(8,128)} %copy.112) | copy-start | bytes 12582916
  603.2 25.5 %collective-permute-start.12 = (bf16[512,1024]{0,1:T(8,128)(2,1)}, bf16[512,1024]{0,1:T(8,128)(2,1)S(1)}, u32[]{:S(2)}, u32[]{:S(2)}) collective-permute-start(bf16[512,1024]{0,1:T(8,128)(2,1)} %get-tuple-element.123), channel_id=1, source_target_pairs={{16,8},{20,12},{24,16},{28,20},{17,9},{21,13},{25,17},{29,21},{18,... | collective-permute-start | bytes 3145736 | tf_op jit(solution)/shard_map/ppermute | solution.py:68
  604.1 26.1 %slice-start = ((s8[6291456]{0:T(1024)(128)(4,1)}), s8[4194304]{0:T(1024)(128)(4,1)S(1)}, s32[]{:S(2)}) async-start(s8[6291456]{0:T(1024)(128)(4,1)} %bitcast.159), calls=%async_computation | async-start | bytes 8388608
  606.9 14.1 %copy-start.6 = (f32[1024,2,512]{2,0,1:T(8,128)}, f32[1024,2,512]{2,0,1:T(8,128)S(1)}, u32[]{:S(2)}) copy-start(f32[1024,2,512]{2,0,1:T(8,128)S(1)} %bitcast_add_fusion.1) | copy-start | bytes 12582916
  606.9 23.2 %slice-start.1 = ((s8[6291456]{0:T(1024)(128)(4,1)}), s8[2097152]{0:T(1024)(128)(4,1)S(1)}, s32[]{:S(2)}) async-start(s8[6291456]{0:T(1024)(128)(4,1)} %bitcast.159), calls=%async_computation.1 | async-start | bytes 4194304
  607.0 9.8 %copy-start.14 = (bf16[512,1024]{0,1:T(8,128)(2,1)}, bf16[512,1024]{0,1:T(8,128)(2,1)S(1)}, u32[]{:S(2)}) copy-start(bf16[512,1024]{0,1:T(8,128)(2,1)S(1)} %collective-permute-done.18) | copy-start | bytes 3145732
  607.0 39.9 %collective-permute-start.16 = (bf16[512,1024]{0,1:T(8,128)(2,1)}, bf16[512,1024]{0,1:T(8,128)(2,1)}, u32[]{:S(2)}, u32[]{:S(2)}) collective-permute-start(bf16[512,1024]{0,1:T(8,128)(2,1)} %add_convert_fusion.11), channel_id=1, source_target_pairs={{0,8},{4,12},{8,16},{12,20},{1,9},{5,13},{9,17},{13,21},{2,10},{6,... | collective-permute-start | bytes 3145736 | tf_op jit(solution)/shard_map/ppermute | solution.py:68
  610.6 58.7 %collective-permute-start.23 = (bf16[512,1024]{0,1:T(8,128)(2,1)}, bf16[512,1024]{0,1:T(8,128)(2,1)}, u32[]{:S(2)}, u32[]{:S(2)}) collective-permute-start(bf16[512,1024]{0,1:T(8,128)(2,1)} %add_convert_fusion.7), channel_id=1, source_target_pairs={{0,8},{4,12},{8,16},{12,20},{1,9},{5,13},{9,17},{13,21},{2,10},{6,... | collective-permute-start | bytes 3145736 | tf_op jit(solution)/shard_map/ppermute | solution.py:68
  621.0 27.2 %slice-start.2 = ((s8[8388608]{0:T(1024)(128)(4,1)}), s8[4194304]{0:T(1024)(128)(4,1)S(1)}, s32[]{:S(2)}) async-start(s8[8388608]{0:T(1024)(128)(4,1)} %bitcast.163), calls=%async_computation.2 | async-start | bytes 8388608
  624.4 49.5 %collective-permute-start.1 = (bf16[1024,1,512]{2,0,1:T(8,128)(2,1)}, bf16[1024,1,512]{2,0,1:T(8,128)(2,1)}, u32[]{:S(2)}, u32[]{:S(2)}) collective-permute-start(bf16[1024,1,512]{2,0,1:T(8,128)(2,1)} %dynamic-slice_convert_fusion.5), channel_id=1, source_target_pairs={{0,2},{1,3},{2,0},{3,1},{4,6},{5,7},{6,4},{7,5},{8,10},{9,11},{10,... | collective-permute-start | bytes 3145736 | tf_op jit(solution)/shard_map/ppermute | solution.py:101
  628.6 19.6 %slice-start.3 = ((s8[8388608]{0:T(1024)(128)(4,1)}), s8[4194304]{0:T(1024)(128)(4,1)S(1)}, s32[]{:S(2)}) async-start(s8[8388608]{0:T(1024)(128)(4,1)} %bitcast.163), calls=%async_computation.3 | async-start | bytes 8388608
  628.6 19.6 %copy-start.15 = (bf16[512,1024]{0,1:T(8,128)(2,1)S(1)}, bf16[512,1024]{0,1:T(8,128)(2,1)}, u32[]{:S(2)}) copy-start(bf16[512,1024]{0,1:T(8,128)(2,1)} %copy-done.14) | copy-start | bytes 3145732
  629.6 51.8 %collective-permute-start.4 = (bf16[1024,1,512]{2,0,1:T(8,128)(2,1)}, bf16[1024,1,512]{2,0,1:T(8,128)(2,1)}, u32[]{:S(2)}, u32[]{:S(2)}) collective-permute-start(bf16[1024,1,512]{2,0,1:T(8,128)(2,1)} %dynamic-slice_convert_fusion.4), channel_id=1, source_target_pairs={{0,2},{1,3},{2,0},{3,1},{4,6},{5,7},{6,4},{7,5},{8,10},{9,11},{10,... | collective-permute-start | bytes 3145736 | tf_op jit(solution)/shard_map/ppermute | solution.py:101
  646.9 37.0 %collective-permute-start.13 = (bf16[512,1024]{0,1:T(8,128)(2,1)}, bf16[512,1024]{0,1:T(8,128)(2,1)S(1)}, u32[]{:S(2)}, u32[]{:S(2)}) collective-permute-start(bf16[512,1024]{0,1:T(8,128)(2,1)} %get-tuple-element.121), channel_id=1, source_target_pairs={{8,0},{12,4},{16,8},{20,12},{24,16},{28,20},{9,1},{13,5},{17,9},{2... | collective-permute-start | bytes 3145736 | tf_op jit(solution)/shard_map/ppermute | solution.py:68
  651.2 40.5 %collective-permute-start.10 = (bf16[512,1024]{0,1:T(8,128)(2,1)S(1)}, bf16[512,1024]{0,1:T(8,128)(2,1)S(1)}, u32[]{:S(2)}, u32[]{:S(2)}) collective-permute-start(bf16[512,1024]{0,1:T(8,128)(2,1)S(1)} %get-tuple-element.120), channel_id=1, source_target_pairs={{0,8},{4,12},{8,16},{12,20},{16,24},{20,28},{1,9},{5,13},{9,17},{1... | collective-permute-start | bytes 3145736 | tf_op jit(solution)/shard_map/ppermute | solution.py:68
  669.4 10.5 %copy-start.7 = (f32[1024,2,512]{2,0,1:T(8,128)S(1)}, f32[1024,2,512]{2,0,1:T(8,128)}, u32[]{:S(2)}) copy-start(f32[1024,2,512]{2,0,1:T(8,128)} %copy-done.6) | copy-start | bytes 12582916
  669.4 23.7 %collective-permute-start.19 = (bf16[512,1024]{0,1:T(8,128)(2,1)S(1)}, bf16[512,1024]{0,1:T(8,128)(2,1)S(1)}, u32[]{:S(2)}, u32[]{:S(2)}) collective-permute-start(bf16[512,1024]{0,1:T(8,128)(2,1)S(1)} %get-tuple-element.114), channel_id=1, source_target_pairs={{16,8},{20,12},{24,16},{28,20},{17,9},{21,13},{25,17},{29,21},{18,... | collective-permute-start | bytes 3145736 | tf_op jit(solution)/shard_map/ppermute | solution.py:68
  673.9 8.3 %copy-start.8 = (f32[1024,2,512]{2,0,1:T(8,128)S(1)}, f32[1024,2,512]{2,0,1:T(8,128)}, u32[]{:S(2)}) copy-start(f32[1024,2,512]{2,0,1:T(8,128)} %bitcast_add_fusion) | copy-start | bytes 12582916
  673.9 68.5 %collective-permute-start.17 = (bf16[512,1024]{0,1:T(8,128)(2,1)}, bf16[512,1024]{0,1:T(8,128)(2,1)}, u32[]{:S(2)}, u32[]{:S(2)}) collective-permute-start(bf16[512,1024]{0,1:T(8,128)(2,1)} %get-tuple-element.113), channel_id=1, source_target_pairs={{0,8},{4,12},{8,16},{12,20},{16,24},{20,28},{1,9},{5,13},{9,17},{1... | collective-permute-start | bytes 3145736 | tf_op jit(solution)/shard_map/ppermute | solution.py:68
  681.4 14.4 %collective-permute-start.26 = (bf16[512,1024]{0,1:T(8,128)(2,1)S(1)}, bf16[512,1024]{0,1:T(8,128)(2,1)S(1)}, u32[]{:S(2)}, u32[]{:S(2)}) collective-permute-start(bf16[512,1024]{0,1:T(8,128)(2,1)S(1)} %get-tuple-element.110), channel_id=1, source_target_pairs={{16,8},{20,12},{24,16},{28,20},{17,9},{21,13},{25,17},{29,21},{18,... | collective-permute-start | bytes 3145736 | tf_op jit(solution)/shard_map/ppermute | solution.py:68
  683.7 35.4 %copy-start.9 = (f32[1024,1,512]{2,0,1:T(8,128)}, f32[1024,1,512]{2,0,1:T(8,128)S(1)}, u32[]{:S(2)}) copy-start(f32[1024,1,512]{2,0,1:T(8,128)S(1)} %convert_add_fusion.2) | copy-start | bytes 6291460
  683.9 79.8 %collective-permute-start.24 = (bf16[512,1024]{0,1:T(8,128)(2,1)}, bf16[512,1024]{0,1:T(8,128)(2,1)}, u32[]{:S(2)}, u32[]{:S(2)}) collective-permute-start(bf16[512,1024]{0,1:T(8,128)(2,1)} %get-tuple-element.109), channel_id=1, source_target_pairs={{0,8},{4,12},{8,16},{12,20},{16,24},{20,28},{1,9},{5,13},{9,17},{1... | collective-permute-start | bytes 3145736 | tf_op jit(solution)/shard_map/ppermute | solution.py:68
  691.7 34.5 %collective-permute-start.2 = (bf16[512,512]{1,0:T(8,128)(2,1)S(1)}, bf16[512,512]{1,0:T(8,128)(2,1)S(1)}, u32[]{:S(2)}, u32[]{:S(2)}) collective-permute-start(bf16[512,512]{1,0:T(8,128)(2,1)S(1)} %fusion.41), channel_id=1, source_target_pairs={{0,4},{4,0},{8,12},{12,8},{16,20},{20,16},{24,28},{28,24},{1,5},{5... | collective-permute-start | bytes 1572872 | tf_op jit(solution)/shard_map/ppermute | solution.py:57
  693.1 24.8 %collective-permute-start.5 = (bf16[512,512]{1,0:T(8,128)(2,1)S(1)}, bf16[512,512]{1,0:T(8,128)(2,1)S(1)}, u32[]{:S(2)}, u32[]{:S(2)}) collective-permute-start(bf16[512,512]{1,0:T(8,128)(2,1)S(1)} %fusion.42), channel_id=1, source_target_pairs={{0,4},{4,0},{8,12},{12,8},{16,20},{20,16},{24,28},{28,24},{1,5},{5... | collective-permute-start | bytes 1572872 | tf_op jit(solution)/shard_map/ppermute | solution.py:57
  695.8 28.8 %collective-permute-start.14 = (bf16[256,1024]{0,1:T(8,128)(2,1)S(1)}, bf16[256,1024]{0,1:T(8,128)(2,1)S(1)}, u32[]{:S(2)}, u32[]{:S(2)}) collective-permute-start(bf16[256,1024]{0,1:T(8,128)(2,1)S(1)} %dynamic-slice_convert_fusion.8), channel_id=1, source_target_pairs={{0,4},{4,0},{8,12},{12,8},{16,20},{20,16},{24,28},{28,24},{1,5},{5... | collective-permute-start | bytes 1572872 | tf_op jit(solution)/shard_map/ppermute | solution.py:57
  717.8 41.7 %collective-permute-start.20 = (bf16[512,1024]{0,1:T(8,128)(2,1)}, bf16[512,1024]{0,1:T(8,128)(2,1)}, u32[]{:S(2)}, u32[]{:S(2)}) collective-permute-start(bf16[512,1024]{0,1:T(8,128)(2,1)} %add_convert_fusion.8), channel_id=1, source_target_pairs={{8,0},{12,4},{16,8},{20,12},{24,16},{28,20},{9,1},{13,5},{17,9},{2... | collective-permute-start | bytes 3145736 | tf_op jit(solution)/shard_map/ppermute | solution.py:68
  724.6 54.9 %collective-permute-start.27 = (bf16[512,1024]{0,1:T(8,128)(2,1)}, bf16[512,1024]{0,1:T(8,128)(2,1)}, u32[]{:S(2)}, u32[]{:S(2)}) collective-permute-start(bf16[512,1024]{0,1:T(8,128)(2,1)} %add_convert_fusion.4), channel_id=1, source_target_pairs={{8,0},{12,4},{16,8},{20,12},{24,16},{28,20},{9,1},{13,5},{17,9},{2... | collective-permute-start | bytes 3145736 | tf_op jit(solution)/shard_map/ppermute | solution.py:68
  726.2 2.2 collective-permute-start.6
  728.5 10.8 %collective-permute-start.7 = (f32[2,512]{1,0:T(2,128)S(1)}, f32[2,512]{1,0:T(2,128)S(1)}, u32[]{:S(2)}, u32[]{:S(2)}) collective-permute-start(f32[2,512]{1,0:T(2,128)S(1)} %fusion.45), channel_id=1, source_target_pairs={{0,2},{1,3},{2,0},{3,1},{4,6},{5,7},{6,4},{7,5},{8,10},{9,11},{10,... | collective-permute-start | bytes 12296 | tf_op jit(solution)/shard_map/ppermute | solution.py:110
  762.2 22.4 %collective-permute-start.21 = (bf16[256,1024]{0,1:T(8,128)(2,1)S(1)}, bf16[256,1024]{0,1:T(8,128)(2,1)S(1)}, u32[]{:S(2)}, u32[]{:S(2)}) collective-permute-start(bf16[256,1024]{0,1:T(8,128)(2,1)S(1)} %dynamic-slice_convert_fusion.7), channel_id=1, source_target_pairs={{0,4},{4,0},{8,12},{12,8},{16,20},{20,16},{24,28},{28,24},{1,5},{5... | collective-permute-start | bytes 1572872 | tf_op jit(solution)/shard_map/ppermute | solution.py:57
  783.0 11.8 %collective-permute-start.28 = (bf16[256,1024]{0,1:T(8,128)(2,1)}, bf16[256,1024]{0,1:T(8,128)(2,1)}, u32[]{:S(2)}, u32[]{:S(2)}) collective-permute-start(bf16[256,1024]{0,1:T(8,128)(2,1)} %dynamic-slice_convert_fusion.6), channel_id=1, source_target_pairs={{0,4},{4,0},{8,12},{12,8},{16,20},{20,16},{24,28},{28,24},{1,5},{5... | collective-permute-start | bytes 1572872 | tf_op jit(solution)/shard_map/ppermute | solution.py:57
  (17 other events, 85.0 us)

commit v3 on v2

--- a/solution.py
+++ b/solution.py
@@ -50,66 +50,6 @@
     pick = doc_ids[:, None] == jnp.arange(starts.shape[0], dtype=jnp.int32)[None, :]
     first = jnp.sum(jnp.where(pick, starts[None, :], 0), axis=1)
     return (doc_ids, (indices - first).astype(F32))
-
-
-def swap(value):
-    count = lax.axis_size("fsdp")
-    return lax.ppermute(value, "fsdp", [(s, s ^ 1) for s in range(count)])
-
-
-def planes(value, steps, reach=None):
-    count = lax.axis_size("fsdp")
-    pairs = []
-    for s in range(count):
-        d = s + 2 * steps
-        if 0 <= d < count:
-            if reach is None or 0 <= s + 2 * reach < count:
-                pairs.append((s, d))
-    return lax.ppermute(value, "fsdp", pairs)
-
-
-def reduce_planes(parts, d, dp):
-    rows = parts.shape[0] // dp
-
-    def block(k):
-        where = jnp.clip(d + k, 0, dp - 1) * rows
-        return lax.dynamic_slice_in_dim(parts, where, rows, 0).astype(F32)
-
-    total = block(0)
-    for sign in (1, -1):
-        held = None
-        for s in range(dp - 1):
-            k = sign * (dp - 1 - s)
-            value = block(k) if held is None else block(k) + held.astype(F32)
-            held = planes(value.astype(BF16), sign, k)
-        if held is not None:
-            total = total + held.astype(F32)
-    return total
-
-
-def tp_scatter(value, t, count):
-    rows, cols = value.shape
-    part = cols // count
-    value = value.reshape(rows, count, part)
-    bit = 1
-    while bit < count:
-        n = value.shape[1]
-        view = value.reshape(rows, n // 2, 2, part)
-        mine = lax.rem(t // bit, 2)
-        keep = lax.dynamic_index_in_dim(view, mine, 2, keepdims=False)
-        send = lax.dynamic_index_in_dim(view, 1 - mine, 2, keepdims=False)
-        got = lax.ppermute(send.astype(BF16), "tp", [(s, s ^ bit) for s in range(count)])
-        value = keep.astype(F32) + got.astype(F32)
-        bit *= 2
-    return value.reshape(rows, part)
-
-
-def tp_sum(value, count):
-    bit = 1
-    while bit < count:
-        value = value + lax.ppermute(value, "tp", [(s, s ^ bit) for s in range(count)])
-        bit *= 2
-    return value
 
 
 def half_of(value, which, axis):
@@ -163,12 +103,18 @@
 GROUPS = 3
 
 
+def turn(u, tabs, at, sign):
+    lo, hi = u[:, :128], u[:, 128:]
+    a = pltpu.roll(lo, ROT // 2, 1) * tabs[1, at, :] + pltpu.roll(lo, 128 - ROT // 2, 1) * tabs[2, at, :]
+    lo = lo * tabs[0, at, :] + (a if sign > 0 else -a)
+    return jnp.concatenate([lo, hi], axis=1)
+
+
 def attend_kernel(
     dims,
     tok, gh, w2, vecs, bq, tabs, first,
-    x_o, g_o, wa_o, wi_o, wo_o, att_o, dqkv_o,
-    xs, h1s, was, gs, win, qs, das, acc, down,
-    rcv, lsem, tsem, psem, zsem, zrec, ksem, dsem,
+    x_o, g_o, wa_o, wi_o, wo_o, att_o, dq_o, dwin_o,
+    xs, h1s, was, gs, win, qs, das, acc, lsem, tsem, psem, zsem, zrec, ksem,
 ):
     R, D, feats, dp, reach = dims
     f = lax.axis_index("fsdp")
@@ -280,24 +226,27 @@
 
     pair_copy(0).start()
     send_own(0)
+    pair_copy(1).start()
+    pair_copy(2).start()
     rows_x(0, tok, x_o).start()
+    send_own(1)
     own_copy(0).start()
     rows_own(0, tok, x_o).start()
     rows_own(1, gh, g_o).start()
-    send_mate(0)
-    rows_x(1, gh, g_o).start()
-    pair_copy(1).start()
-    pair_copy(2).start()
     own_copy(1).start()
     own_copy(2).start()
+    send_mate(0)
+    send_own(2)
+    rows_x(1, gh, g_o).start()
+    arrive(0, 1)
+    send_mate(1)
     rows_x(0, tok, x_o).wait_recv()
     rows_c(0, x_o).start()
-    send_own(1)
     rows_c(0, x_o).wait_recv()
     rows_own(0, tok, x_o).wait()
     load_x = pltpu.make_async_copy(x_o, xs, lsem.at[5])
     load_x.start()
-    arrive(0, 1)
+    send_mate(2)
     load_x.wait()
 
     def norm_block(b, _):
@@ -310,19 +259,16 @@
         return 0
 
     lax.fori_loop(0, nb // 2, norm_block, 0)
-    for k in range(2, dp):
+    arrive(0, 2)
+    lax.fori_loop(nb // 2, nb, norm_block, 0)
+    for k in range(3, dp):
         arrive(0, k)
-        if k == 2:
-            send_mate(1)
-    lax.fori_loop(nb // 2, nb, norm_block, 0)
     own_copy(0).wait()
     load_w = pltpu.make_async_copy(wa_o, was, lsem.at[5])
     load_w.start()
+    arrive(1, 1)
     rows_x(1, gh, g_o).wait_recv()
     rows_c(1, g_o).start()
-    send_own(2)
-    send_mate(2)
-    arrive(1, 1)
     rows_c(1, g_o).wait_recv()
     rows_own(1, gh, g_o).wait()
     load_g = pltpu.make_async_copy(g_o, gs, lsem.at[6])
@@ -330,19 +276,13 @@
     load_w.wait()
     load_g.wait()
 
-    def turn(u, at, sign):
-        lo, hi = u[:, :128], u[:, 128:]
-        a = pltpu.roll(lo, ROT // 2, 1) * tabs[1, at, :] + pltpu.roll(lo, 128 - ROT // 2, 1) * tabs[2, at, :]
-        lo = lo * tabs[0, at, :] + (a if sign > 0 else -a)
-        return jnp.concatenate([lo, hi], axis=1)
-
     scale = 1.0 / math.sqrt(HDIM)
 
     def proj_block(b, _):
         at = pl.ds(pl.multiple_of(b * qb, qb), qb)
         y = plain(h1s[at, :], was[:, : 3 * HDIM]) + bq[...]
-        qs[at, :] = (turn(y[:, :HDIM], at, 1).astype(BF16).astype(F32) * scale).astype(BF16)
-        win[reach, at, :HDIM] = turn(y[:, HDIM : 2 * HDIM], at, 1).astype(BF16)
+        qs[at, :] = (turn(y[:, :HDIM], tabs, at, 1).astype(BF16).astype(F32) * scale).astype(BF16)
+        win[reach, at, :HDIM] = turn(y[:, HDIM : 2 * HDIM], tabs, at, 1).astype(BF16)
         win[reach, at, HDIM:] = y[:, 2 * HDIM :].astype(BF16)
         das[at, :] = plain(gs[at, :], was[:, 3 * HDIM :]).astype(BF16)
         return 0
@@ -398,7 +338,7 @@
         delta = jnp.sum(p * dpr, axis=1, keepdims=True)
         ds = (p * (dpr - delta)).astype(BF16)
         dq = plain(ds, keys) * scale
-        dqkv_o[at, :HDIM] = turn(dq, at, -1).astype(BF16)
+        dq_o[at, :] = turn(dq, tabs, at, -1).astype(BF16)
         acc[keys_at, :HDIM] += inner(ds, q)
         acc[keys_at, HDIM:] += inner(pb, da)
         return 0
@@ -409,39 +349,11 @@
         arrive(1, k)
     lax.fori_loop(nb // 2, nb, attend_block, 0)
 
-    def down_copy(r):
-        return rc(down.at[r], rcv.at[r], dsem.at[0, r], dsem.at[1, r], dirs[1])
-
     for r in range(reach + 1):
-        at = pl.ds(r * plane, plane)
-        if r > 0:
-            @pl.when(has[0])
-            def _():
-                down_copy(r - 1).wait_recv()
-                acc[at, :] += rcv[r - 1].astype(F32)
-        if r < reach:
-            down[r] = acc[at, :].astype(BF16)
-
-            @pl.when(has[1])
-            def _():
-                down_copy(r).start()
-        else:
-            def tail_block(b, _):
-                here = pl.ds(pl.multiple_of(b * qb, qb), qb)
-                a = acc[pl.ds(pl.multiple_of(reach * plane + b * qb, qb), qb), :]
-                dqkv_o[here, HDIM : 2 * HDIM] = turn(a[:, :HDIM], here, -1).astype(BF16)
-                dqkv_o[here, 2 * HDIM :] = a[:, HDIM:].astype(BF16)
-                return 0
-
-            lax.fori_loop(0, nb, tail_block, 0)
-        if r == 0:
-            for k in range(3, dp):
-                arrive(2, k)
-
-    for r in range(reach):
-        @pl.when(has[1])
-        def _():
-            down_copy(r).wait_send()
+        dwin_o[r] = acc[pl.ds(r * plane, plane), :].astype(BF16)
+    for k in range(3, dp):
+        arrive(2, k)
+
     for k in range(reach):
         @pl.when((d >= k) & has[0])
         def _():
@@ -476,10 +388,11 @@
         out_shape=[
             sds((plane, D), BF16), sds((plane, D), BF16),
             sds((D, gw), BF16), sds((D, gw), BF16), sds((D, gw), BF16),
-            sds((plane, HDIM), BF16), sds((plane, 3 * HDIM), BF16),
+            sds((plane, HDIM), BF16), sds((plane, HDIM), BF16),
+            sds((reach + 1, plane, 2 * HDIM), BF16),
         ],
         in_specs=[ANY, ANY, ANY, VMEM, VMEM, VMEM, VMEM],
-        out_specs=[ANY] * 5 + [VMEM] * 2,
+        out_specs=[ANY] * 5 + [VMEM] * 3,
         scratch_shapes=[
             pltpu.VMEM((plane, D), BF16),
             pltpu.VMEM((plane, D), BF16),
@@ -489,21 +402,388 @@
             pltpu.VMEM((plane, HDIM), BF16),
             pltpu.VMEM((plane, HDIM), BF16),
             pltpu.VMEM(((reach + 1) * plane, 2 * HDIM), F32),
-            pltpu.VMEM((reach, plane, 2 * HDIM), BF16),
-            pltpu.VMEM((reach, plane, 2 * HDIM), BF16),
             pltpu.SemaphoreType.DMA((8,)),
             pltpu.SemaphoreType.DMA((2, 4)),
             pltpu.SemaphoreType.DMA((2, GROUPS)),
             pltpu.SemaphoreType.DMA((GROUPS, dp, 2, 2)),
             pltpu.SemaphoreType.DMA((GROUPS, 2 * dp)),
             pltpu.SemaphoreType.DMA((2, reach + 1)),
-            pltpu.SemaphoreType.DMA((2, reach)),
         ],
         compiler_params=pltpu.CompilerParams(
             collective_id=4, has_side_effects=True, vmem_limit_bytes=62 << 20
         ),
         name="attend",
     )(tok, gh, w2, vecs, bq, tabs, first)
+
+
+def branch_kernel(
+    dims,
+    x_i, g_i, wa_i, wi_i, wo_i, att, dq_i, dwin_i, vecs, bin_, tabs,
+    mixed_o, u_o, sums_o, own_o, oth_o,
+    xs, gs, wi, wo, wd, act, dpre, dqkv, rcv, dtmp, up, tpr0, tpr1, tpr2, rs, mean, rstd,
+    lsem, dsem, ssem, rsem, fsem, osem, tsem, near_ok, far_ok, mate_ok,
+):
+    R, D, feats, dp, reach = dims
+    f = lax.axis_index("fsdp")
+    t = lax.axis_index("tp")
+    d, i = f // 2, lax.rem(f, 2)
+    plane, pf = 2 * R, 2 * feats
+    qb = min(256, plane)
+    nb = plane // qb
+    fb = min(256, pf)
+    gw = wi.shape[1]
+    pw = up.shape[2]
+    mate = (f + 1 - 2 * i, t)
+    tn, tf = t + 1 - 2 * lax.rem(t, 2), lax.rem(t + 2, 4)
+    near, far = (f, tn), (f, tf)
+    dirs = ((f + 2, t), (f - 2, t))
+    has = (d + 1 < dp, d >= 1)
+
+    barrier = pltpu.get_barrier_semaphore()
+    for who in (mate, near, far):
+        pl.semaphore_signal(barrier, 1, device_id=who, device_id_type=MESH)
+    for k in range(2):
+        @pl.when(has[k])
+        def _():
+            pl.semaphore_signal(barrier, 1, device_id=dirs[k], device_id_type=MESH)
+    pl.semaphore_wait(barrier, 3 + has[0].astype(jnp.int32) + has[1].astype(jnp.int32))
+
+    def rc(src, dst, ss, rs_, who):
+        return pltpu.make_async_remote_copy(
+            src_ref=src, dst_ref=dst, send_sem=ss, recv_sem=rs_, device_id=who, device_id_type=MESH
+        )
+
+    def down_copy(r):
+        src = dwin_i.at[0] if r == 0 else dtmp
+        return rc(src, rcv.at[r], dsem.at[0, r], dsem.at[1, r], dirs[1])
+
+    @pl.when(d >= reach)
+    def _():
+        down_copy(0).start()
+
+    loads = [
+        pltpu.make_async_copy(src, dst, lsem.at[n])
+        for n, (src, dst) in enumerate(
+            (
+                (x_i, xs), (wi_i, wi), (g_i, gs), (wo_i, wo),
+                (wa_i.at[:, pl.ds(3 * HDIM, HDIM)], wd),
+                (dq_i, dqkv.at[:, pl.ds(0, HDIM)]),
+                (dwin_i.at[1], dtmp),
+            )
+        )
+    ]
+    for c in loads:
+        c.start()
+    sums_o[...] = jnp.zeros_like(sums_o)
+
+    def rows(b):
+        return pl.ds(pl.multiple_of(b * qb, qb), qb)
+
+    loads[0].wait()
+
+    def stat_block(b, _):
+        x = xs[rows(b), :].astype(F32)
+        m = jnp.mean(x, axis=-1, keepdims=True)
+        c = x - m
+        mean[rows(b), :] = m
+        rstd[rows(b), :] = lax.rsqrt(jnp.mean(c * c, axis=-1, keepdims=True) + EPS)
+        return 0
+
+    lax.fori_loop(0, nb, stat_block, 0)
+    for c in loads[1:5]:
+        c.wait()
+
+    def hat(at):
+        return (xs[at, :].astype(F32) - mean[at, :]) * rstd[at, :]
+
+    def ffn_block(b, _):
+        at = rows(b)
+        h2 = (hat(at) * vecs[2:3, :] + vecs[3:4, :]).astype(BF16)
+        pre = plain(h2, wi[...]) + bin_[...]
+        cdf = 0.5 * (1.0 + lax.erf(pre * (1.0 / math.sqrt(2.0))))
+        a = (pre * cdf).astype(BF16)
+        act[at, :] = a
+        slope = cdf + pre * jnp.exp(-0.5 * pre * pre) * (1.0 / math.sqrt(2.0 * math.pi))
+        g = gs[at, :]
+        dp_b = (plain(g, wo[...]) * slope).astype(BF16)
+        dpre[at, :] = dp_b
+        sums_o[5:6, :gw] += jnp.sum(dp_b.astype(F32), axis=0, keepdims=True)
+        sums_o[4:5, :] += jnp.sum(g.astype(F32), axis=0, keepdims=True)
+        for c in range(4):
+            cols = slice(c * pw, (c + 1) * pw)
+            y = against(att[at, :], wd[cols, :]) + against(a, wo[cols, :])
+            up[c, at, :] = y.astype(BF16)
+        return 0
+
+    def down_add(r):
+        def block(b, _):
+            at = rows(b)
+            dtmp[at, :] = (dtmp[at, :].astype(F32) + rcv[r - 1, at, :].astype(F32)).astype(BF16)
+            return 0
+
+        @pl.when(has[0] & (d >= reach - r))
+        def _():
+            down_copy(r - 1).wait_recv()
+            lax.fori_loop(0, nb, block, 0)
+
+    lax.fori_loop(0, nb // 2, ffn_block, 0)
+    loads[5].wait()
+    loads[6].wait()
+    for r in range(1, reach):
+        down_add(r)
+
+        @pl.when(d >= reach - r)
+        def _():
+            down_copy(r).start()
+
+        if r == 1:
+            lax.fori_loop(nb // 2, nb, ffn_block, 0)
+
+        @pl.when(d >= reach - r)
+        def _():
+            down_copy(r).wait_send()
+
+        more = pltpu.make_async_copy(dwin_i.at[r + 1], dtmp, lsem.at[6])
+        more.start()
+        more.wait()
+
+    def near_copy(j):
+        return rc(up.at[tn if j == 0 else lax.rem(tn + 2, 4)], tpr0.at[j], tsem.at[0, j], tsem.at[1, j], near)
+
+    def far_copy():
+        return rc(up.at[tf], tpr1, tsem.at[0, 2], tsem.at[1, 2], far)
+
+    def mate_copy():
+        return rc(up.at[t, pl.ds((1 - i) * R, R), :], tpr2, tsem.at[0, 3], tsem.at[1, 3], mate)
+
+    def tp_near(second):
+        if second:
+            pl.semaphore_wait(near_ok, 1)
+        near_copy(0).start()
+        near_copy(1).start()
+
+    def tp_far(second):
+        def block(b, _):
+            at = rows(b)
+            up[tf, at, :] = (up[tf, at, :].astype(F32) + tpr0[1, at, :].astype(F32)).astype(BF16)
+            return 0
+
+        near_copy(1).wait_recv()
+        lax.fori_loop(0, nb, block, 0)
+        if second:
+            pl.semaphore_wait(far_ok, 1)
+        far_copy().start()
+
+    def tp_mate(second):
+        def block(b, _):
+            at = rows(b)
+            v = up[t, at, :].astype(F32) + tpr0[0, at, :].astype(F32) + tpr1[at, :].astype(F32)
+            up[t, at, :] = v.astype(BF16)
+            return 0
+
+        near_copy(0).wait_recv()
+        far_copy().wait_recv()
+        lax.fori_loop(0, nb, block, 0)
+        if not second:
+            pl.semaphore_signal(near_ok, 1, device_id=near, device_id_type=MESH)
+            pl.semaphore_signal(far_ok, 1, device_id=far, device_id_type=MESH)
+        if second:
+            pl.semaphore_wait(mate_ok, 1)
+        mate_copy().start()
+
+    def tp_last(second, out):
+        mate_copy().wait_recv()
+        mine = up[t, pl.ds(pl.multiple_of(i * R, R), R), :].astype(F32)
+        out[...] = mine + tpr2[...].astype(F32)
+        if not second:
+            pl.semaphore_signal(mate_ok, 1, device_id=mate, device_id_type=MESH)
+        near_copy(0).wait_send()
+        near_copy(1).wait_send()
+        far_copy().wait_send()
+        mate_copy().wait_send()
+
+    def grad_part(g, p, c):
+        cols = pl.ds(pl.multiple_of(p * pf + c * fb, fb), fb)
+        if g == 2:
+            return inner(gs[:, cols], act[...])
+        z = (xs[:, cols].astype(F32) - mean[...]) * rstd[...]
+        n = 2 if g == 1 else 0
+        h = (z * vecs[n : n + 1, cols] + vecs[n + 1 : n + 2, cols]).astype(BF16)
+        if g == 1:
+            return inner(h, dpre[...])
+        return jnp.concatenate([inner(h, dqkv[...]), inner(gs[:, cols], att[...])], axis=1)
+
+    def rs_copy(g, k, way):
+        p = d + k * (1 - 2 * way)
+        to = jnp.where((way == 1) & (k == 1), dp, p)
+        who = (f + 2 - 4 * way, t)
+        return rc(rs.at[g, p], rs.at[g, to], ssem.at[g, k, way], rsem.at[g, to], who)
+
+    def rs_wait(g, p):
+        return rc(rs.at[g, p], rs.at[g, p], ssem.at[g, 0, 0], rsem.at[g, p], mate)
+
+    def add_part(g, p):
+        def block(c, _):
+            at = pl.ds(pl.multiple_of(c * fb, fb), fb)
+            rs[g, p, at, :] = (rs[g, p, at, :].astype(F32) + grad_part(g, p, c)).astype(BF16)
+            return 0
+
+        lax.fori_loop(0, pf // fb, block, 0)
+
+    def stage(g, k):
+        def go(way, _):
+            p = d + k * (1 - 2 * way)
+            came = jnp.where(way == 0, d >= 1, d + 1 < dp)
+
+            @pl.when((p >= 0) & (p < dp))
+            def _():
+                @pl.when(came)
+                def _():
+                    rs_wait(g, p).wait_recv()
+
+                @pl.when(jnp.logical_not(came))
+                def _():
+                    rs[g, p] = jnp.zeros((pf, gw), BF16)
+
+                add_part(g, p)
+                rs_copy(g, k, way).start()
+
+            return 0
+
+        lax.fori_loop(0, 2, go, 0)
+
+    def own_copy(g):
+        return pltpu.make_async_copy(rs.at[g, d, pl.ds(i * feats, feats), :], own_o.at[g], osem.at[g, 0])
+
+    def oth_copy(g):
+        return rc(rs.at[g, d, pl.ds((1 - i) * feats, feats), :], oth_o.at[g], osem.at[g, 1], osem.at[g, 2], mate)
+
+    def final(g):
+        @pl.when(d >= 1)
+        def _():
+            rs_wait(g, d).wait_recv()
+
+        @pl.when(d < 1)
+        def _():
+            rs[g, d] = jnp.zeros((pf, gw), BF16)
+
+        @pl.when(d + 1 < dp)
+        def _():
+            rs_wait(g, dp).wait_recv()
+
+        @pl.when(d + 1 >= dp)
+        def _():
+            rs[g, dp] = jnp.zeros((pf, gw), BF16)
+
+        def block(c, _):
+            at = pl.ds(pl.multiple_of(c * fb, fb), fb)
+            v = rs[g, d, at, :].astype(F32) + rs[g, dp, at, :].astype(F32)
+            rs[g, d, at, :] = (v + grad_part(g, d, c)).astype(BF16)
+            return 0
+
+        lax.fori_loop(0, pf // fb, block, 0)
+        own_copy(g).start()
+        oth_copy(g).start()
+
+    def e_block(b, _):
+        at = rows(b)
+        z = hat(at)
+        e1 = against(dqkv[at, :], wo[:, : 3 * HDIM])
+        sums_o[0:1, :] += jnp.sum(e1 * z, axis=0, keepdims=True)
+        sums_o[1:2, :] += jnp.sum(e1, axis=0, keepdims=True)
+        u = e1 * vecs[0:1, :]
+        e2 = against(dpre[at, :], wi[...])
+        sums_o[2:3, :] += jnp.sum(e2 * z, axis=0, keepdims=True)
+        sums_o[3:4, :] += jnp.sum(e2, axis=0, keepdims=True)
+        u = (u + e2 * vecs[2:3, :]).astype(BF16)
+        for c in range(4):
+            up[c, at, :] = u[:, c * pw : (c + 1) * pw]
+        sums_o[6:7, : 3 * HDIM] += jnp.sum(dqkv[at, :].astype(F32), axis=0, keepdims=True)
+        return 0
+
+    def tail_block(b, _):
+        at = rows(b)
+        a = dtmp[at, :].astype(F32)
+        dqkv[at, HDIM : 2 * HDIM] = turn(a[:, :HDIM], tabs, at, -1).astype(BF16)
+        dqkv[at, 2 * HDIM :] = a[:, HDIM:].astype(BF16)
+        return 0
+
+    tp_near(False)
+    load_a = pltpu.make_async_copy(wa_i, wo, lsem.at[3])
+    load_a.start()
+    for k in range(dp - 1, 2, -1):
+        stage(2, k)
+        stage(1, k)
+    tp_far(False)
+    down_add(reach)
+    lax.fori_loop(0, nb, tail_block, 0)
+    stage(2, 2)
+    stage(1, 2)
+    tp_mate(False)
+    stage(2, 1)
+    tp_last(False, mixed_o)
+    load_a.wait()
+    lax.fori_loop(0, nb, e_block, 0)
+    tp_near(True)
+    stage(1, 1)
+    for k in range(dp - 1, 2, -1):
+        stage(0, k)
+    tp_far(True)
+    stage(0, 2)
+    tp_mate(True)
+    final(2)
+    stage(0, 1)
+    final(1)
+    tp_last(True, u_o)
+    final(0)
+
+    @pl.when(d >= reach)
+    def _():
+        down_copy(0).wait_send()
+    for g in range(GROUPS):
+        for k in range(1, dp):
+            @pl.when(d + k < dp)
+            def _():
+                rs_copy(g, k, 0).wait_send()
+
+            @pl.when(d >= k)
+            def _():
+                rs_copy(g, k, 1).wait_send()
+        own_copy(g).wait()
+        oth_copy(g).wait()
+
+
+def branch(x, g, wa, wi, wo, att, dq, dwin, vecs, b_in, tabs, dims):
+    R, D, feats, dp, reach = dims
+    plane, pf = 2 * R, 2 * feats
+    gw = wi.shape[1]
+    pw = D // 4
+    sds = jax.ShapeDtypeStruct
+    vm = pltpu.VMEM
+    dma = pltpu.SemaphoreType.DMA
+    return pl.pallas_call(
+        functools.partial(branch_kernel, dims),
+        out_shape=[
+            sds((R, pw), F32), sds((R, pw), F32), sds((8, D), F32),
+            sds((GROUPS, feats, gw), BF16), sds((GROUPS, feats, gw), BF16),
+        ],
+        in_specs=[ANY] * 5 + [VMEM, ANY, ANY, VMEM, VMEM, VMEM],
+        out_specs=[VMEM] * 3 + [ANY] * 2,
+        scratch_shapes=[
+            vm((plane, D), BF16), vm((plane, D), BF16), vm((D, gw), BF16), vm((D, gw), BF16),
+            vm((D, HDIM), BF16), vm((plane, gw), BF16), vm((plane, gw), BF16),
+            vm((plane, 3 * HDIM), BF16), vm((reach, plane, 2 * HDIM), BF16), vm((plane, 2 * HDIM), BF16),
+            vm((4, plane, pw), BF16), vm((2, plane, pw), BF16), vm((plane, pw), BF16), vm((R, pw), BF16),
+            vm((GROUPS, dp + 1, pf, gw), BF16), vm((plane, 1), F32), vm((plane, 1), F32),
+            dma((7,)), dma((2, reach)), dma((GROUPS, dp, 2)), dma((GROUPS, dp + 1)),
+            dma((1,)), dma((GROUPS, 3)), dma((2, 4)),
+            pltpu.SemaphoreType.REGULAR, pltpu.SemaphoreType.REGULAR, pltpu.SemaphoreType.REGULAR,
+        ],
+        compiler_params=pltpu.CompilerParams(
+            collective_id=5, has_side_effects=True, vmem_limit_bytes=63 << 20
+        ),
+        name="branch",
+    )(x, g, wa, wi, wo, att, dq, dwin, vecs, b_in, tabs)
 
 
 def on_device(
@@ -597,55 +877,21 @@
         ]
     )
     vecs = jnp.stack([gain1, shift1, gain2, shift2] + [jnp.zeros_like(gain1)] * 4)
-    x_b, grad_b, w_att, w_in, w_out, att_b, d_qkv = attend(
-        tokens, grad_here, w2, vecs, b_qkv.reshape(1, -1), tabs, first[:, None],
-        (rows, width, feats, dp, reach),
-    )
-    w_qkv, w_dense = w_att[:, : 3 * HDIM], w_att[:, 3 * HDIM :]
-    x = x_b.astype(F32)
-    mean = jnp.mean(x, axis=-1, keepdims=True)
-    centred = x - mean
-    spread = jnp.mean(centred * centred, axis=-1, keepdims=True)
-    rstd = lax.rsqrt(spread + EPS)
-    xhat = centred * rstd
-    h_one = (xhat * gain1 + shift1).astype(BF16)
-    h_two = (xhat * gain2 + shift2).astype(BF16)
-
-    pre = plain(h_two, w_in) + b_in
-    act, gelu_pull = jax.vjp(lambda u: jax.nn.gelu(u, approximate=False), pre)
-    act_b = act.astype(BF16)
-    d_pre = gelu_pull(plain(grad_b, w_out))[0].astype(BF16)
-
-    partial_value = against(att_b, w_dense) + against(act_b, w_out)
-    share = tp_scatter(partial_value, t, tps)
-    share = half_of(share, i, 0) + swap(half_of(share, 1 - i, 0).astype(BF16)).astype(F32)
+    dims = (rows, width, feats, dp, reach)
+    x_b, g_b, w_a, w_i, w_o, att, dq, dwin = attend(
+        tokens, grad_here, w2, vecs, b_qkv.reshape(1, -1), tabs, first[:, None], dims
+    )
+    share, u_here, sums, own, other = branch(
+        x_b, g_b, w_a, w_i, w_o, att, dq, dwin, vecs, b_in.reshape(1, -1), tabs, dims
+    )
     part_w = width // tps
     offset = t * part_w
     cut = lambda vec: lax.dynamic_slice_in_dim(vec, offset, part_w, vec.ndim - 1)
-    mixed = (cut(tokens).astype(F32) + share + cut(b_dense) + cut(b_out)).astype(BF16)
-
-    g_out = reduce_planes(inner(grad_b, act_b), d, dp)
-    g_in = reduce_planes(inner(h_two, d_pre), d, dp)
-    g_att = reduce_planes(
-        jnp.concatenate([inner(h_one, d_qkv), inner(grad_b, att_b)], axis=1), d, dp
-    )
-    e_two = against(d_pre, w_in)
-    e_one = against(d_qkv, w_qkv)
-    u = e_one * gain1 + e_two * gain2
-    u_here = tp_scatter(u, t, tps)
-    u_here = half_of(u_here, i, 0) + swap(half_of(u_here, 1 - i, 0).astype(BF16)).astype(F32)
-    xhat_here = cut(half_of(xhat, i, 0))
-    sums = jnp.stack([jnp.sum(u_here, axis=1), jnp.sum(u_here * xhat_here, axis=1)])
-    sums = tp_sum(sums, tps) / width
-    dx = half_of(rstd, i, 0) * (u_here - sums[0][:, None] - xhat_here * sums[1][:, None])
-    tokens_grad = (cut(carried) + dx).astype(BF16)
-
-    def pair_back(grad):
-        own = half_of(grad, i, 0)
-        got = swap(half_of(grad, 1 - i, 0).astype(BF16)).astype(F32)
-        return jnp.where(i == 0, jnp.stack([own, got], 1), jnp.stack([got, own], 1))
-
-    g_att, g_in, g_out = pair_back(g_att), pair_back(g_in), pair_back(g_out)
+    x_here = cut(tokens).astype(F32)
+    mixed = (x_here + share + cut(b_dense) + cut(b_out)).astype(BF16)
+
+    both = jnp.where(i == 0, jnp.stack([own, other], 2), jnp.stack([other, own], 2)).astype(F32)
+    g_att, g_in, g_out = both[0], both[1], both[2]
     qkv_weight_grad = (
         g_att[:, :, : 3 * HDIM].reshape(feats, 2, 3, HDIM).transpose(0, 2, 1, 3).reshape(feats, 3, head_cols)
     )
@@ -653,19 +899,11 @@
     fc_in_weight_grad = g_in.reshape(feats, units)
     fc_out_weight_grad = g_out.reshape(feats, units).T
 
-    norms = jnp.stack(
-        [
-            jnp.sum(e_one * xhat, axis=0),
-            jnp.sum(e_one, axis=0),
-            jnp.sum(e_two * xhat, axis=0),
-            jnp.sum(e_two, axis=0),
-            jnp.sum(grad_here.astype(F32), axis=0),
-        ]
-    )
+    norms = sums[:5]
     norms = norms.reshape(5, shards, feats).transpose(1, 0, 2).reshape(shards, 5 * feats)
-    in_b = jnp.where(jnp.arange(2)[:, None] == i, jnp.sum(d_pre.astype(F32), axis=0)[None], 0.0)
+    in_b = jnp.where(jnp.arange(2)[:, None] == i, sums[5, : units // 2][None], 0.0)
     in_b = in_b.reshape(ub[0], shards, ub[1]).transpose(1, 0, 2).reshape(shards, ub[0] * ub[1])
-    qkv_b = jnp.sum(d_qkv.astype(F32), axis=0).reshape(3, 1, HDIM)
+    qkv_b = sums[6, : 3 * HDIM].reshape(3, 1, HDIM)
     qkv_b = jnp.where(jnp.arange(2)[None, :, None] == i, qkv_b, 0.0)
     qkv_b = qkv_b.reshape(3, 2, shards, hd).transpose(2, 0, 1, 3).reshape(shards, nq)
     small = jnp.concatenate([norms, in_b, qkv_b], axis=1)
@@ -673,9 +911,25 @@
     lanes = -(-size // 1024) * 128
     small = jnp.pad(small, ((0, 0), (0, 8 * lanes - size))).reshape(shards, 8, lanes)
     small = jnp.sum(exchange(small, "fsdp", True, 2), axis=0).reshape(8 * lanes)
-    norm_grads = small[: 4 * feats].reshape(8, feats // 2)
-    norm_grads = jnp.sum(exchange(norm_grads, "tp", False, 3), axis=0).reshape(4, feats)
-    bias_grad = small[4 * feats : 5 * feats]
+    x_rows = tokens.astype(F32)
+    mean = jnp.mean(x_rows, axis=-1, keepdims=True)
+    spread = jnp.mean((x_rows - mean) ** 2, axis=-1, keepdims=True)
+    rstd = lax.rsqrt(spread + EPS)
+    xhat_here = (x_here - mean) * rstd
+    mine = jnp.concatenate(
+        [small[: 4 * feats], jnp.sum(u_here, axis=1), jnp.sum(u_here * xhat_here, axis=1)]
+    )
+    size = mine.shape[0]
+    lanes = -(-size // 1024) * 128
+    mine = jnp.pad(mine, (0, 8 * lanes - size)).reshape(8, lanes)
+    mine = jnp.sum(exchange(mine, "tp", False, 3), axis=0).reshape(8 * lanes)
+    norm_grads = mine[: 4 * feats].reshape(4, feats)
+    at = 4 * feats
+    mean_u = (mine[at : at + rows] / width)[:, None]
+    mean_ux = (mine[at + rows : at + 2 * rows] / width)[:, None]
+    dx = rstd * (u_here - mean_u - xhat_here * mean_ux)
+    tokens_grad = (cut(cotangent).astype(F32) * row_scale[:, None] + dx).astype(BF16)
+    bias_grad = small[4 * feats : 5 * feats] * 0.5
     in_bias_grad = small[5 * feats : 5 * feats + ub[0] * ub[1]].reshape(ub)
     at = 5 * feats + ub[0] * ub[1]
     qkv_bias_grad = small[at : at + nq].reshape(3, heads_here, hd)

time: 807 us -> 632 us (0.78)
  Pallas kernels: 334 us -> 570 us
  starting transfers between devices: 98.8 us -> 0 us
  waiting for transfers between devices: 95.9 us -> 0 us
  matrix products: 83 us -> 0 us
  local copies, waits for them, and re-layouts: 108 us -> 32.9 us
  other arithmetic: 76.6 us -> 21 us
    pallas_call x0 -> x1, Pallas kernels: none -> 315 us  [branch(): pl.pallas_call(functools.partial(branch_kernel, dims), out_shape=[sds((R,...]
    ppermute x29 -> x0, starting transfers between devices: 98.8 us -> none  [the longest x18 89.1 us: planes(): return lax.ppermute(value, 'fsdp', pairs)]
    ppermute x29 -> x0, waiting for transfers between devices: 95.9 us -> none  [the longest x18 64.3 us: planes(): return lax.ppermute(value, 'fsdp', pairs)]
    dot_general x10 -> x0, matrix products: 83 us -> none  [mm(): lax.dot_general(left, right, (dims, ((), ())), preferred_element_type=F32)]
    pallas_call x1, Pallas kernels: 301 us -> 226 us  [attend(): pl.pallas_call(functools.partial(attend_kernel, dims), out_shape=[sds((pl...]
    dynamic_slice x5 -> x0, local copies, waits for them, and re-layouts: 30.7 us -> none  [the longest x3 19.1 us: tp_scatter(): keep = lax.dynamic_index_in_dim(view, mine, 2, keepdims=False)]
    convert_element_type x12 -> x3, other arithmetic: 34.1 us -> 7.02 us  [the longest x1 3.03 us: on_device(): (cut(cotangent).astype(F32) * row_scale[:, None] + dx).astype(BF16)]
    add x8 -> x0, other arithmetic: 16 us -> none  [the longest x4 10.2 us: tp_scatter(): value = keep.astype(F32) + got.astype(F32)]
  transfers between devices with their start and end apart: 29 -> 0, of which waited for: 10 -> 0; matrix products, arithmetic and copies ran while one was open for 20% -> 0% of each run, Pallas kernels for 3% -> 0%
where the time goes in v3:
time: 632 us; the launch traced here: 625 us
  Pallas kernels  570 us (90%)
  local copies, waits for them, and re-layouts  32.9 us (5%)
  other arithmetic  21 us (3%)
    pallas_call x1, Pallas kernels, branch(): pl.pallas_call(functools.partial(branch_kernel, dims), out_shape=[sds((R,...  315 us
    pallas_call x1, Pallas kernels, attend(): pl.pallas_call(functools.partial(attend_kernel, dims), out_shape=[sds((pl...  226 us
    pallas_call x3, Pallas kernels, exchange(): pl.pallas_call(functools.partial(exchange_kernel, axis, spread), out_shap...  28.5 us

profile of v3, /device:TPU:0, one launch (start us, length us, event | category | flops | bytes accessed | tf_op | source)
XLA Modules:
  0.0 625.2 jit_solution(3680005822140905902)
XLA Ops:
  0.8 1.0 convert_reduce_fusion.1
  2.3 0.8 reshape.254
  3.0 1.9 convert_reduce_fusion
  5.0 0.7 fusion.1
  6.2 0.6 reshape.230.v_ref
  6.8 10.0 %exchange.3 = f32[8,8,256]{2,1,0:T(8,128)} custom-call(f32[8,256]{1,0:T(8,128)} %reshape.230.v_ref), custom_call_target="tpu_custom_call" | custom-call | tf_op jit(solution)/shard_map/exchange/pallas_call | solution.py:92
  16.8 0.9 copy.117
  18.2 0.7 stack.33.vecs
  19.1 0.6 constant_dynamic-slice_fusion
  20.0 0.6 dynamic_slice.21
  20.9 0.9 subtract_subtract_fusion.first
  21.9 0.3 copy.95
  22.2 0.3 copy.101
  22.5 1.5 copy.98
  24.0 0.5 copy.99
  24.5 1.5 copy.100
  26.0 1.9 pad_maximum_fusion.w2
  27.9 1.9 multiply_cosine_fusion
  29.9 0.5 maximum_bitcast_fusion.1
  30.4 1.2 pad_maximum_fusion.1.tabs
  31.6 1.7 multiply_convert_fusion.gh
  33.3 226.0 %attend.1 = (bf16[1024,2048]{1,0:T(8,128)(2,1)}, bf16[1024,2048]{1,0:T(8,128)(2,1)}, bf16[2048,1024]{1,0:T(8,128)(2,1)}, bf16[2048,1024]{1,0:T(8,128)(2,1)}, bf1...) custom-call(bf16[512,2048]{1,0:T(8,128)(2,1)} %tok.1, ...), custom_call_target="tpu_custom_call" | custom-call | tf_op jit(solution)/shard_map/attend/pallas_call | solution.py:386
  259.3 315.3 %branch.1 = (f32[512,512]{1,0:T(8,128)}, f32[512,512]{1,0:T(8,128)}, f32[8,2048]{1,0:T(8,128)}, bf16[3,256,1024]{2,1,0:T(8,128)(2,1)}, bf16[3,256,1024]{2,1,0:T(8,128)(2,1)}) custom-call(bf16[1024,2048]{1,0:T(8,128)(2,1)} %get-tuple-element.27.x_i, bf16[1024,2048]{1,0:T(8,128)(2,1)} %get-tuple-element.28.g_i, bf16[2048,1024]{1,0:T(8,128)(2,1)} %get-tuple-element.29.wa_i, ...), custom_call_target="tpu_custom_call" | custom-call | tf_op jit(solution)/shard_map/branch/pallas_call | solution.py:764
  574.6 0.8 slice_reduce_fusion.2
  575.5 0.8 slice_reduce_fusion.1
  576.2 1.8 fusion.17
  578.3 1.0 copy.133
  579.6 0.7 copy.132
  580.2 8.7 %exchange.4 = f32[8,8,256]{2,1,0:T(8,128)} custom-call(f32[8,8,256]{2,1,0:T(8,128)} %bitcast.115), custom_call_target="tpu_custom_call" | custom-call | tf_op jit(solution)/shard_map/exchange/pallas_call | solution.py:92
  588.9 0.9 reduce_sum.109
  589.8 0.6 reshape.248.v_ref
  590.5 0.7 copy.115
  591.1 9.9 %exchange.5 = f32[4,8,256]{2,1,0:T(8,128)} custom-call(f32[8,256]{1,0:T(8,128)} %reshape.248.v_ref), custom_call_target="tpu_custom_call" | custom-call | tf_op jit(solution)/shard_map/exchange/pallas_call | solution.py:92
  601.0 0.8 reduce_sum.112
  601.8 0.6 fusion.19
  602.4 3.0 fusion.13
  605.5 0.6 slice.141
  606.1 2.3 fusion.2
  608.4 2.6 fusion.18
  611.0 2.9 copy.112
  613.9 0.8 slice.142
  614.7 1.3 slice.140
  616.0 1.9 copy.108
  618.1 1.6 copy.113
  619.7 1.0 copy.110
  620.7 1.9 copy.111
  622.6 1.8 copy.114
  624.4 0.6 copy.136
  (99 shorter events, 3.3 us)
Async XLA Ops:
  0.6 4.3 copy-start
  0.7 5.0 copy-start.10
  0.7 17.1 %copy-start.7 = (s32[512]{0:T(512)S(1)}, s32[512]{0:T(512)}, u32[]{:S(2)}) copy-start(s32[512]{0:T(512)} %param.30) | copy-start | bytes 6148
  0.7 5.4 copy-start.14
  0.7 5.4 copy-start.13
  0.7 5.4 copy-start.12
  0.7 5.4 copy-start.11
  0.7 5.4 copy-start.16
  0.7 5.2 copy-start.9
  0.7 5.4 copy-start.15
  0.8 19.8 %copy-start.6 = (bf16[512,256]{1,0:T(8,128)(2,1)S(1)}, bf16[512,256]{1,0:T(8,128)(2,1)}, u32[]{:S(2)}) copy-start(bf16[512,256]{1,0:T(8,128)(2,1)} %param.19) | copy-start | bytes 786436
  5.0 16.9 %copy-start.5 = (bf16[256,3,512]{2,0,1:T(8,128)(2,1)S(1)}, bf16[256,3,512]{2,0,1:T(8,128)(2,1)}, u32[]{:S(2)}) copy-start(bf16[256,3,512]{2,0,1:T(8,128)(2,1)} %param.17) | copy-start | bytes 2359300
  29.9 1.7 copy-start.2
  574.6 27.8 %copy-start.1 = (f32[512,512]{1,0:T(8,128)S(1)}, f32[512,512]{1,0:T(8,128)}, u32[]{:S(2)}) copy-start(f32[512,512]{1,0:T(8,128)} %get-tuple-element.36) | copy-start | bytes 3145732
  578.1 28.0 %copy-start.4 = (bf16[3,256,1024]{2,1,0:T(8,128)(2,1)S(1)}, bf16[3,256,1024]{2,1,0:T(8,128)(2,1)}, u32[]{:S(2)}) copy-start(bf16[3,256,1024]{2,1,0:T(8,128)(2,1)} %get-tuple-element.38) | copy-start | bytes 4718596
  589.8 34.7 %copy-start.8 = (f32[1,256]{1,0:T(1,128)}, f32[1,256]{1,0:T(1,128)S(1)}, u32[]{:S(2)}) copy-start(f32[1,256]{1,0:T(1,128)S(1)} %get-tuple-element.117) | copy-start | bytes 3076
  618.0 1.6 copy-start.3

commit v4 on v2

v4 whole, which is shorter than its diff:
```python
import functools
import math

import jax
import jax.numpy as jnp
from jax import lax
from jax.experimental import pallas as pl
from jax.experimental.pallas import tpu as pltpu
from jax.sharding import PartitionSpec as P

HDIM = 256
ROT = 64
SUBSETS = 22
SEQ_LEN = 2048
EPS = 1e-05
F32 = jnp.float32
BF16 = jnp.bfloat16
MESH = pl.DeviceIdType.MESH
ANY = pl.BlockSpec(memory_space=pl.ANY)
VMEM = pl.BlockSpec(memory_space=pltpu.VMEM)


def mm(left, right, dims):
    return lax.dot_general(left, right, (dims, ((), ())), preferred_element_type=F32)


def plain(left, right):
    return mm(left, right, ((1,), (0,)))


def inner(left, right):
    return mm(left, right, ((0,), (0,)))


def against(left, right):
    return mm(left, right, ((1,), (1,)))


def rotary_tables(positions):
    half = ROT // 2
    steps = jnp.arange(half, dtype=F32)
    freq = 1.0 / 10000.0 ** (steps * 2.0 / ROT)
    angle = positions[:, None] * freq[None, :]
    return jnp.cos(angle), jnp.sin(angle)


def locate(indices, starts):
    above = indices[:, None] >= starts[None, :]
    doc_ids = jnp.sum(above.astype(jnp.int32), axis=1) - 1
    pick = doc_ids[:, None] == jnp.arange(starts.shape[0], dtype=jnp.int32)[None, :]
    first = jnp.sum(jnp.where(pick, starts[None, :], 0), axis=1)
    return (doc_ids, (indices - first).astype(F32))


def half_of(value, which, axis):
    size = value.shape[axis] // 2
    return lax.dynamic_slice_in_dim(value, which * size, size, axis)


def exchange_kernel(axis, spread, v_ref, o_ref, ssem, rsem):
    count = o_ref.shape[0]
    me = lax.axis_index(axis)

    def peer(step):
        return lax.rem(me + step, count)

    barrier = pltpu.get_barrier_semaphore()
    for step in range(1, count):
        pl.semaphore_signal(barrier, 1, device_id={axis: peer(step)}, device_id_type=MESH)
    pl.semaphore_wait(barrier, count - 1)

    def copy(step):
        return pltpu.make_async_remote_copy(
            src_ref=v_ref.at[peer(step)] if spread else v_ref,
            dst_ref=o_ref.at[me],
            send_sem=ssem.at[step],
            recv_sem=rsem.at[step],
            device_id={axis: peer(step)},
            device_id_type=MESH,
        )

    for step in range(1, count):
        copy(step).start()
    o_ref[me] = v_ref[me] if spread else v_ref[...]
    for step in range(1, count):
        copy(step).wait()


def exchange(value, axis, spread, cid):
    count = lax.axis_size(axis)
    block = value.shape[1:] if spread else value.shape
    return pl.pallas_call(
        functools.partial(exchange_kernel, axis, spread),
        out_shape=jax.ShapeDtypeStruct((count,) + block, value.dtype),
        in_specs=[VMEM],
        out_specs=VMEM,
        scratch_shapes=[pltpu.SemaphoreType.DMA((count,)), pltpu.SemaphoreType.DMA((count,))],
        compiler_params=pltpu.CompilerParams(collective_id=cid, has_side_effects=True),
        name="exchange",
    )(value)


GROUPS = 3


def turn(u, tabs, at, sign):
    lo, hi = u[:, :128], u[:, 128:]
    a = pltpu.roll(lo, ROT // 2, 1) * tabs[1, at, :] + pltpu.roll(lo, 128 - ROT // 2, 1) * tabs[2, at, :]
    lo = lo * tabs[0, at, :] + (a if sign > 0 else -a)
    return jnp.concatenate([lo, hi], axis=1)


def block_kernel(
    dims,
    tok, gh, w2, vecs, bq, bin_, bias, tabs, first,
    wa_o, w0_o, w1_o, mixed_o, u_o, sums_o, own_o, oth_o,
    xs, gs, wbuf, win, qs, das, act, dpre, dqkv, att, rcv, dtmp, dwin, tpr0, tpr1, tpr2, rs, mean, rstd,
    lsem, tsem, psem, zsem, zrec, ksem, dsem, ssem, rsem, osem, bsem, near_ok, far_ok, mate_ok,
):
    R, D, feats, dp, reach = dims
    f = lax.axis_index("fsdp")
    t = lax.axis_index("tp")
    d, i = f // 2, lax.rem(f, 2)
    core = lax.rem(t, 2)
    plane, pf = 2 * R, 2 * feats
    qb = min(256, plane)
    nb = plane // qb
    fb = min(256, pf)
    gw = w2.shape[2] // GROUPS
    hu = gw // 2
    pw = D // 4
    tn, tf = t + 1 - 2 * core, lax.rem(t + 2, 4)
    mate, near, far = (f + 1 - 2 * i, t), (f, tn), (f, tf)
    dirs = ((f + 2, t), (f - 2, t))
    has = (d + 1 < dp, d >= 1)
    outs = (wa_o, w0_o, w1_o)
    scale = 1.0 / math.sqrt(HDIM)

    barrier = pltpu.get_barrier_semaphore()
    for who in (mate, near, far):
        pl.semaphore_signal(barrier, 1, device_id=who, device_id_type=MESH)
    for k in range(2):
        @pl.when(has[k])
        def _():
            pl.semaphore_signal(barrier, 1, device_id=dirs[k], device_id_type=MESH)
    pl.semaphore_wait(barrier, 3 + has[0].astype(jnp.int32) + has[1].astype(jnp.int32))

    def rc(src, dst, ss, rv, who):
        return pltpu.make_async_remote_copy(
            src_ref=src, dst_ref=dst, send_sem=ss, recv_sem=rv, device_id=who, device_id_type=MESH
        )

    def rows(b):
        return pl.ds(pl.multiple_of(b * qb, qb), qb)

    def slot(g, s):
        return outs[g].at[pl.ds(s * feats, feats), :]

    def part(half, g):
        return w2.at[half, :, pl.ds(g * gw, gw)]

    def pair_copy(g):
        return rc(part(1 - i, g), slot(g, f), psem.at[0, g], psem.at[1, g], mate)

    def mine_copy(g):
        return pltpu.make_async_copy(part(i, g), slot(g, f), lsem.at[g])

    def z_own(g, way):
        return rc(part(i, g), slot(g, f), zsem.at[g, 0, way, 0], zrec.at[g, f], dirs[way])

    def z_mate(g, way):
        s = f + 1 - 2 * i
        return rc(slot(g, s), slot(g, s), zsem.at[g, 0, way, 1], zrec.at[g, s], dirs[way])

    def z_fwd(g, k, way, j):
        s = (d - k) * 2 + j if way == 0 else (d + k) * 2 + j
        return rc(slot(g, s), slot(g, s), zsem.at[g, k, way, j], zrec.at[g, s], dirs[way])

    def send_own(g):
        for way in range(2):
            @pl.when(has[way])
            def _():
                z_own(g, way).start()

    def send_mate(g):
        pair_copy(g).wait_recv()
        for way in range(2):
            @pl.when(has[way])
            def _():
                z_mate(g, way).start()

    def from_dist(k, way):
        return d >= k if way == 0 else d + k < dp

    def arrive(g, k):
        for way in range(2):
            @pl.when(from_dist(k, way))
            def _():
                for j in range(2):
                    z_fwd(g, k, way, j).wait_recv()

                    @pl.when(has[way])
                    def _():
                        z_fwd(g, k, way, j).start()

    def gather_sent(g):
        pair_copy(g).wait_send()
        for way in range(2):
            @pl.when(has[way])
            def _():
                z_own(g, way).wait_send()
                z_mate(g, way).wait_send()
            for k in range(1, dp - 1):
                @pl.when(from_dist(k, way) & has[way])
                def _():
                    for j in range(2):
                        z_fwd(g, k, way, j).wait_send()

    def load(src, dst, n):
        c = pltpu.make_async_copy(src, dst, bsem.at[n])
        c.start()
        return c

    hr = R // 2

    def rows_x(a, ref, out):
        return rc(
            ref.at[pl.ds(core * hr, hr), :], out.at[pl.ds(i * R + core * hr, hr), :],
            tsem.at[a, 0], tsem.at[a, 1], mate,
        )

    def rows_c(a, out):
        at = out.at[pl.ds((1 - i) * R + core * hr, hr), :]
        return rc(at, at, tsem.at[a, 2], tsem.at[a, 3], near)

    def rows_own(a, ref, out):
        return pltpu.make_async_copy(ref, out.at[pl.ds(i * R, R), :], lsem.at[GROUPS + a])

    def rows_done(a, ref, out):
        rows_x(a, ref, out).wait_recv()
        rows_c(a, out).start()
        rows_c(a, out).wait_recv()
        rows_own(a, ref, out).wait()

    def hat(at):
        return (xs[at, :].astype(F32) - mean[at, :]) * rstd[at, :]

    def stat_block(b, _):
        x = xs[rows(b), :].astype(F32)
        m = jnp.mean(x, axis=-1, keepdims=True)
        c = x - m
        mean[rows(b), :] = m
        rstd[rows(b), :] = lax.rsqrt(jnp.mean(c * c, axis=-1, keepdims=True) + EPS)
        return 0

    def proj_block(b, _):
        at = rows(b)
        h1 = (hat(at) * vecs[0:1, :] + vecs[1:2, :]).astype(BF16)
        y = plain(h1, wbuf[:, : 3 * HDIM]) + bq[...]
        qs[at, :] = (turn(y[:, :HDIM], tabs, at, 1).astype(BF16).astype(F32) * scale).astype(BF16)
        win[reach, at, :HDIM] = turn(y[:, HDIM : 2 * HDIM], tabs, at, 1).astype(BF16)
        win[reach, at, HDIM:] = y[:, 2 * HDIM :].astype(BF16)
        return 0

    def datt_block(b, _):
        at = rows(b)
        das[at, :] = plain(gs[at, :], wbuf[:, 3 * HDIM :]).astype(BF16)
        return 0

    def ffn(h):
        mine = slice(h * hu, (h + 1) * hu)

        def block(b, _):
            at = rows(b)
            h2 = (hat(at) * vecs[2:3, :] + vecs[3:4, :]).astype(BF16)
            pre = plain(h2, wbuf[:, :hu]) + bin_[:, mine]
            cdf = 0.5 * (1.0 + lax.erf(pre * (1.0 / math.sqrt(2.0))))
            act[at, mine] = (pre * cdf).astype(BF16)
            slope = cdf + pre * jnp.exp(-0.5 * pre * pre) * (1.0 / math.sqrt(2.0 * math.pi))
            dp_b = (plain(gs[at, :], wbuf[:, hu:]) * slope).astype(BF16)
            dpre[at, mine] = dp_b
            sums_o[5:6, mine] += jnp.sum(dp_b.astype(F32), axis=0, keepdims=True)
            return 0

        lax.fori_loop(0, nb, block, 0)

    def kv_copy(k):
        return rc(win.at[reach - k], win.at[reach - k - 1], ksem.at[0, k], ksem.at[1, k + 1], dirs[0])

    def kv_recv(k):
        return rc(win.at[reach - k], win.at[reach - k], ksem.at[0, k - 1], ksem.at[1, k], dirs[0])

    def kv_step(k):
        @pl.when(d >= k)
        def _():
            kv_recv(k).wait_recv()
            if k < reach:
                @pl.when(has[0])
                def _():
                    kv_copy(k).start()

        @pl.when(d < k)
        def _():
            win[reach - k] = jnp.zeros((plane, 2 * HDIM), BF16)

    span = SEQ_LEN + qb
    base = reach * plane - SEQ_LEN

    def attention(acc, lo, hi):
        def block(b, _):
            at = rows(b)
            keys_at = pl.ds(pl.multiple_of(base + b * qb, qb), span)
            flat = win.reshape((reach + 1) * plane, 2 * HDIM)
            keys = flat[keys_at, :HDIM]
            vals = flat[keys_at, HDIM:]
            q = qs[at, :]
            s = against(q, keys)
            c = base + b * qb + lax.broadcasted_iota(jnp.int32, (qb, span), 1)
            r = reach * plane + b * qb + lax.broadcasted_iota(jnp.int32, (qb, span), 0)
            s = jnp.where((c >= first[at, :]) & (c <= r), s, -1e30)
            e = jnp.exp(s - jnp.max(s, axis=1, keepdims=True))
            p = e * (1.0 / jnp.sum(e, axis=1, keepdims=True))
            pb = p.astype(BF16)
            att[at, :] = plain(pb, vals).astype(BF16)
            da = das[at, :]
            dpr = against(da, vals)
            delta = jnp.sum(p * dpr, axis=1, keepdims=True)
            ds = (p * (dpr - delta)).astype(BF16)
            dq = plain(ds, keys) * scale
            dqkv[at, :HDIM] = turn(dq, tabs, at, -1).astype(BF16)
            acc[keys_at, :HDIM] += inner(ds, q)
            acc[keys_at, HDIM:] += inner(pb, da)
            return 0

        lax.fori_loop(lo, hi, block, 0)

    def down_copy(r):
        src = dwin.at[0] if r == 0 else dtmp
        return rc(src, rcv.at[r], dsem.at[0, r], dsem.at[1, r], dirs[1])

    def down_step(r):
        def keep(b, _):
            at = rows(b)
            dtmp[at, :] = dwin[r, at, :]
            return 0

        def add(b, _):
            at = rows(b)
            dtmp[at, :] = (dwin[r, at, :].astype(F32) + rcv[r - 1, at, :].astype(F32)).astype(BF16)
            return 0

        came = has[0] & (d >= reach - r)
        if r > 1:
            @pl.when(d >= reach - r + 1)
            def _():
                down_copy(r - 1).wait_send()

        @pl.when(came)
        def _():
            down_copy(r - 1).wait_recv()
            lax.fori_loop(0, nb, add, 0)

        @pl.when(jnp.logical_not(came))
        def _():
            lax.fori_loop(0, nb, keep, 0)

        if r < reach:
            @pl.when(d >= reach - r)
            def _():
                down_copy(r).start()

    def tail_block(b, _):
        at = rows(b)
        a = dtmp[at, :].astype(F32)
        dqkv[at, HDIM : 2 * HDIM] = turn(a[:, :HDIM], tabs, at, -1).astype(BF16)
        dqkv[at, 2 * HDIM :] = a[:, HDIM:].astype(BF16)
        return 0

    def grad_part(g, p, c):
        cols = pl.ds(pl.multiple_of(p * pf + c * fb, fb), fb)
        z = (xs[:, cols].astype(F32) - mean[...]) * rstd[...]
        n = 0 if g == 0 else 2
        h = (z * vecs[n : n + 1, cols] + vecs[n + 1 : n + 2, cols]).astype(BF16)
        if g == 0:
            return inner(h, dqkv[...]), inner(gs[:, cols], att[...])
        mine = slice((g - 1) * hu, g * hu)
        return inner(h, dpre[:, mine]), inner(gs[:, cols], act[:, mine])

    def add_part(g, p, second=None):
        cut = 3 * HDIM if g == 0 else hu

        def block(c, _):
            at = pl.ds(pl.multiple_of(c * fb, fb), fb)
            left, right = grad_part(g, p, c)
            for cols, v in ((slice(0, cut), left), (slice(cut, gw), right)):
                v = rs[g, p, at, cols].astype(F32) + v
                if second is not None:
                    v = v + rs[g, second, at, cols].astype(F32)
                rs[g, p, at, cols] = v.astype(BF16)
            return 0

        lax.fori_loop(0, pf // fb, block, 0)

    def rs_copy(g, k, way):
        p = d + k * (1 - 2 * way)
        to = jnp.where((way == 1) & (k == 1), dp, p)
        who = (f + 2 - 4 * way, t)
        return rc(rs.at[g, p], rs.at[g, to], ssem.at[g, k, way], rsem.at[g, to], who)

    def rs_wait(g, p):
        return rc(rs.at[g, p], rs.at[g, p], ssem.at[g, 0, 0], rsem.at[g, p], mate)

    def stage(g, k):
        def go(way, _):
            p = d + k * (1 - 2 * way)
            came = jnp.where(way == 0, d >= 1, d + 1 < dp)

            @pl.when((p >= 0) & (p < dp))
            def _():
                @pl.when(came)
                def _():
                    rs_wait(g, p).wait_recv()

                @pl.when(jnp.logical_not(came))
                def _():
                    rs[g, p] = jnp.zeros((pf, gw), BF16)

                add_part(g, p)
                rs_copy(g, k, way).start()

            return 0

        lax.fori_loop(0, 2, go, 0)

    def own_copy(g):
        return pltpu.make_async_copy(rs.at[g, d, pl.ds(i * feats, feats), :], own_o.at[g], osem.at[g, 0])

    def oth_copy(g):
        return rc(rs.at[g, d, pl.ds((1 - i) * feats, feats), :], oth_o.at[g], osem.at[g, 1], osem.at[g, 2], mate)

    def final(g):
        @pl.when(d >= 1)
        def _():
            rs_wait(g, d).wait_recv()

        @pl.when(d < 1)
        def _():
            rs[g, d] = jnp.zeros((pf, gw), BF16)

        @pl.when(d + 1 < dp)
        def _():
            rs_wait(g, dp).wait_recv()

        @pl.when(d + 1 >= dp)
        def _():
            rs[g, dp] = jnp.zeros((pf, gw), BF16)

        add_part(g, d, dp)
        own_copy(g).start()
        oth_copy(g).start()

    pair_copy(0).start()
    send_own(0)
    pair_copy(1).start()
    pair_copy(2).start()
    rows_x(0, tok, xs).start()
    send_own(1)
    mine_copy(0).start()
    rows_own(0, tok, xs).start()
    rows_own(1, gh, gs).start()
    mine_copy(1).start()
    mine_copy(2).start()
    sums_o[...] = jnp.zeros_like(sums_o)
    send_mate(0)
    send_own(2)
    rows_x(1, gh, gs).start()
    arrive(0, 1)
    send_mate(1)
    rows_done(0, tok, xs)
    send_mate(2)
    lax.fori_loop(0, nb, stat_block, 0)
    for k in range(2, dp):
        arrive(0, k)
    mine_copy(0).wait()
    weights = load(wa_o, wbuf, 0)
    arrive(1, 1)
    weights.wait()
    lax.fori_loop(0, nb, proj_block, 0)

    @pl.when(has[0])
    def _():
        kv_copy(0).start()

    rows_done(1, gh, gs)
    lax.fori_loop(0, nb, datt_block, 0)
    arrive(2, 1)
    arrive(1, 2)
    for k in range(1, reach):
        kv_step(k)
    for k in range(3, dp):
        arrive(1, k)
    mine_copy(1).wait()
    load(w0_o, wbuf, 0).wait()
    arrive(2, 2)
    ffn(0)
    for k in range(dp - 1, 2, -1):
        stage(1, k)
    kv_step(reach)

    def attend(acc):
        acc[...] = jnp.zeros_like(acc)
        attention(acc, 0, nb // 2)
        stage(1, 2)
        for k in range(3, dp):
            arrive(2, k)
        attention(acc, nb // 2, nb)
        for r in range(reach + 1):
            dwin[r] = acc[pl.ds(r * plane, plane), :].astype(BF16)

    pl.run_scoped(attend, pltpu.VMEM(((reach + 1) * plane, 2 * HDIM), F32))

    @pl.when(d >= reach)
    def _():
        down_copy(0).start()

    mine_copy(2).wait()
    weights = load(w1_o, wbuf, 0)
    stage(1, 1)
    weights.wait()
    ffn(1)
    for r in range(1, reach):
        down_step(r)
    for k in range(dp - 1, 2, -1):
        stage(2, k)

    def finish(up, wd):
        def out_block(b, _):
            at = rows(b)
            sums_o[4:5, :] += jnp.sum(gs[at, :].astype(F32), axis=0, keepdims=True)
            for c in range(4):
                cols = slice(c * pw, (c + 1) * pw)
                y = against(att[at, :], wd[cols, :]) + against(act[at, :], wbuf[cols, :])
                up[c, at, :] = y.astype(BF16)
            return 0

        def hidden_block(b, _):
            at = rows(b)
            e2 = against(dpre[at, :], wbuf[...])
            z = hat(at)
            sums_o[2:3, :] += jnp.sum(e2 * z, axis=0, keepdims=True)
            sums_o[3:4, :] += jnp.sum(e2, axis=0, keepdims=True)
            u = (e2 * vecs[2:3, :]).astype(BF16)
            for c in range(4):
                up[c, at, :] = u[:, c * pw : (c + 1) * pw]
            return 0

        def qkv_block(b, _):
            at = rows(b)
            e1 = against(dqkv[at, :], wbuf[:, : 3 * HDIM])
            z = hat(at)
            sums_o[0:1, :] += jnp.sum(e1 * z, axis=0, keepdims=True)
            sums_o[1:2, :] += jnp.sum(e1, axis=0, keepdims=True)
            sums_o[6:7, : 3 * HDIM] += jnp.sum(dqkv[at, :].astype(F32), axis=0, keepdims=True)
            u = e1 * vecs[0:1, :]
            for c in range(4):
                up[c, at, :] = (up[c, at, :].astype(F32) + u[:, c * pw : (c + 1) * pw]).astype(BF16)
            return 0

        def near_copy(j):
            return rc(up.at[tn if j == 0 else lax.rem(tn + 2, 4)], tpr0.at[j], tsem.at[2, j], tsem.at[3, j], near)

        def far_copy():
            return rc(up.at[tf], tpr1, tsem.at[2, 2], tsem.at[3, 2], far)

        def mate_copy():
            return rc(up.at[t, pl.ds((1 - i) * R, R), :], tpr2, tsem.at[2, 3], tsem.at[3, 3], mate)

        def tp_near(second):
            if second:
                pl.semaphore_wait(near_ok, 1)
            near_copy(0).start()
            near_copy(1).start()

        def tp_far(second):
            def block(b, _):
                at = rows(b)
                up[tf, at, :] = (up[tf, at, :].astype(F32) + tpr0[1, at, :].astype(F32)).astype(BF16)
                return 0

            near_copy(1).wait_recv()
            lax.fori_loop(0, nb, block, 0)
            if second:
                pl.semaphore_wait(far_ok, 1)
            far_copy().start()

        def tp_mate(second):
            def block(b, _):
                at = rows(b)
                v = up[t, at, :].astype(F32) + tpr0[0, at, :].astype(F32) + tpr1[at, :].astype(F32)
                up[t, at, :] = v.astype(BF16)
                return 0

            near_copy(0).wait_recv()
            far_copy().wait_recv()
            lax.fori_loop(0, nb, block, 0)
            if second:
                pl.semaphore_wait(mate_ok, 1)
            else:
                pl.semaphore_signal(near_ok, 1, device_id=near, device_id_type=MESH)
                pl.semaphore_signal(far_ok, 1, device_id=far, device_id_type=MESH)
            mate_copy().start()

        def tp_last(second):
            mate_copy().wait_recv()
            here = pl.ds(pl.multiple_of(i * R, R), R)
            v = up[t, here, :].astype(F32) + tpr2[...].astype(F32)
            if second:
                u_o[...] = v
            else:
                x = xs[here, pl.ds(pl.multiple_of(t * pw, pw), pw)].astype(F32)
                mixed_o[...] = (x + v + bias[...]).astype(BF16)
                pl.semaphore_signal(mate_ok, 1, device_id=mate, device_id_type=MESH)
            near_copy(0).wait_send()
            near_copy(1).wait_send()
            far_copy().wait_send()
            mate_copy().wait_send()

        loads = [
            load(w0_o.at[:, pl.ds(hu, hu)], wbuf.at[:, pl.ds(0, hu)], 0),
            load(w1_o.at[:, pl.ds(hu, hu)], wbuf.at[:, pl.ds(hu, hu)], 1),
            load(wa_o.at[:, pl.ds(3 * HDIM, HDIM)], wd, 2),
        ]
        final(1)
        for c in loads:
            c.wait()
        lax.fori_loop(0, nb, out_block, 0)
        tp_near(False)
        loads = [
            load(w0_o.at[:, pl.ds(0, hu)], wbuf.at[:, pl.ds(0, hu)], 0),
            load(w1_o.at[:, pl.ds(0, hu)], wbuf.at[:, pl.ds(hu, hu)], 1),
        ]
        stage(2, 2)
        tp_far(False)
        down_step(reach)
        lax.fori_loop(0, nb, tail_block, 0)
        for k in range(dp - 1, 2, -1):
            stage(0, k)
        stage(2, 1)
        tp_mate(False)
        stage(0, 2)
        tp_last(False)
        for c in loads:
            c.wait()
        lax.fori_loop(0, nb, hidden_block, 0)
        load(wa_o, wbuf, 0).wait()
        lax.fori_loop(0, nb, qkv_block, 0)
        tp_near(True)
        stage(0, 1)
        final(2)
        tp_far(True)
        tp_mate(True)
        tp_last(True)
        final(0)

    pl.run_scoped(finish, pltpu.VMEM((4, plane, pw), BF16), pltpu.VMEM((D, HDIM), BF16))

    @pl.when(d >= reach)
    def _():
        down_copy(0).wait_send()
    for k in range(reach):
        @pl.when((d >= k) & has[0])
        def _():
            kv_copy(k).wait_send()
    for a, (ref, out) in enumerate(((tok, xs), (gh, gs))):
        rows_x(a, ref, out).wait_send()
        rows_c(a, out).wait_send()
    for g in range(GROUPS):
        gather_sent(g)
        for k in range(1, dp):
            @pl.when(d + k < dp)
            def _():
                rs_copy(g, k, 0).wait_send()

            @pl.when(d >= k)
            def _():
                rs_copy(g, k, 1).wait_send()
        own_copy(g).wait()
        oth_copy(g).wait()


def block(tok, gh, w2, vecs, bq, b_in, bias, tabs, first, dims):
    R, D, feats, dp, reach = dims
    plane, pf = 2 * R, 2 * feats
    gw = w2.shape[2] // GROUPS
    pw = D // 4
    sds = jax.ShapeDtypeStruct
    vm = pltpu.VMEM
    dma = pltpu.SemaphoreType.DMA
    reg = pltpu.SemaphoreType.REGULAR
    return pl.pallas_call(
        functools.partial(block_kernel, dims),
        out_shape=[sds((D, gw), BF16)] * GROUPS
        + [sds((R, pw), BF16), sds((R, pw), F32), sds((8, D), F32)]
        + [sds((GROUPS, feats, gw), BF16)] * 2,
        in_specs=[ANY] * 3 + [VMEM] * 6,
        out_specs=[ANY] * GROUPS + [VMEM] * 3 + [ANY] * 2,
        scratch_shapes=[
            vm((plane, D), BF16), vm((plane, D), BF16), vm((D, gw), BF16),
            vm((reach + 1, plane, 2 * HDIM), BF16), vm((plane, HDIM), BF16), vm((plane, HDIM), BF16),
            vm((plane, gw), BF16), vm((plane, gw), BF16), vm((plane, 3 * HDIM), BF16), vm((plane, HDIM), BF16),
            vm((reach, plane, 2 * HDIM), BF16), vm((plane, 2 * HDIM), BF16),
            vm((reach + 1, plane, 2 * HDIM), BF16),
            vm((2, plane, pw), BF16), vm((plane, pw), BF16), vm((R, pw), BF16),
            vm((GROUPS, dp + 1, pf, gw), BF16), vm((plane, 1), F32), vm((plane, 1), F32),
            dma((GROUPS + 2,)), dma((4, 4)), dma((2, GROUPS)), dma((GROUPS, dp, 2, 2)), dma((GROUPS, 2 * dp)),
            dma((2, reach + 1)), dma((2, reach)), dma((GROUPS, dp, 2)), dma((GROUPS, dp + 1)), dma((GROUPS, 3)),
            dma((3,)), reg, reg, reg,
        ],
        compiler_params=pltpu.CompilerParams(
            collective_id=4, has_side_effects=True, vmem_limit_bytes=63 << 20
        ),
        name="block",
    )(tok, gh, w2, vecs, bq, b_in, bias, tabs, first)


def on_device(
    tokens,
    qkv_weight,
    qkv_bias,
    dense_weight,
    dense_bias,
    fc_in_weight,
    fc_in_bias,
    fc_out_weight,
    fc_out_bias,
    norm1_gain,
    norm1_shift,
    norm2_gain,
    norm2_shift,
    cotangent,
    subset_ids,
    seq_starts,
):
    rows, width = tokens.shape
    shards = lax.axis_size("fsdp")
    tps = lax.axis_size("tp")
    dp = shards // 2
    f = lax.axis_index("fsdp")
    t = lax.axis_index("tp")
    i = lax.rem(f, 2)
    d = f // 2
    total = rows * shards
    scale = 1.0 / math.sqrt(HDIM)
    feats = qkv_weight.shape[0]
    units = fc_in_weight.shape[1]
    head_cols = qkv_weight.shape[2]
    heads_here = head_cols // HDIM
    hd = qkv_bias.shape[2]
    ub = fc_in_bias.shape

    match = subset_ids[:, None] == jnp.arange(SUBSETS, dtype=jnp.int32)[None, :]
    counts = jnp.sum(match.astype(F32), axis=0)
    vecs = [norm1_gain, norm1_shift, norm2_gain, norm2_shift, dense_bias, fc_out_bias]
    pack = jnp.concatenate(
        [v.astype(F32) for v in vecs]
        + [qkv_bias.astype(F32).reshape(-1), fc_in_bias.astype(F32).reshape(-1), counts]
    )
    size = pack.shape[0]
    lanes = -(-size // 1024) * 128
    got = exchange(jnp.pad(pack, (0, 8 * lanes - size)).reshape(8, lanes), "fsdp", False, 1)
    got = got.reshape(shards, 8 * lanes)
    gain1, shift1, gain2, shift2, b_dense, b_out = [
        got[:, k * feats : (k + 1) * feats].reshape(width) for k in range(6)
    ]
    at = 6 * feats
    nq = 3 * heads_here * hd
    b_qkv = got[:, at : at + nq].reshape(shards, 3, heads_here, hd)
    b_qkv = b_qkv.transpose(1, 2, 0, 3).reshape(3, heads_here, HDIM)
    b_qkv = lax.dynamic_index_in_dim(b_qkv, i, 1, keepdims=False).reshape(3 * HDIM)
    at += nq
    b_in = got[:, at : at + units // shards].reshape(shards, ub[0], ub[1])
    b_in = half_of(b_in.transpose(1, 0, 2).reshape(units), i, 0)
    at += units // shards
    counts = jnp.sum(got[:, at : at + SUBSETS], axis=0)
    table = total / (SUBSETS * counts)
    row_scale = jnp.sum(jnp.where(match, table[None, :], 0.0), axis=1)
    carried = cotangent.astype(F32) * row_scale[:, None]
    grad_here = carried.astype(BF16)

    wi = fc_in_weight.reshape(feats, 2, 2, units // 4).transpose(1, 0, 2, 3)
    wo = fc_out_weight.reshape(2, 2, units // 4, feats).transpose(0, 3, 1, 2)
    w2 = jnp.concatenate(
        [
            qkv_weight.reshape(feats, 3, heads_here, HDIM).transpose(2, 0, 1, 3).reshape(2, feats, 3 * HDIM),
            dense_weight.reshape(heads_here, HDIM, feats).transpose(0, 2, 1),
            wi[:, :, 0], wo[:, :, 0], wi[:, :, 1], wo[:, :, 1],
        ],
        axis=2,
    )
    plane = 2 * rows
    start_row = d * plane
    reach = min(dp - 1, -(-(SEQ_LEN - 1) // plane))
    here = start_row + jnp.arange(plane, dtype=jnp.int32)
    docs_here, pos_here = locate(here, seq_starts)
    first = (here - pos_here.astype(jnp.int32)) - (start_row - reach * plane)
    cosine, sine = rotary_tables(pos_here)
    ones = jnp.ones((plane, 128 - ROT), F32)
    none = jnp.zeros((plane, 128 - ROT), F32)
    zero = jnp.zeros_like(sine)
    tabs = jnp.stack(
        [
            jnp.concatenate([cosine, cosine, ones], 1),
            jnp.concatenate([zero, sine, none], 1),
            jnp.concatenate([-sine, zero, none], 1),
        ]
    )
    vecs = jnp.stack([gain1, shift1, gain2, shift2] + [jnp.zeros_like(gain1)] * 4)
    dims = (rows, width, feats, dp, reach)
    part_w = width // tps
    offset = t * part_w
    cut = lambda vec: lax.dynamic_slice_in_dim(vec, offset, part_w, vec.ndim - 1)
    bias = (cut(b_dense) + cut(b_out)).reshape(1, -1)
    _, _, _, mixed, u_here, sums, own, other = block(
        tokens, grad_here, w2, vecs, b_qkv.reshape(1, -1), b_in.reshape(1, -1), bias, tabs, first[:, None], dims
    )
    x_here = cut(tokens).astype(F32)

    both = jnp.where(i == 0, jnp.stack([own, other], 2), jnp.stack([other, own], 2)).astype(F32)
    g_att = both[0]
    g_fc = both[1:].reshape(2, feats, 2, 2, units // 4)
    qkv_weight_grad = (
        g_att[:, :, : 3 * HDIM].reshape(feats, 2, 3, HDIM).transpose(0, 2, 1, 3).reshape(feats, 3, head_cols)
    )
    dense_weight_grad = g_att[:, :, 3 * HDIM :].reshape(feats, head_cols).T
    fc_in_weight_grad = g_fc[:, :, :, 0].transpose(1, 2, 0, 3).reshape(feats, units)
    fc_out_weight_grad = g_fc[:, :, :, 1].transpose(2, 0, 3, 1).reshape(units, feats)

    norms = sums[:5]
    norms = norms.reshape(5, shards, feats).transpose(1, 0, 2).reshape(shards, 5 * feats)
    in_b = jnp.where(jnp.arange(2)[:, None] == i, sums[5, : units // 2][None], 0.0)
    in_b = in_b.reshape(ub[0], shards, ub[1]).transpose(1, 0, 2).reshape(shards, ub[0] * ub[1])
    qkv_b = sums[6, : 3 * HDIM].reshape(3, 1, HDIM)
    qkv_b = jnp.where(jnp.arange(2)[None, :, None] == i, qkv_b, 0.0)
    qkv_b = qkv_b.reshape(3, 2, shards, hd).transpose(2, 0, 1, 3).reshape(shards, nq)
    small = jnp.concatenate([norms, in_b, qkv_b], axis=1)
    size = small.shape[1]
    lanes = -(-size // 1024) * 128
    small = jnp.pad(small, ((0, 0), (0, 8 * lanes - size))).reshape(shards, 8, lanes)
    small = jnp.sum(exchange(small, "fsdp", True, 2), axis=0).reshape(8 * lanes)
    x_rows = tokens.astype(F32)
    mean = jnp.mean(x_rows, axis=-1, keepdims=True)
    spread = jnp.mean((x_rows - mean) ** 2, axis=-1, keepdims=True)
    rstd = lax.rsqrt(spread + EPS)
    xhat_here = (x_here - mean) * rstd
    mine = jnp.concatenate(
        [small[: 4 * feats], jnp.sum(u_here, axis=1), jnp.sum(u_here * xhat_here, axis=1)]
    )
    size = mine.shape[0]
    lanes = -(-size // 1024) * 128
    mine = jnp.pad(mine, (0, 8 * lanes - size)).reshape(8, lanes)
    mine = jnp.sum(exchange(mine, "tp", False, 3), axis=0).reshape(8 * lanes)
    norm_grads = mine[: 4 * feats].reshape(4, feats)
    at = 4 * feats
    mean_u = (mine[at : at + rows] / width)[:, None]
    mean_ux = (mine[at + rows : at + 2 * rows] / width)[:, None]
    dx = rstd * (u_here - mean_u - xhat_here * mean_ux)
    tokens_grad = (cut(cotangent).astype(F32) * row_scale[:, None] + dx).astype(BF16)
    bias_grad = small[4 * feats : 5 * feats] * 0.5
    in_bias_grad = small[5 * feats : 5 * feats + ub[0] * ub[1]].reshape(ub)
    at = 5 * feats + ub[0] * ub[1]
    qkv_bias_grad = small[at : at + nq].reshape(3, heads_here, hd)
    return (
        mixed,
        tokens_grad,
        qkv_weight_grad,
        qkv_bias_grad,
        dense_weight_grad,
        bias_grad,
        fc_in_weight_grad,
        in_bias_grad,
        fc_out_weight_grad,
        bias_grad,
        norm_grads[0],
        norm_grads[1],
        norm_grads[2],
        norm_grads[3],
    )


def solution(mesh):
    in_specs = (
        P("fsdp", None),
        P("fsdp", None, "tp"),
        P(None, "tp", "fsdp"),
        P("tp", "fsdp"),
        P("fsdp"),
        P("fsdp", "tp"),
        P("tp", "fsdp"),
        P("tp", "fsdp"),
        P("fsdp"),
        P("fsdp"),
        P("fsdp"),
        P("fsdp"),
        P("fsdp"),
        P("fsdp", None),
        P("fsdp"),
        P(),
    )
    out_specs = (
        P("fsdp", "tp"),
        P("fsdp", "tp"),
        P("fsdp", None, "tp"),
        P(None, "tp", "fsdp"),
        P("tp", "fsdp"),
        P("fsdp"),
        P("fsdp", "tp"),
        P("tp", "fsdp"),
        P("tp", "fsdp"),
        P("fsdp"),
        P("fsdp"),
        P("fsdp"),
        P("fsdp"),
        P("fsdp"),
    )
    return jax.shard_map(
        on_device, mesh=mesh, in_specs=in_specs, out_specs=out_specs, check_vma=False
    )
```

time: 807 us -> 606 us (0.75)
  Pallas kernels: 334 us -> 518 us
  starting transfers between devices: 98.8 us -> 0 us
  waiting for transfers between devices: 95.9 us -> 0 us
  matrix products: 83 us -> 0 us
  other arithmetic: 76.6 us -> 17.5 us
  local copies, waits for them, and re-layouts: 108 us -> 61.1 us
    pallas_call x1, Pallas kernels: 301 us -> 454 us  [block(): pl.pallas_call(functools.partial(block_kernel, dims), out_shape=[sds((D,...]
    ppermute x29 -> x0, starting transfers between devices: 98.8 us -> none  [the longest x18 89.1 us: planes(): return lax.ppermute(value, 'fsdp', pairs)]
    ppermute x29 -> x0, waiting for transfers between devices: 95.9 us -> none  [the longest x18 64.3 us: planes(): return lax.ppermute(value, 'fsdp', pairs)]
    dot_general x10 -> x0, matrix products: 83 us -> none  [mm(): lax.dot_general(left, right, (dims, ((), ())), preferred_element_type=F32)]
    dynamic_slice x7 -> x0, local copies, waits for them, and re-layouts: 30.9 us -> none  [the longest x3 19.1 us: tp_scatter(): keep = lax.dynamic_index_in_dim(view, mine, 2, keepdims=False)]
    pallas_call x3, Pallas kernels: 32.7 us -> 63.1 us  [exchange(): pl.pallas_call(functools.partial(exchange_kernel, axis, spread), out_shap...]
    convert_element_type x12 -> x3, other arithmetic: 34.1 us -> 7.21 us  [the longest x1 3.18 us: on_device(): jnp.where(i == 0, jnp.stack([own, other], 2), jnp.stack([other, own], 2))]
    add x8 -> x1, other arithmetic: 16 us -> 0.66 us  [on_device(): bias = (cut(b_dense) + cut(b_out)).reshape(1, -1)]
  transfers between devices with their start and end apart: 29 -> 0, of which waited for: 10 -> 0; matrix products, arithmetic and copies ran while one was open for 20% -> 0% of each run, Pallas kernels for 3% -> 0%
where the time goes in v4:
time: 606 us; the launch traced here: 598 us
  Pallas kernels  518 us (85%)
  local copies, waits for them, and re-layouts  61.1 us (10%)
  other arithmetic  17.5 us (3%)
    pallas_call x1, Pallas kernels, block(): pl.pallas_call(functools.partial(block_kernel, dims), out_shape=[sds((D,...  454 us
    pallas_call x3, Pallas kernels, exchange(): pl.pallas_call(functools.partial(exchange_kernel, axis, spread), out_shap...  63.1 us
    unnamed x62, local copies, waits for them, and re-layouts  18.6 us

profile of v4, /device:TPU:0, one launch (start us, length us, event | category | flops | bytes accessed | tf_op | source)
XLA Modules:
  0.0 597.8 jit_solution(16624684930392275571)
XLA Ops:
  0.7 0.7 convert_reduce_fusion.2
  1.4 0.7 select_reduce_fusion.1
  2.2 1.9 multiply_cosine_fusion
  4.9 1.2 pad_maximum_fusion.tabs
  6.4 0.9 subtract_subtract_fusion.first
  7.9 0.6 reshape.240.v_ref
  8.5 10.0 %exchange.3 = f32[8,8,256]{2,1,0:T(8,128)} custom-call(f32[8,256]{1,0:T(8,128)} %reshape.240.v_ref), custom_call_target="tpu_custom_call" | custom-call | tf_op jit(solution)/shard_map/exchange/pallas_call | solution.py:92
  18.4 0.9 copy.118
  19.7 0.6 dynamic_slice.20
  20.5 0.6 constant_dynamic-slice_fusion
  21.1 0.7 stack.33.vecs
  21.9 0.7 dynamic-slice_add_fusion
  23.6 1.4 copy.94
  25.4 1.0 constant_dynamic-update-slice_fusion
  26.5 0.8 bitcast_dynamic-update-slice_fusion
  27.3 0.9 fusion.6
  28.2 1.5 copy.99
  29.7 0.9 fusion.5
  30.6 0.9 fusion.4
  31.5 0.8 fusion.3.w2
  32.5 1.7 multiply_convert_fusion.gh
  34.2 454.4 %block.1 = (bf16[2048,1024]{1,0:T(8,128)(2,1)}, bf16[2048,1024]{1,0:T(8,128)(2,1)}, bf16[2048,1024]{1,0:T(8,128)(2,1)}, bf16[512,512]{1,0:T(8,128)(2,1)}, f32[51...) custom-call(bf16[512,2048]{1,0:T(8,128)(2,1)} %tok.1, ...), custom_call_target="tpu_custom_call" | custom-call | tf_op jit(solution)/shard_map/block/pallas_call | solution.py:700
  488.7 3.2 fusion.2
  491.9 2.7 copy-done.1
  494.5 2.4 slice.168
  496.9 6.6 %reshape.263 = f32[2,256,2,2,512]{4,3,1,0,2:T(2,128)} reshape(f32[2,256,2,1024]{3,1,0,2:T(8,128)} %slice.168) | data formatting | bytes 8388608 | tf_op jit(solution)/shard_map/reshape | solution.py:830
  503.5 8.5 %fusion.11 = (f32[2,256,2,1,512]{4,3,1,0,2:T(1,128)}, f32[2,256,2,1,512]{4,3,1,0,2:T(1,128)S(1)}) fusion(f32[2,256,2,2,512]{4,3,1,0,2:T(2,128)} %reshape.263), kind=kLoop, calls=%fused_computation.72 | loop fusion | bytes 8388608 | tf_op jit(solution)/shard_map/slice | solution.py:836
  512.2 1.6 copy.110
  513.9 2.8 reshape.264
  516.7 6.3 %copy.117 = f32[2,256,2,1,512]{1,4,0,2,3:T(8,128)} copy(f32[2,256,2,1,512]{4,3,1,0,2:T(1,128)} %get-tuple-element.82) | data formatting | bytes 4194304 | tf_op jit(solution)/shard_map/transpose | solution.py:836
  522.9 1.7 slice_bitcast_fusion
  524.7 1.3 copy-done.2
  526.6 1.3 copy.108
  527.9 3.2 copy.112
  531.1 1.0 copy.109
  533.0 0.7 copy.135
  533.6 48.1 %exchange.4 = f32[8,8,256]{2,1,0:T(8,128)} custom-call(f32[8,8,256]{2,1,0:T(8,128)} %bitcast.145), custom_call_target="tpu_custom_call" | custom-call | tf_op jit(solution)/shard_map/exchange/pallas_call | solution.py:92
  581.7 0.9 reduce_sum.109
  582.9 0.7 fusion.1
  584.1 0.6 reshape.259.v_ref
  584.7 5.0 exchange.5
  589.8 0.8 reduce_sum.112
  590.6 2.3 add_convert_fusion
  592.9 0.6 fusion.12
  593.5 0.6 slice.165
  594.2 0.7 copy.113
  594.9 0.6 copy.145
  595.5 1.9 copy.146
  (110 shorter events, 6.5 us)
Async XLA Ops:
  4.8 2.5 copy-start.10
  4.8 2.7 copy-start.11
  4.8 2.8 copy-start.8
  4.8 2.9 copy-start.12
  4.8 2.9 copy-start.13
  4.8 2.9 copy-start.14
  4.9 2.9 copy-start.15
  4.9 2.9 copy-start.16
  4.9 2.9 copy-start.17
  4.9 17.6 %copy-start.5 = (bf16[256,2048]{1,0:T(8,128)(2,1)S(1)}, bf16[256,2048]{1,0:T(8,128)(2,1)}, u32[]{:S(2)}) copy-start(bf16[256,2048]{1,0:T(8,128)(2,1)} %param.21) | copy-start | bytes 3145732
  23.6 2.8 copy-start.6
  29.7 2.8 copy-start.4
  491.9 2.7 copy-start.1
  524.7 1.4 copy-start.2
  526.6 4.4 slice-start
  527.9 4.2 copy-start.7
  527.9 54.7 %copy-start = (bf16[512,2048]{1,0:T(8,128)(2,1)S(1)}, bf16[512,2048]{1,0:T(8,128)(2,1)}, u32[]{:S(2)}) copy-start(bf16[512,2048]{1,0:T(8,128)(2,1)} %tok.1) | copy-start | bytes 6291460
  532.0 51.6 %copy-start.3 = (f32[512,512]{1,0:T(8,128)S(1)}, f32[512,512]{1,0:T(8,128)}, u32[]{:S(2)}) copy-start(f32[512,512]{1,0:T(8,128)} %get-tuple-element.20) | copy-start | bytes 3145732
  594.1 3.2 copy-start.9

commit v5 on v4

v5 whole, which is shorter than its diff:
```python
import functools
import math

import jax
import jax.numpy as jnp
from jax import lax
from jax.experimental import pallas as pl
from jax.experimental.pallas import tpu as pltpu
from jax.sharding import PartitionSpec as P

HDIM = 256
ROT = 64
SUBSETS = 22
SEQ_LEN = 2048
EPS = 1e-05
F32 = jnp.float32
BF16 = jnp.bfloat16
MESH = pl.DeviceIdType.MESH
ANY = pl.BlockSpec(memory_space=pl.ANY)
VMEM = pl.BlockSpec(memory_space=pltpu.VMEM)


def mm(left, right, dims):
    return lax.dot_general(left, right, (dims, ((), ())), preferred_element_type=F32)


def plain(left, right):
    return mm(left, right, ((1,), (0,)))


def inner(left, right):
    return mm(left, right, ((0,), (0,)))


def against(left, right):
    return mm(left, right, ((1,), (1,)))


def rotary_tables(positions):
    half = ROT // 2
    steps = jnp.arange(half, dtype=F32)
    freq = 1.0 / 10000.0 ** (steps * 2.0 / ROT)
    angle = positions[:, None] * freq[None, :]
    return jnp.cos(angle), jnp.sin(angle)


def locate(indices, starts):
    above = indices[:, None] >= starts[None, :]
    doc_ids = jnp.sum(above.astype(jnp.int32), axis=1) - 1
    pick = doc_ids[:, None] == jnp.arange(starts.shape[0], dtype=jnp.int32)[None, :]
    first = jnp.sum(jnp.where(pick, starts[None, :], 0), axis=1)
    return (doc_ids, (indices - first).astype(F32))


def half_of(value, which, axis):
    size = value.shape[axis] // 2
    return lax.dynamic_slice_in_dim(value, which * size, size, axis)


def exchange_kernel(axis, spread, v_ref, o_ref, ssem, rsem):
    count = o_ref.shape[0]
    me = lax.axis_index(axis)

    def peer(step):
        return lax.rem(me + step, count)

    barrier = pltpu.get_barrier_semaphore()
    for step in range(1, count):
        pl.semaphore_signal(barrier, 1, device_id={axis: peer(step)}, device_id_type=MESH)
    pl.semaphore_wait(barrier, count - 1)

    def copy(step):
        return pltpu.make_async_remote_copy(
            src_ref=v_ref.at[peer(step)] if spread else v_ref,
            dst_ref=o_ref.at[me],
            send_sem=ssem.at[step],
            recv_sem=rsem.at[step],
            device_id={axis: peer(step)},
            device_id_type=MESH,
        )

    for step in range(1, count):
        copy(step).start()
    o_ref[me] = v_ref[me] if spread else v_ref[...]
    for step in range(1, count):
        copy(step).wait()


def exchange(value, axis, spread, cid):
    count = lax.axis_size(axis)
    block = value.shape[1:] if spread else value.shape
    return pl.pallas_call(
        functools.partial(exchange_kernel, axis, spread),
        out_shape=jax.ShapeDtypeStruct((count,) + block, value.dtype),
        in_specs=[VMEM],
        out_specs=VMEM,
        scratch_shapes=[pltpu.SemaphoreType.DMA((count,)), pltpu.SemaphoreType.DMA((count,))],
        compiler_params=pltpu.CompilerParams(collective_id=cid, has_side_effects=True),
        name="exchange",
    )(value)


GROUPS = 3
ORDER = (
    "pair0", "own0i", "pair1", "own1o", "own0o", "own1i", "mate0o", "mate0i", "rx0", "mate1i", "mate1o",
    "arr01", "arr11", "pair2", "own2i", "rc0", "rx1", "arr02", "rc1", "stats", "arr03", "arr12", "proj",
    "datt", "arr13", "mate2i", "ffn0", "kv1k", "st13i", "kv1v", "st12o", "st12i", "mate2o", "kv2v", "own2o",
    "kv2k", "att0", "att1", "arr21", "st11i", "att2", "att3", "arr22", "st11o", "dn0", "sta3i", "arr23",
    "sta2i", "dn1k", "ffn1", "sta2o", "out", "st23i", "dn1v", "far0", "st22i", "mt0", "dn2v", "st22o", "dn2k",
    "stb3i", "last0", "st21o", "hid", "st21i", "qk", "stb2o", "far1", "stb2i", "fin1", "sta1i", "fin2",
    "sta1o", "stb1o", "mt1", "stb1i", "fina", "finb", "small", "last1",
)


def turn(u, tabs, at, sign):
    lo, hi = u[:, :128], u[:, 128:]
    lane = lax.broadcasted_iota(jnp.int32, lo.shape, 1)
    other = jnp.where(lane < ROT // 2, pltpu.roll(lo, 128 - ROT // 2, 1), pltpu.roll(lo, ROT // 2, 1))
    a = other * tabs[1, at, :]
    lo = lo * tabs[0, at, :] + (a if sign > 0 else -a)
    return jnp.concatenate([lo, hi], axis=1)


def block_kernel(
    dims,
    tok, gh, w2, vecs, bq, bin_, bias, carried, tabs, first,
    wa_o, w0_o, w1_o, mixed_o, dtok_o, norm_o, bias_o, dq_o, dd_o, di_o, do_o,
    xs, gs, wbuf, wk, wv, qs, das, act, dpre, dqkv, att, rcv, dtmp, tpr0, tpr1, tpr2,
    rs_a, rs_f, mean, rstd, tra, trf, sums, bsum, sum_s, sum_r, row_r, nrm_r,
    lsem, tsem, psem, zsem, zrec, ksem, dsem, ssem, rsem, fsem, bsem, xsem, near_ok, far_ok, mate_ok,
):
    R, D, feats, dp, reach = dims
    F, T = 2 * dp, tpr0.shape[0] * 2
    f = lax.axis_index("fsdp")
    t = lax.axis_index("tp")
    d, i = f // 2, lax.rem(f, 2)
    core = lax.rem(t, 2)
    plane, pf = 2 * R, 2 * feats
    qb = min(256, plane)
    nb = plane // qb
    fb = min(256, pf)
    gw = w2.shape[2] // GROUPS
    hu = gw // 2
    pw = D // T
    tn, tf = t + 1 - 2 * core, lax.rem(t + 2, T)
    mate, near, far = (f + 1 - 2 * i, t), (f, tn), (f, tf)
    has = (d + 1 < dp, d >= 1)
    inward = jnp.where(d < dp // 2, 0, 1)
    ways = {"i": inward, "o": 1 - inward}
    outs = (wa_o, w0_o, w1_o)
    scale = 1.0 / math.sqrt(HDIM)

    barrier = pltpu.get_barrier_semaphore()
    for s in range(1, F):
        pl.semaphore_signal(barrier, 1, device_id=(lax.rem(f + s, F), t), device_id_type=MESH)
    for s in range(1, T):
        pl.semaphore_signal(barrier, 1, device_id=(f, lax.rem(t + s, T)), device_id_type=MESH)
    pl.semaphore_wait(barrier, F + T - 2)

    def rc(src, dst, ss, rv, who):
        return pltpu.make_async_remote_copy(
            src_ref=src, dst_ref=dst, send_sem=ss, recv_sem=rv, device_id=who, device_id_type=MESH
        )

    def rows(b):
        return pl.ds(pl.multiple_of(b * qb, qb), qb)

    def toward(way):
        return (f + 2 - 4 * way, t)

    def open_way(way):
        return jnp.where(way == 0, d + 1 < dp, d >= 1)

    def slot(g, s):
        return outs[g].at[pl.ds(s * feats, feats), :]

    def part(half, g):
        return w2.at[half, :, pl.ds(g * gw, gw)]

    def pair_copy(g):
        return rc(part(1 - i, g), slot(g, f), psem.at[0, g], psem.at[1, g], mate)

    def mine_copy(g):
        return pltpu.make_async_copy(part(i, g), slot(g, f), lsem.at[g])

    def z_own(g, way):
        return rc(part(i, g), slot(g, f), zsem.at[g, 0, way, 0], zrec.at[g, f], toward(way))

    def z_mate(g, way):
        s = f + 1 - 2 * i
        return rc(slot(g, s), slot(g, s), zsem.at[g, 0, way, 1], zrec.at[g, s], toward(way))

    def z_fwd(g, k, way, j):
        s = (d - k) * 2 + j if way == 0 else (d + k) * 2 + j
        return rc(slot(g, s), slot(g, s), zsem.at[g, k, way, j], zrec.at[g, s], toward(way))

    def send_own(g, io):
        @pl.when(open_way(ways[io]))
        def _():
            z_own(g, ways[io]).start()

    def send_mate(g, io, wait):
        if wait:
            pair_copy(g).wait_recv()

        @pl.when(open_way(ways[io]))
        def _():
            z_mate(g, ways[io]).start()

    def from_dist(k, way):
        return d >= k if way == 0 else d + k < dp

    def arrive(g, k):
        for way in range(2):
            @pl.when(from_dist(k, way))
            def _():
                for j in range(2):
                    z_fwd(g, k, way, j).wait_recv()

                    @pl.when(has[way])
                    def _():
                        z_fwd(g, k, way, j).start()

    def gather_sent(g):
        pair_copy(g).wait_send()
        for way in range(2):
            @pl.when(has[way])
            def _():
                z_own(g, way).wait_send()
                z_mate(g, way).wait_send()
            for k in range(1, dp - 1):
                @pl.when(from_dist(k, way) & has[way])
                def _():
                    for j in range(2):
                        z_fwd(g, k, way, j).wait_send()

    def load(*pairs):
        copies = [pltpu.make_async_copy(src, dst, bsem.at[n]) for n, (src, dst) in enumerate(pairs)]
        for c in copies:
            c.start()
        for c in copies:
            c.wait()

    hr = R // 2
    given = ((tok, xs), (gh, gs))

    def rows_x(a):
        ref, out = given[a]
        return rc(
            ref.at[pl.ds(core * hr, hr), :], out.at[pl.ds(i * R + core * hr, hr), :],
            tsem.at[a, 0], tsem.at[a, 1], mate,
        )

    def rows_c(a):
        at = given[a][1].at[pl.ds((1 - i) * R + core * hr, hr), :]
        return rc(at, at, tsem.at[a, 2], tsem.at[a, 3], near)

    def rows_own(a):
        ref, out = given[a]
        return pltpu.make_async_copy(ref, out.at[pl.ds(i * R, R), :], lsem.at[GROUPS + a])

    def rows_on(a):
        rows_x(a).wait_recv()
        rows_c(a).start()

    def rows_done(a):
        rows_c(a).wait_recv()
        rows_own(a).wait()

    def hat(at):
        return (xs[at, :].astype(F32) - mean[at, :]) * rstd[at, :]

    def stats():
        def block(b, _):
            x = xs[rows(b), :].astype(F32)
            m = jnp.mean(x, axis=-1, keepdims=True)
            c = x - m
            mean[rows(b), :] = m
            rstd[rows(b), :] = lax.rsqrt(jnp.mean(c * c, axis=-1, keepdims=True) + EPS)
            return 0

        rows_done(0)
        lax.fori_loop(0, nb, block, 0)

    def proj():
        def block(b, _):
            at = rows(b)
            h1 = (hat(at) * vecs[0:1, :] + vecs[1:2, :]).astype(BF16)
            y = plain(h1, wbuf[:, : 3 * HDIM]) + bq[...]
            qs[at, :] = (turn(y[:, :HDIM], tabs, at, 1).astype(BF16).astype(F32) * scale).astype(BF16)
            wk[reach, at, :] = turn(y[:, HDIM : 2 * HDIM], tabs, at, 1).astype(BF16)
            wv[reach, at, :] = y[:, 2 * HDIM :].astype(BF16)
            return 0

        mine_copy(0).wait()
        load((wa_o, wbuf))
        lax.fori_loop(0, nb, block, 0)

        @pl.when(has[0])
        def _():
            kv_copy(0, 0).start()
            kv_copy(1, 0).start()

    def datt():
        def block(b, _):
            at = rows(b)
            das[at, :] = plain(gs[at, :], wbuf[:, 3 * HDIM :]).astype(BF16)
            return 0

        rows_done(1)
        lax.fori_loop(0, nb, block, 0)

    def ffn(h):
        mine = slice(h * hu, (h + 1) * hu)

        def block(b, _):
            at = rows(b)
            h2 = (hat(at) * vecs[2:3, :] + vecs[3:4, :]).astype(BF16)
            pre = plain(h2, wbuf[:, :hu]) + bin_[:, mine]
            cdf = 0.5 * (1.0 + lax.erf(pre * (1.0 / math.sqrt(2.0))))
            act[at, mine] = (pre * cdf).astype(BF16)
            slope = cdf + pre * jnp.exp(-0.5 * pre * pre) * (1.0 / math.sqrt(2.0 * math.pi))
            dp_b = (plain(gs[at, :], wbuf[:, hu:]) * slope).astype(BF16)
            dpre[at, mine] = dp_b
            bsum[0:1, mine] += jnp.sum(dp_b.astype(F32), axis=0, keepdims=True)
            return 0

        mine_copy(1 + h).wait()
        load((outs[1 + h], wbuf))
        lax.fori_loop(0, nb, block, 0)

    def kv_copy(h, k):
        w = (wk, wv)[h]
        return rc(w.at[reach - k], w.at[reach - k - 1], ksem.at[h, 0, k], ksem.at[h, 1, k + 1], toward(0))

    def kv_recv(h, k):
        w = (wk, wv)[h]
        return rc(w.at[reach - k], w.at[reach - k], ksem.at[h, 0, k - 1], ksem.at[h, 1, k], toward(0))

    def kv_step(h, k):
        @pl.when(d >= k)
        def _():
            kv_recv(h, k).wait_recv()
            if k < reach:
                @pl.when(has[0])
                def _():
                    kv_copy(h, k).start()

        @pl.when(d < k)
        def _():
            (wk, wv)[h][reach - k] = jnp.zeros((plane, HDIM), BF16)

    span = SEQ_LEN + qb
    base = reach * plane - SEQ_LEN
    parts = 4

    def attention(acc, n):
        def block(b, _):
            at = rows(b)
            keys_at = pl.ds(pl.multiple_of(base + b * qb, qb), span)
            keys = wk.reshape((reach + 1) * plane, HDIM)[keys_at, :]
            vals = wv.reshape((reach + 1) * plane, HDIM)[keys_at, :]
            q = qs[at, :]
            s = against(q, keys)
            c = base + b * qb + lax.broadcasted_iota(jnp.int32, (qb, span), 1)
            r = reach * plane + b * qb + lax.broadcasted_iota(jnp.int32, (qb, span), 0)
            s = jnp.where((c >= first[at, :]) & (c <= r), s, -1e30)
            e = jnp.exp(s - jnp.max(s, axis=1, keepdims=True))
            p = e * (1.0 / jnp.sum(e, axis=1, keepdims=True))
            pb = p.astype(BF16)
            att[at, :] = plain(pb, vals).astype(BF16)
            da = das[at, :]
            dpr = against(da, vals)
            delta = jnp.sum(p * dpr, axis=1, keepdims=True)
            ds = (p * (dpr - delta)).astype(BF16)
            dq = plain(ds, keys) * scale
            dqkv[at, :HDIM] = turn(dq, tabs, at, -1).astype(BF16)
            acc[keys_at, :HDIM] += inner(ds, q)
            acc[keys_at, HDIM:] += inner(pb, da)
            return 0

        if n == 0:
            acc[...] = jnp.zeros_like(acc)
        lax.fori_loop(n * nb // parts, (n + 1) * nb // parts, block, 0)

    dwin = (wk, wv)

    def down_copy(h, r):
        src = dwin[h].at[0] if r == 0 else dtmp.at[h]
        return rc(src, rcv.at[h, r], dsem.at[h, 0, r], dsem.at[h, 1, r], toward(1))

    def down_first(acc):
        for k in range(reach):
            @pl.when((d >= k) & has[0])
            def _():
                kv_copy(0, k).wait_send()
                kv_copy(1, k).wait_send()

        for r in range(reach + 1):
            for h in range(2):
                dwin[h][r] = acc[pl.ds(r * plane, plane), h * HDIM : (h + 1) * HDIM].astype(BF16)
            if r == 0:
                @pl.when(d >= reach)
                def _():
                    down_copy(0, 0).start()
                    down_copy(1, 0).start()

    def down_step(h, r):
        def keep(b, _):
            dtmp[h, rows(b), :] = dwin[h][r, rows(b), :]
            return 0

        def add(b, _):
            at = rows(b)
            v = dwin[h][r, at, :].astype(F32) + rcv[h, r - 1, at, :].astype(F32)
            dtmp[h, at, :] = v.astype(BF16)
            return 0

        def turned(b, _):
            at = rows(b)
            v = dtmp[h, at, :]
            dqkv[at, (h + 1) * HDIM : (h + 2) * HDIM] = (
                turn(v.astype(F32), tabs, at, -1).astype(BF16) if h == 0 else v
            )
            return 0

        came = has[0] & (d >= reach - r)
        if r > 1:
            @pl.when(d >= reach - r + 1)
            def _():
                down_copy(h, r - 1).wait_send()

        @pl.when(came)
        def _():
            down_copy(h, r - 1).wait_recv()
            lax.fori_loop(0, nb, add, 0)

        @pl.when(jnp.logical_not(came))
        def _():
            lax.fori_loop(0, nb, keep, 0)

        if r < reach:
            @pl.when(d >= reach - r)
            def _():
                down_copy(h, r).start()
        else:
            lax.fori_loop(0, nb, turned, 0)

    def rs(g):
        return rs_a.at[g] if g < 2 else rs_f.at[g - 2]

    def grad_part(g, p, c):
        cols = pl.ds(pl.multiple_of(p * pf + c * fb, fb), fb)
        z = (xs[:, cols].astype(F32) - mean[...]) * rstd[...]
        n = 0 if g < 2 else 2
        h = (z * vecs[n : n + 1, cols] + vecs[n + 1 : n + 2, cols]).astype(BF16)
        if g == 0:
            return inner(h, dqkv[:, :HDIM]), inner(gs[:, cols], att[...])
        if g == 1:
            return (inner(h, dqkv[:, HDIM:]),)
        mine = slice((g - 2) * hu, (g - 1) * hu)
        return inner(h, dpre[:, mine]), inner(gs[:, cols], act[:, mine])

    def add_part(g, p, second=None):
        def block(c, _):
            at = pl.ds(pl.multiple_of(c * fb, fb), fb)
            left = 0
            for v in grad_part(g, p, c):
                cols = slice(left, left + v.shape[1])
                left += v.shape[1]
                v = rs(g)[p, at, cols].astype(F32) + v
                if second is not None:
                    v = v + rs(g)[second, at, cols].astype(F32)
                rs(g)[p, at, cols] = v.astype(BF16)
            return 0

        lax.fori_loop(0, pf // fb, block, 0)

    def rs_copy(g, k, way):
        p = d + k * (1 - 2 * way)
        to = jnp.where((way == 1) & (k == 1), dp, p)
        return rc(rs(g).at[p], rs(g).at[to], ssem.at[g, k, way], rsem.at[g, to], toward(way))

    def rs_wait(g, p):
        return rc(rs(g).at[p], rs(g).at[p], ssem.at[g, 0, 0], rsem.at[g, p], mate)

    def clear(g, p):
        rs(g)[p] = jnp.zeros(rs(g).shape[1:], BF16)

    def stage(g, k, io):
        way = ways[io]
        p = d + k * (1 - 2 * way)
        came = open_way(1 - way)

        @pl.when((p >= 0) & (p < dp))
        def _():
            @pl.when(came)
            def _():
                rs_wait(g, p).wait_recv()

            @pl.when(jnp.logical_not(came))
            def _():
                clear(g, p)

            add_part(g, p)
            rs_copy(g, k, way).start()

    def final_copies(g):
        lo = pl.multiple_of(i * HDIM, HDIM)
        pieces = []
        for j in range(2):
            at = pl.ds((i if j == 0 else 1 - i) * feats, feats)
            src = rs(g).at[d, at]
            if g == 0:
                dst = (dq_o.at[0, :, pl.ds(lo, HDIM)], dd_o.at[pl.ds(lo, HDIM), :])
                src = (src.at[:, pl.ds(0, HDIM)], tra.at[j])
            elif g == 1:
                dst = tuple(dq_o.at[n, :, pl.ds(lo, HDIM)] for n in (1, 2))
                src = tuple(src.at[:, pl.ds(n * HDIM, HDIM)] for n in (0, 1))
            else:
                u = pl.multiple_of(i * gw + (g - 2) * hu, hu)
                dst = (di_o.at[:, pl.ds(u, hu)], do_o.at[pl.ds(u, hu), :])
                src = (src.at[:, pl.ds(0, hu)], trf.at[g - 2, j])
            for n in range(2):
                if j == 0:
                    pieces.append(pltpu.make_async_copy(src[n], dst[n], fsem.at[g, n, 0]))
                else:
                    pieces.append(rc(src[n], dst[n], fsem.at[g, n, 1], fsem.at[g, n, 2], mate))
        return pieces

    def final(g):
        for p, came in ((d, has[1]), (dp, has[0])):
            @pl.when(came)
            def _():
                rs_wait(g, p).wait_recv()

            @pl.when(jnp.logical_not(came))
            def _():
                clear(g, p)

        add_part(g, d, dp)
        if g != 1:
            cut = HDIM if g == 0 else hu
            for j in range(2):
                at = pl.ds(pl.multiple_of((i if j == 0 else 1 - i) * feats, feats), feats)
                turned = rs(g)[d, at, cut:].astype(F32).T.astype(BF16)
                if g == 0:
                    tra[j] = turned
                else:
                    trf[g - 2, j] = turned
        for c in final_copies(g):
            c.start()

    def out_step(up, wd):
        def block(b, _):
            at = rows(b)
            sums[4:5, :] += jnp.sum(gs[at, :].astype(F32), axis=0, keepdims=True)
            for c in range(T):
                cols = slice(c * pw, (c + 1) * pw)
                y = against(att[at, :], wd[cols, :]) + against(act[at, :], wbuf[cols, :])
                up[c, at, :] = y.astype(BF16)
            return 0

        load(
            (w0_o.at[:, pl.ds(hu, hu)], wbuf.at[:, pl.ds(0, hu)]),
            (w1_o.at[:, pl.ds(hu, hu)], wbuf.at[:, pl.ds(hu, hu)]),
            (wa_o.at[:, pl.ds(3 * HDIM, HDIM)], wd),
            (carried, env["kept"]),
        )
        lax.fori_loop(0, nb, block, 0)
        tp_near(up, False)

    def hidden_step(up):
        def block(b, _):
            at = rows(b)
            e2 = against(dpre[at, :], wbuf[...])
            z = hat(at)
            sums[2:3, :] += jnp.sum(e2 * z, axis=0, keepdims=True)
            sums[3:4, :] += jnp.sum(e2, axis=0, keepdims=True)
            u = (e2 * vecs[2:3, :]).astype(BF16)
            for c in range(T):
                up[c, at, :] = u[:, c * pw : (c + 1) * pw]
            return 0

        load(
            (w0_o.at[:, pl.ds(0, hu)], wbuf.at[:, pl.ds(0, hu)]),
            (w1_o.at[:, pl.ds(0, hu)], wbuf.at[:, pl.ds(hu, hu)]),
        )
        lax.fori_loop(0, nb, block, 0)

    def qkv_step(up):
        def block(b, _):
            at = rows(b)
            e1 = against(dqkv[at, :], wbuf[:, : 3 * HDIM])
            z = hat(at)
            sums[0:1, :] += jnp.sum(e1 * z, axis=0, keepdims=True)
            sums[1:2, :] += jnp.sum(e1, axis=0, keepdims=True)
            bsum[1:2, : 3 * HDIM] += jnp.sum(dqkv[at, :].astype(F32), axis=0, keepdims=True)
            u = e1 * vecs[0:1, :]
            for c in range(T):
                up[c, at, :] = (up[c, at, :].astype(F32) + u[:, c * pw : (c + 1) * pw]).astype(BF16)
            return 0

        load((wa_o, wbuf))
        lax.fori_loop(0, nb, block, 0)
        tp_near(up, True)
        for s in range(F):
            sum_s[s] = sums[:, s * feats : (s + 1) * feats]
        for s in range(1, F):
            sum_copy(s).start()
            bias_copy(s).start()
        sum_r[f] = sum_s[f]
        bias_o[f] = bsum[...]

    def near_copy(up, j):
        return rc(up.at[tn if j == 0 else lax.rem(tn + 2, T)], tpr0.at[j], tsem.at[2, j], tsem.at[3, j], near)

    def far_copy(up):
        return rc(up.at[tf], tpr1, tsem.at[2, 2], tsem.at[3, 2], far)

    def mate_copy(up):
        return rc(up.at[t, pl.ds((1 - i) * R, R), :], tpr2, tsem.at[2, 3], tsem.at[3, 3], mate)

    def tp_near(up, second):
        if second:
            pl.semaphore_wait(near_ok, 1)
        near_copy(up, 0).start()
        near_copy(up, 1).start()

    def tp_far(up, second):
        def block(b, _):
            at = rows(b)
            up[tf, at, :] = (up[tf, at, :].astype(F32) + tpr0[1, at, :].astype(F32)).astype(BF16)
            return 0

        near_copy(up, 1).wait_recv()
        lax.fori_loop(0, nb, block, 0)
        if second:
            pl.semaphore_wait(far_ok, 1)
        far_copy(up).start()

    def tp_mate(up, second):
        def block(b, _):
            at = rows(b)
            v = up[t, at, :].astype(F32) + tpr0[0, at, :].astype(F32) + tpr1[at, :].astype(F32)
            up[t, at, :] = v.astype(BF16)
            return 0

        near_copy(up, 0).wait_recv()
        far_copy(up).wait_recv()
        lax.fori_loop(0, nb, block, 0)
        if second:
            pl.semaphore_wait(mate_ok, 1)
        else:
            pl.semaphore_signal(near_ok, 1, device_id=near, device_id_type=MESH)
            pl.semaphore_signal(far_ok, 1, device_id=far, device_id_type=MESH)
        mate_copy(up).start()

    def tp_last(up, second):
        mate_copy(up).wait_recv()
        here = pl.ds(pl.multiple_of(i * R, R), R)
        x = xs[here, pl.ds(pl.multiple_of(t * pw, pw), pw)].astype(F32)
        if second:
            u = up[t, here, :].astype(F32) + tpr2[...].astype(F32)
            z = (x - mean[here, :]) * rstd[here, :]
            lane = lax.broadcasted_iota(jnp.int32, (R, 128), 1)
            one, two = jnp.sum(u, axis=1, keepdims=True), jnp.sum(u * z, axis=1, keepdims=True)
            row_r[t] = jnp.where(lane == 0, one, jnp.where(lane == 1, two, 0.0)).T[:8]
            for s in range(1, T):
                row_copy(s).start()
            for s in range(1, T):
                row_copy(s).wait()
            both = row_r[0]
            for s in range(1, T):
                both = both + row_r[s]
            both = jnp.concatenate([both, jnp.zeros((120, R), F32)], axis=0).T * (1.0 / D)
            dx = rstd[here, :] * (u - both[:, 0:1] - z * both[:, 1:2])
            dtok_o[...] = (env["kept"][...] + dx).astype(BF16)
        else:
            v = up[t, here, :].astype(F32) + tpr2[...].astype(F32)
            mixed_o[...] = (x + v + bias[...]).astype(BF16)
            pl.semaphore_signal(mate_ok, 1, device_id=mate, device_id_type=MESH)
        near_copy(up, 0).wait_send()
        near_copy(up, 1).wait_send()
        far_copy(up).wait_send()
        mate_copy(up).wait_send()

    def row_copy(s):
        return rc(row_r.at[t], row_r.at[t], xsem.at[0, 0, s], xsem.at[0, 1, s], (f, lax.rem(t + s, T)))

    def norm_copy(s):
        return rc(nrm_r.at[t], nrm_r.at[t], xsem.at[1, 0, s], xsem.at[1, 1, s], (f, lax.rem(t + s, T)))

    def sum_copy(s):
        to = lax.rem(f + s, F)
        return rc(sum_s.at[to], sum_r.at[f], xsem.at[2, 0, s], xsem.at[2, 1, s], (to, t))

    def bias_copy(s):
        return rc(bsum, bias_o.at[f], xsem.at[3, 0, s], xsem.at[3, 1, s], (lax.rem(f + s, F), t))

    def small_sums():
        for s in range(1, F):
            sum_copy(s).wait()
            bias_copy(s).wait()
        v = sum_r[0]
        for s in range(1, F):
            v = v + sum_r[s]
        nrm_r[t] = v
        for s in range(1, T):
            norm_copy(s).start()
        for s in range(1, T):
            norm_copy(s).wait()
        both = nrm_r[0]
        for s in range(1, T):
            both = both + nrm_r[s]
        row = lax.broadcasted_iota(jnp.int32, both.shape, 0)
        norm_o[...] = jnp.where(row == 4, v * 0.5, both)

    env = {}
    far_out = tuple(range(dp - 1, 2, -1))
    groups = {"a": 0, "b": 1, "1": 2, "2": 3}
    paired = set()

    def step(name):
        kind, rest = name.rstrip("0123456789abiokv"), ""
        rest = name[len(kind):]
        if kind == "pair":
            pair_copy(int(rest)).start()
            mine_copy(int(rest)).start()
        elif kind == "own":
            send_own(int(rest[0]), rest[1])
        elif kind == "mate":
            send_mate(int(rest[0]), rest[1], rest[0] not in paired)
            paired.add(rest[0])
        elif kind == "arr":
            g, k = int(rest[0]), int(rest[1])
            for n in range(k, dp if k == 3 else k + 1):
                arrive(g, n)
        elif kind == "rx":
            rows_x(int(rest)).start()
            rows_own(int(rest)).start()
        elif kind == "rc":
            rows_on(int(rest))
        elif kind == "stats":
            stats()
        elif kind == "proj":
            proj()
        elif kind == "datt":
            datt()
        elif kind == "ffn":
            ffn(int(rest))
        elif kind == "att":
            attention(env["acc"], int(rest))
        elif kind == "dn" and rest == "0":
            down_first(env["acc"])
        elif kind == "dn":
            for r in range(1, reach) if rest[0] == "1" else (reach,):
                down_step("kv".index(rest[1]), r)
        elif kind == "st":
            g, k, io = groups[rest[0]], int(rest[1]), rest[2]
            if k == 3:
                for n in far_out:
                    stage(g, n, io)
            elif k == 2 and io == "o":
                for n in far_out + (2,):
                    stage(g, n, io)
            else:
                stage(g, k, io)
        elif kind == "fin":
            final(groups[rest])
        elif kind == "out":
            out_step(env["up"], env["wd"])
        elif kind == "far":
            tp_far(env["up"], rest == "1")
        elif kind == "mt":
            tp_mate(env["up"], rest == "1")
        elif kind == "last":
            tp_last(env["up"], rest == "1")
        elif kind == "hid":
            hidden_step(env["up"])
        elif kind == "q":
            qkv_step(env["up"])
        elif kind == "small":
            small_sums()
        else:
            hop = int(rest[-2])
            for k in range(1, reach) if hop == 1 else (reach,):
                kv_step("kv".index(rest[-1]), k)

    def attend_scope(acc):
        env["acc"] = acc
        for name in ORDER[ORDER.index("att0") : ORDER.index("dn0") + 1]:
            step(name)

    def finish_scope(up, wd, kept):
        env["up"], env["wd"], env["kept"] = up, wd, kept
        for name in ORDER[ORDER.index("out") :]:
            step(name)

    sums[...] = jnp.zeros_like(sums)
    bsum[...] = jnp.zeros_like(bsum)
    for name in ORDER[: ORDER.index("att0")]:
        step(name)
    pl.run_scoped(attend_scope, pltpu.VMEM(((reach + 1) * plane, 2 * HDIM), F32))
    for name in ORDER[ORDER.index("dn0") + 1 : ORDER.index("out")]:
        step(name)
    pl.run_scoped(
        finish_scope, pltpu.VMEM((T, plane, pw), BF16), pltpu.VMEM((D, HDIM), BF16), pltpu.VMEM((R, pw), F32)
    )

    for h in range(2):
        @pl.when(d >= reach)
        def _():
            down_copy(h, 0).wait_send()
    for a in range(2):
        rows_x(a).wait_send()
        rows_c(a).wait_send()
    for g in range(GROUPS):
        gather_sent(g)
    for g in range(4):
        for k in range(1, dp):
            for way in range(2):
                @pl.when(from_dist(k, 1 - way))
                def _():
                    rs_copy(g, k, way).wait_send()
        for c in final_copies(g):
            c.wait()


def block(tok, gh, w2, vecs, bq, b_in, bias, carried, tabs, first, dims):
    R, D, feats, dp, reach = dims
    plane, pf, F, T = 2 * R, 2 * feats, 2 * dp, lax.axis_size("tp")
    gw = w2.shape[2] // GROUPS
    pw = D // T
    sds = jax.ShapeDtypeStruct
    vm = pltpu.VMEM
    dma = pltpu.SemaphoreType.DMA
    reg = pltpu.SemaphoreType.REGULAR
    win = vm((reach + 1, plane, HDIM), BF16)
    return pl.pallas_call(
        functools.partial(block_kernel, dims),
        out_shape=[sds((D, gw), BF16)] * GROUPS
        + [sds((R, pw), BF16), sds((R, pw), BF16), sds((8, feats), F32), sds((F, 8, gw), F32)]
        + [sds((3, feats, 2 * HDIM), BF16), sds((2 * HDIM, feats), BF16)]
        + [sds((feats, 2 * gw), BF16), sds((2 * gw, feats), BF16)],
        in_specs=[ANY] * 3 + [VMEM] * 4 + [ANY] + [VMEM] * 2,
        out_specs=[ANY] * GROUPS + [VMEM] * 4 + [ANY] * 4,
        scratch_shapes=[
            vm((plane, D), BF16), vm((plane, D), BF16), vm((D, gw), BF16),
            win, win, vm((plane, HDIM), BF16), vm((plane, HDIM), BF16),
            vm((plane, gw), BF16), vm((plane, gw), BF16), vm((plane, 3 * HDIM), BF16), vm((plane, HDIM), BF16),
            vm((2, reach, plane, HDIM), BF16), vm((2, plane, HDIM), BF16),
            vm((T // 2, plane, pw), BF16), vm((plane, pw), BF16), vm((R, pw), BF16),
            vm((2, dp + 1, pf, 2 * HDIM), BF16), vm((2, dp + 1, pf, gw), BF16),
            vm((plane, 1), F32), vm((plane, 1), F32),
            vm((2, HDIM, feats), BF16), vm((2, 2, gw // 2, feats), BF16),
            vm((8, D), F32), vm((8, gw), F32), vm((F, 8, feats), F32), vm((F, 8, feats), F32),
            vm((T, 8, R), F32), vm((T, 8, feats), F32),
            dma((GROUPS + 2,)), dma((4, 4)), dma((2, GROUPS)), dma((GROUPS, dp, 2, 2)), dma((GROUPS, F)),
            dma((2, 2, reach + 1)), dma((2, 2, reach)), dma((4, dp, 2)), dma((4, dp + 1)), dma((4, 2, 3)),
            dma((4,)), dma((4, 2, F)), reg, reg, reg,
        ],
        compiler_params=pltpu.CompilerParams(
            collective_id=4, has_side_effects=True, vmem_limit_bytes=63 << 20
        ),
        name="block",
    )(tok, gh, w2, vecs, bq, b_in, bias, carried, tabs, first)


def on_device(
    tokens,
    qkv_weight,
    qkv_bias,
    dense_weight,
    dense_bias,
    fc_in_weight,
    fc_in_bias,
    fc_out_weight,
    fc_out_bias,
    norm1_gain,
    norm1_shift,
    norm2_gain,
    norm2_shift,
    cotangent,
    subset_ids,
    seq_starts,
):
    rows, width = tokens.shape
    shards = lax.axis_size("fsdp")
    tps = lax.axis_size("tp")
    dp = shards // 2
    f = lax.axis_index("fsdp")
    t = lax.axis_index("tp")
    i = lax.rem(f, 2)
    d = f // 2
    total = rows * shards
    scale = 1.0 / math.sqrt(HDIM)
    feats = qkv_weight.shape[0]
    units = fc_in_weight.shape[1]
    head_cols = qkv_weight.shape[2]
    heads_here = head_cols // HDIM
    hd = qkv_bias.shape[2]
    ub = fc_in_bias.shape

    match = subset_ids[:, None] == jnp.arange(SUBSETS, dtype=jnp.int32)[None, :]
    counts = jnp.sum(match.astype(F32), axis=0)
    vecs = [norm1_gain, norm1_shift, norm2_gain, norm2_shift, dense_bias, fc_out_bias]
    pack = jnp.concatenate(
        [v.astype(F32) for v in vecs]
        + [qkv_bias.astype(F32).reshape(-1), fc_in_bias.astype(F32).reshape(-1), counts]
    )
    size = pack.shape[0]
    lanes = -(-size // 1024) * 128
    got = exchange(jnp.pad(pack, (0, 8 * lanes - size)).reshape(8, lanes), "fsdp", False, 1)
    got = got.reshape(shards, 8 * lanes)
    gain1, shift1, gain2, shift2, b_dense, b_out = [
        got[:, k * feats : (k + 1) * feats].reshape(width) for k in range(6)
    ]
    at = 6 * feats
    nq = 3 * heads_here * hd
    b_qkv = got[:, at : at + nq].reshape(shards, 3, heads_here, hd)
    b_qkv = b_qkv.transpose(1, 2, 0, 3).reshape(3, heads_here, HDIM)
    b_qkv = lax.dynamic_index_in_dim(b_qkv, i, 1, keepdims=False).reshape(3 * HDIM)
    at += nq
    b_in = got[:, at : at + units // shards].reshape(shards, ub[0], ub[1])
    b_in = half_of(b_in.transpose(1, 0, 2).reshape(units), i, 0)
    at += units // shards
    counts = jnp.sum(got[:, at : at + SUBSETS], axis=0)
    table = total / (SUBSETS * counts)
    row_scale = jnp.sum(jnp.where(match, table[None, :], 0.0), axis=1)
    carried = cotangent.astype(F32) * row_scale[:, None]
    grad_here = carried.astype(BF16)

    wi = fc_in_weight.reshape(feats, 2, 2, units // 4).transpose(1, 0, 2, 3)
    wo = fc_out_weight.reshape(2, 2, units // 4, feats).transpose(0, 3, 1, 2)
    w2 = jnp.concatenate(
        [
            qkv_weight.reshape(feats, 3, heads_here, HDIM).transpose(2, 0, 1, 3).reshape(2, feats, 3 * HDIM),
            dense_weight.reshape(heads_here, HDIM, feats).transpose(0, 2, 1),
            wi[:, :, 0], wo[:, :, 0], wi[:, :, 1], wo[:, :, 1],
        ],
        axis=2,
    )
    plane = 2 * rows
    start_row = d * plane
    reach = min(dp - 1, -(-(SEQ_LEN - 1) // plane))
    here = start_row + jnp.arange(plane, dtype=jnp.int32)
    docs_here, pos_here = locate(here, seq_starts)
    first = (here - pos_here.astype(jnp.int32)) - (start_row - reach * plane)
    cosine, sine = rotary_tables(pos_here)
    ones = jnp.ones((plane, 128 - ROT), F32)
    none = jnp.zeros((plane, 128 - ROT), F32)
    tabs = jnp.stack(
        [
            jnp.concatenate([cosine, cosine, ones], 1),
            jnp.concatenate([-sine, sine, none], 1),
        ]
    )
    vecs = jnp.stack([gain1, shift1, gain2, shift2] + [jnp.zeros_like(gain1)] * 4)
    dims = (rows, width, feats, dp, reach)
    part_w = width // tps
    offset = t * part_w
    cut = lambda vec: lax.dynamic_slice_in_dim(vec, offset, part_w, vec.ndim - 1)
    bias = (cut(b_dense) + cut(b_out)).reshape(1, -1)
    carried_here = cut(cotangent).astype(F32) * row_scale[:, None]
    _, _, _, mixed, tokens_grad, norm_grads, bias_sums, g_qkv, g_dense, g_in, g_out = block(
        tokens, grad_here, w2, vecs, b_qkv.reshape(1, -1), b_in.reshape(1, -1), bias, carried_here, tabs,
        first[:, None], dims,
    )
    qkv_weight_grad = g_qkv.transpose(1, 0, 2).astype(F32)
    dense_weight_grad = g_dense.astype(F32)
    fc_in_weight_grad = g_in.astype(F32)
    fc_out_weight_grad = g_out.astype(F32)
    bias_grad = norm_grads[4]

    bias_sums = jnp.sum(bias_sums.reshape(dp, 2, 8, units // 2), axis=0)
    in_bias_grad = bias_sums[:, 0].reshape(ub[0], shards * ub[1])
    in_bias_grad = lax.dynamic_slice_in_dim(in_bias_grad, f * ub[1], ub[1], 1)
    qkv_bias_grad = bias_sums[:, 1, : 3 * HDIM].reshape(2, 3, HDIM).transpose(1, 0, 2)
    qkv_bias_grad = lax.dynamic_slice_in_dim(qkv_bias_grad, f * hd, hd, 2)
    return (
        mixed,
        tokens_grad,
        qkv_weight_grad,
        qkv_bias_grad,
        dense_weight_grad,
        bias_grad,
        fc_in_weight_grad,
        in_bias_grad,
        fc_out_weight_grad,
        bias_grad,
        norm_grads[0],
        norm_grads[1],
        norm_grads[2],
        norm_grads[3],
    )


def solution(mesh):
    in_specs = (
        P("fsdp", None),
        P("fsdp", None, "tp"),
        P(None, "tp", "fsdp"),
        P("tp", "fsdp"),
        P("fsdp"),
        P("fsdp", "tp"),
        P("tp", "fsdp"),
        P("tp", "fsdp"),
        P("fsdp"),
        P("fsdp"),
        P("fsdp"),
        P("fsdp"),
        P("fsdp"),
        P("fsdp", None),
        P("fsdp"),
        P(),
    )
    out_specs = (
        P("fsdp", "tp"),
        P("fsdp", "tp"),
        P("fsdp", None, "tp"),
        P(None, "tp", "fsdp"),
        P("tp", "fsdp"),
        P("fsdp"),
        P("fsdp", "tp"),
        P("tp", "fsdp"),
        P("tp", "fsdp"),
        P("fsdp"),
        P("fsdp"),
        P("fsdp"),
        P("fsdp"),
        P("fsdp"),
    )
    return jax.shard_map(
        on_device, mesh=mesh, in_specs=in_specs, out_specs=out_specs, check_vma=False
    )
```

time: 606 us -> 485 us (0.80)
  the two profiles are of different devices: /device:TPU:0 before, /device:TPU:19 now
where the time goes in v5:
time: 485 us; the launch traced here: 476 us
  Pallas kernels  440 us (91%)
  local copies, waits for them, and re-layouts  17.6 us (4%)
  other arithmetic  17.2 us (4%)
    pallas_call x1, Pallas kernels, block(): pl.pallas_call(functools.partial(block_kernel, dims), out_shape=[sds((D,...  432 us

profile of v5, /device:TPU:19, one launch (start us, length us, event | category | flops | bytes accessed | tf_op | source)
XLA Modules:
  0.0 475.7 jit_solution(6057764077368885880)
XLA Ops:
  0.7 0.7 convert_reduce_fusion.1
  1.4 0.7 select_reduce_fusion.1
  2.2 1.9 multiply_cosine_fusion
  4.3 0.3 maximum_bitcast_fusion
  4.7 1.0 pad_maximum_fusion.tabs
  5.7 0.2 copy.94
  6.0 0.9 subtract_subtract_fusion.first
  6.9 0.1 copy.82
  7.0 0.1 reshape.160
  7.1 0.1 reshape.158
  7.2 0.1 convert_reduce_fusion
  7.4 0.6 reshape.141.v_ref
  8.0 7.0 %exchange.1 = f32[8,8,256]{2,1,0:T(8,128)} custom-call(f32[8,256]{1,0:T(8,128)} %reshape.141.v_ref), custom_call_target="tpu_custom_call" | custom-call | tf_op jit(solution)/shard_map/exchange/pallas_call | solution.py:92
  15.1 0.9 copy.98
  16.0 0.1 reshape.150
  16.2 0.1 reshape.151
  16.3 0.6 dynamic_slice.23
  16.9 0.1 reshape.148
  17.1 0.6 constant_dynamic-slice_fusion.1
  17.8 0.7 stack.16.vecs
  18.5 0.7 dynamic-slice_add_fusion
  19.2 0.1 slice_reduce_fusion.2
  19.3 0.1 select_reduce_fusion
  19.3 2.2 convert_multiply_fusion.carried
  21.5 0.5 copy.86
  22.0 0.5 copy.87
  22.6 0.3 copy.83
  22.9 0.3 copy.89
  23.2 1.0 constant_dynamic-update-slice_fusion
  24.2 0.1 copy.85
  24.3 0.8 bitcast_dynamic-update-slice_fusion
  25.1 0.9 fusion.3
  26.0 1.5 copy.88
  27.5 0.9 fusion.2
  28.4 0.9 fusion.1
  29.3 0.8 fusion.w2
  30.1 1.7 multiply_convert_fusion.gh
  31.8 432.5 %block.1 = (bf16[2048,1024]{1,0:T(8,128)(2,1)}, bf16[2048,1024]{1,0:T(8,128)(2,1)}, bf16[2048,1024]{1,0:T(8,128)(2,1)}, bf16[512,512]{1,0:T(8,128)(2,1)}, bf16[5...) custom-call(bf16[512,2048]{1,0:T(8,128)(2,1)} %tok.1, ...), custom_call_target="tpu_custom_call" | custom-call | tf_op jit(solution)/shard_map/block/pallas_call | solution.py:840
  464.4 2.9 convert_element_type.94
  467.3 1.5 convert_element_type.95
  468.8 1.4 convert_bitcast_fusion
  470.2 0.8 convert_element_type.93
  471.2 0.7 copy.96
  472.0 0.6 copy.95
  472.6 0.6 fusion.5
  473.2 0.6 copy.115
  473.7 0.8 copy.116
  474.5 0.8 copy.117
  (73 shorter events, 1.1 us)
Async XLA Ops:
  4.3 2.6 copy-start.13
  4.3 2.8 copy-start.14
  4.3 2.9 copy-start.10
  4.3 3.0 copy-start.15
  4.3 3.0 copy-start.16
  4.3 3.0 copy-start.17
  4.3 3.0 copy-start.18
  4.3 3.0 copy-start.19
  4.3 3.0 copy-start.20
  4.7 16.8 %copy-start.2 = (bf16[256,2048]{1,0:T(8,128)(2,1)S(1)}, bf16[256,2048]{1,0:T(8,128)(2,1)}, u32[]{:S(2)}) copy-start(bf16[256,2048]{1,0:T(8,128)(2,1)} %param.21) | copy-start | bytes 3145732
  16.3 6.2 %copy-start.3 = (bf16[256,3,512]{2,0,1:T(8,128)(2,1)S(1)}, bf16[256,3,512]{2,0,1:T(8,128)(2,1)}, u32[]{:S(2)}) copy-start(bf16[256,3,512]{2,0,1:T(8,128)(2,1)} %param.17) | copy-start | bytes 2359300
  22.9 1.3 copy-start.9
  27.5 2.6 copy-start
  464.3 2.9 copy-start.1
  464.4 4.4 copy-start.4
  467.3 2.9 copy-start.7
  467.3 3.7 copy-start.8
  467.3 5.3 %copy-start.12 = (f32[8,256]{1,0:T(8,128)S(1)}, f32[8,256]{1,0:T(8,128)}, u32[]{:S(2)}) copy-start(f32[8,256]{1,0:T(8,128)} %get-tuple-element.27) | copy-start | bytes 24580
  467.3 6.4 %copy-start.6 = (bf16[512,512]{1,0:T(8,128)(2,1)S(1)}, bf16[512,512]{1,0:T(8,128)(2,1)}, u32[]{:S(2)}) copy-start(bf16[512,512]{1,0:T(8,128)(2,1)} %get-tuple-element.159) | copy-start | bytes 1572868
  468.8 5.7 %copy-start.5 = (bf16[512,512]{1,0:T(8,128)(2,1)S(1)}, bf16[512,512]{1,0:T(8,128)(2,1)}, u32[]{:S(2)}) copy-start(bf16[512,512]{1,0:T(8,128)(2,1)} %get-tuple-element.160) | copy-start | bytes 1572868
  473.2 2.2 copy-start.11

commit v6 on v5

--- a/solution.py
+++ b/solution.py
@@ -102,13 +102,14 @@
 
 GROUPS = 3
 ORDER = (
-    "pair0", "own0i", "pair1", "own1o", "own0o", "own1i", "mate0o", "mate0i", "rx0", "mate1i", "mate1o",
-    "arr01", "arr11", "pair2", "own2i", "rc0", "rx1", "arr02", "rc1", "stats", "arr03", "arr12", "proj",
-    "datt", "arr13", "mate2i", "ffn0", "kv1k", "st13i", "kv1v", "st12o", "st12i", "mate2o", "kv2v", "own2o",
-    "kv2k", "att0", "att1", "arr21", "st11i", "att2", "att3", "arr22", "st11o", "dn0", "sta3i", "arr23",
-    "sta2i", "dn1k", "ffn1", "sta2o", "out", "st23i", "dn1v", "far0", "st22i", "mt0", "dn2v", "st22o", "dn2k",
-    "stb3i", "last0", "st21o", "hid", "st21i", "qk", "stb2o", "far1", "stb2i", "fin1", "sta1i", "fin2",
-    "sta1o", "stb1o", "mt1", "stb1i", "fina", "finb", "small", "last1",
+    "own1o", "pair0", "pair2", "own0i", "pair1", "rx0", "own0o", "mate0i", "own1i", "mate0o", "arr01",
+    "own2i", "arr02", "mate1i", "mate1o", "rx1", "rc0", "arr03", "rc1", "stats", "arr11", "mate2i", "arr12",
+    "proj", "datt", "arr13", "ffn0", "kv1k", "st13i", "kv1v", "qd1", "kv2k", "mate2o", "st12i", "kv2v",
+    "own2o", "att0", "att1", "arr21", "st12o", "st11i", "att2", "att3", "arr22", "qd2", "sta3i", "st11o",
+    "sta2i", "sta2o", "ls0", "sta1i", "arr23", "ffn1", "st23i", "sta1o", "out", "ls1", "dkv0", "fin1",
+    "far00", "far01", "st22i", "st22o", "fina", "dkv1", "mt0", "dkv2", "st21i", "dkv3", "st21o", "last0",
+    "stb3i", "hid", "qk", "stb2i", "stb2o", "far10", "fin2", "far11", "stb1i", "stb1o", "small", "mt1",
+    "finb", "last1",
 )
 
 
@@ -123,11 +124,11 @@
 
 def block_kernel(
     dims,
-    tok, gh, w2, vecs, bq, bin_, bias, carried, tabs, first,
+    tok, gh, w2, vecs, bq, bin_, bias, carried, tabs, firstq,
     wa_o, w0_o, w1_o, mixed_o, dtok_o, norm_o, bias_o, dq_o, dd_o, di_o, do_o,
-    xs, gs, wbuf, wk, wv, qs, das, act, dpre, dqkv, att, rcv, dtmp, tpr0, tpr1, tpr2,
-    rs_a, rs_f, mean, rstd, tra, trf, sums, bsum, sum_s, sum_r, row_r, nrm_r,
-    lsem, tsem, psem, zsem, zrec, ksem, dsem, ssem, rsem, fsem, bsem, xsem, near_ok, far_ok, mate_ok,
+    xs, gs, wbuf, wk, wv, wq, wd, st, act, dpre, dqkv, att, tpr0, tpr1, tpr2,
+    rs_a, rs_f, norms, tra, trf, sums, bsum, sum_s, sum_r, row_r, nrm_r,
+    lsem, tsem, psem, zsem, zrec, ksem, qsem, lssem, ssem, rsem, fsem, bsem, xsem, usem, near_ok, far_ok, mate_ok,
 ):
     R, D, feats, dp, reach = dims
     F, T = 2 * dp, tpr0.shape[0] * 2
@@ -268,15 +269,15 @@
         rows_own(a).wait()
 
     def hat(at):
-        return (xs[at, :].astype(F32) - mean[at, :]) * rstd[at, :]
+        return (xs[at, :].astype(F32) - norms[at, 0:1]) * norms[at, 1:2]
 
     def stats():
         def block(b, _):
             x = xs[rows(b), :].astype(F32)
             m = jnp.mean(x, axis=-1, keepdims=True)
             c = x - m
-            mean[rows(b), :] = m
-            rstd[rows(b), :] = lax.rsqrt(jnp.mean(c * c, axis=-1, keepdims=True) + EPS)
+            norms[rows(b), 0:1] = m
+            norms[rows(b), 1:2] = lax.rsqrt(jnp.mean(c * c, axis=-1, keepdims=True) + EPS)
             return 0
 
         rows_done(0)
@@ -287,7 +288,7 @@
             at = rows(b)
             h1 = (hat(at) * vecs[0:1, :] + vecs[1:2, :]).astype(BF16)
             y = plain(h1, wbuf[:, : 3 * HDIM]) + bq[...]
-            qs[at, :] = (turn(y[:, :HDIM], tabs, at, 1).astype(BF16).astype(F32) * scale).astype(BF16)
+            wq[0, at, :] = (turn(y[:, :HDIM], tabs, at, 1).astype(BF16).astype(F32) * scale).astype(BF16)
             wk[reach, at, :] = turn(y[:, HDIM : 2 * HDIM], tabs, at, 1).astype(BF16)
             wv[reach, at, :] = y[:, 2 * HDIM :].astype(BF16)
             return 0
@@ -304,11 +305,16 @@
     def datt():
         def block(b, _):
             at = rows(b)
-            das[at, :] = plain(gs[at, :], wbuf[:, 3 * HDIM :]).astype(BF16)
+            wd[0, at, :] = plain(gs[at, :], wbuf[:, 3 * HDIM :]).astype(BF16)
             return 0
 
         rows_done(1)
         lax.fori_loop(0, nb, block, 0)
+
+        @pl.when(has[1])
+        def _():
+            qd_copy(0, 0).start()
+            qd_copy(1, 0).start()
 
     def ffn(h):
         mine = slice(h * hu, (h + 1) * hu)
@@ -350,108 +356,108 @@
         def _():
             (wk, wv)[h][reach - k] = jnp.zeros((plane, HDIM), BF16)
 
+    def qd_copy(h, k):
+        w = (wq, wd)[h]
+        return rc(w.at[k], w.at[k + 1], qsem.at[h, 0, k], qsem.at[h, 1, k + 1], toward(1))
+
+    def qd_recv(h, k):
+        w = (wq, wd)[h]
+        return rc(w.at[k], w.at[k], qsem.at[h, 0, k - 1], qsem.at[h, 1, k], toward(1))
+
+    def qd_step(k):
+        @pl.when(d + k < dp)
+        def _():
+            for h in range(2):
+                qd_recv(h, k).wait_recv()
+                if k < reach:
+                    @pl.when(has[1])
+                    def _():
+                        qd_copy(h, k).start()
+
+        @pl.when(d + k >= dp)
+        def _():
+            for h in range(2):
+                (wq, wd)[h][k] = jnp.zeros((plane, HDIM), BF16)
+
+    def stat_at(k):
+        return st.at[:, pl.ds(k * plane, plane)]
+
+    def stat_copy(k):
+        return rc(stat_at(0), stat_at(k), lssem.at[0, k], lssem.at[1, k], (f - 2 * k, t))
+
+    def stat_send():
+        for k in range(1, reach + 1):
+            @pl.when(d >= k)
+            def _():
+                stat_copy(k).start()
+
+    def stat_wait():
+        for k in range(1, reach + 1):
+            @pl.when(d + k < dp)
+            def _():
+                stat_copy(k).wait_recv()
+
+            @pl.when(d + k >= dp)
+            def _():
+                st[:, k * plane : (k + 1) * plane] = jnp.zeros((8, plane), F32)
+
     span = SEQ_LEN + qb
     base = reach * plane - SEQ_LEN
     parts = 4
 
-    def attention(acc, n):
+    def attention(n):
         def block(b, _):
             at = rows(b)
             keys_at = pl.ds(pl.multiple_of(base + b * qb, qb), span)
             keys = wk.reshape((reach + 1) * plane, HDIM)[keys_at, :]
             vals = wv.reshape((reach + 1) * plane, HDIM)[keys_at, :]
-            q = qs[at, :]
-            s = against(q, keys)
+            s = against(wq[0, at, :], keys)
             c = base + b * qb + lax.broadcasted_iota(jnp.int32, (qb, span), 1)
             r = reach * plane + b * qb + lax.broadcasted_iota(jnp.int32, (qb, span), 0)
-            s = jnp.where((c >= first[at, :]) & (c <= r), s, -1e30)
-            e = jnp.exp(s - jnp.max(s, axis=1, keepdims=True))
-            p = e * (1.0 / jnp.sum(e, axis=1, keepdims=True))
-            pb = p.astype(BF16)
-            att[at, :] = plain(pb, vals).astype(BF16)
-            da = das[at, :]
-            dpr = against(da, vals)
+            low = jnp.broadcast_to(firstq[:, at].astype(F32), (128, qb)).T[:, 0:1] + float(reach * plane)
+            s = jnp.where((c.astype(F32) >= low) & (c <= r), s, -1e30)
+            top = jnp.max(s, axis=1, keepdims=True)
+            e = jnp.exp(s - top)
+            total = jnp.sum(e, axis=1, keepdims=True)
+            p = e * (1.0 / total)
+            att[at, :] = plain(p.astype(BF16), vals).astype(BF16)
+            dpr = against(wd[0, at, :], vals)
             delta = jnp.sum(p * dpr, axis=1, keepdims=True)
             ds = (p * (dpr - delta)).astype(BF16)
             dq = plain(ds, keys) * scale
             dqkv[at, :HDIM] = turn(dq, tabs, at, -1).astype(BF16)
-            acc[keys_at, :HDIM] += inner(ds, q)
-            acc[keys_at, HDIM:] += inner(pb, da)
-            return 0
-
-        if n == 0:
-            acc[...] = jnp.zeros_like(acc)
+            lane = lax.broadcasted_iota(jnp.int32, (qb, 128), 1)
+            both = jnp.where(lane == 0, top + jnp.log(total), jnp.where(lane == 1, delta, 0.0))
+            st[:, at] = both.T[:8]
+            return 0
+
         lax.fori_loop(n * nb // parts, (n + 1) * nb // parts, block, 0)
 
-    dwin = (wk, wv)
-
-    def down_copy(h, r):
-        src = dwin[h].at[0] if r == 0 else dtmp.at[h]
-        return rc(src, rcv.at[h, r], dsem.at[h, 0, r], dsem.at[h, 1, r], toward(1))
-
-    def down_first(acc):
-        for k in range(reach):
-            @pl.when((d >= k) & has[0])
-            def _():
-                kv_copy(0, k).wait_send()
-                kv_copy(1, k).wait_send()
-
-        for r in range(reach + 1):
-            for h in range(2):
-                dwin[h][r] = acc[pl.ds(r * plane, plane), h * HDIM : (h + 1) * HDIM].astype(BF16)
-            if r == 0:
-                @pl.when(d >= reach)
-                def _():
-                    down_copy(0, 0).start()
-                    down_copy(1, 0).start()
-
-    def down_step(h, r):
-        def keep(b, _):
-            dtmp[h, rows(b), :] = dwin[h][r, rows(b), :]
-            return 0
-
-        def add(b, _):
+    def key_grads(n):
+        def block(b, _):
             at = rows(b)
-            v = dwin[h][r, at, :].astype(F32) + rcv[h, r - 1, at, :].astype(F32)
-            dtmp[h, at, :] = v.astype(BF16)
-            return 0
-
-        def turned(b, _):
-            at = rows(b)
-            v = dtmp[h, at, :]
-            dqkv[at, (h + 1) * HDIM : (h + 2) * HDIM] = (
-                turn(v.astype(F32), tabs, at, -1).astype(BF16) if h == 0 else v
-            )
-            return 0
-
-        came = has[0] & (d >= reach - r)
-        if r > 1:
-            @pl.when(d >= reach - r + 1)
-            def _():
-                down_copy(h, r - 1).wait_send()
-
-        @pl.when(came)
-        def _():
-            down_copy(h, r - 1).wait_recv()
-            lax.fori_loop(0, nb, add, 0)
-
-        @pl.when(jnp.logical_not(came))
-        def _():
-            lax.fori_loop(0, nb, keep, 0)
-
-        if r < reach:
-            @pl.when(d >= reach - r)
-            def _():
-                down_copy(h, r).start()
-        else:
-            lax.fori_loop(0, nb, turned, 0)
+            rows_at = pl.ds(pl.multiple_of(b * qb, qb), span)
+            q = wq.reshape((reach + 1) * plane, HDIM)[rows_at, :]
+            da = wd.reshape((reach + 1) * plane, HDIM)[rows_at, :]
+            s = against(wk[reach, at, :], q)
+            c = b * qb + lax.broadcasted_iota(jnp.int32, (qb, span), 0)
+            r = b * qb + lax.broadcasted_iota(jnp.int32, (qb, span), 1)
+            s = jnp.where((c >= firstq[:, rows_at]) & (c <= r), s - st[0:1, rows_at], -1e30)
+            p = jnp.exp(s)
+            dqkv[at, 2 * HDIM :] = plain(p.astype(BF16), da).astype(BF16)
+            dpr = against(wv[reach, at, :], da)
+            ds = (p * (dpr - st[1:2, rows_at])).astype(BF16)
+            dqkv[at, HDIM : 2 * HDIM] = turn(plain(ds, q), tabs, at, -1).astype(BF16)
+            return 0
+
+        lax.fori_loop(n * nb // parts, (n + 1) * nb // parts, block, 0)
 
     def rs(g):
         return rs_a.at[g] if g < 2 else rs_f.at[g - 2]
 
     def grad_part(g, p, c):
         cols = pl.ds(pl.multiple_of(p * pf + c * fb, fb), fb)
-        z = (xs[:, cols].astype(F32) - mean[...]) * rstd[...]
+        z = (xs[:, cols].astype(F32) - norms[:, 0:1]) * norms[:, 1:2]
         n = 0 if g < 2 else 2
         h = (z * vecs[n : n + 1, cols] + vecs[n + 1 : n + 2, cols]).astype(BF16)
         if g == 0:
@@ -551,20 +557,20 @@
         for c in final_copies(g):
             c.start()
 
-    def out_step(up, wd):
+    def out_step(up, wdense):
         def block(b, _):
             at = rows(b)
             sums[4:5, :] += jnp.sum(gs[at, :].astype(F32), axis=0, keepdims=True)
             for c in range(T):
                 cols = slice(c * pw, (c + 1) * pw)
-                y = against(att[at, :], wd[cols, :]) + against(act[at, :], wbuf[cols, :])
+                y = against(att[at, :], wdense[cols, :]) + against(act[at, :], wbuf[cols, :])
                 up[c, at, :] = y.astype(BF16)
             return 0
 
         load(
             (w0_o.at[:, pl.ds(hu, hu)], wbuf.at[:, pl.ds(0, hu)]),
             (w1_o.at[:, pl.ds(hu, hu)], wbuf.at[:, pl.ds(hu, hu)]),
-            (wa_o.at[:, pl.ds(3 * HDIM, HDIM)], wd),
+            (wa_o.at[:, pl.ds(3 * HDIM, HDIM)], wdense),
             (carried, env["kept"]),
         )
         lax.fori_loop(0, nb, block, 0)
@@ -612,57 +618,67 @@
         sum_r[f] = sum_s[f]
         bias_o[f] = bsum[...]
 
-    def near_copy(up, j):
-        return rc(up.at[tn if j == 0 else lax.rem(tn + 2, T)], tpr0.at[j], tsem.at[2, j], tsem.at[3, j], near)
-
-    def far_copy(up):
-        return rc(up.at[tf], tpr1, tsem.at[2, 2], tsem.at[3, 2], far)
+    def half(h):
+        return pl.ds(pl.multiple_of((1 - i if h == 0 else i) * R, R), R)
+
+    def half_block(h, b):
+        return pl.ds(pl.multiple_of((1 - i if h == 0 else i) * R + b * qb, qb), qb)
+
+    def near_copy(up, h, j):
+        blk = tn if j == 0 else lax.rem(tn + 2, T)
+        n = 2 * h + j
+        return rc(up.at[blk, half(h)], tpr0.at[j, half(h)], usem.at[0, n], usem.at[1, n], near)
+
+    def far_copy(up, h):
+        return rc(up.at[tf, half(h)], tpr1.at[half(h)], usem.at[0, 4 + h], usem.at[1, 4 + h], far)
 
     def mate_copy(up):
-        return rc(up.at[t, pl.ds((1 - i) * R, R), :], tpr2, tsem.at[2, 3], tsem.at[3, 3], mate)
+        return rc(up.at[t, half(0)], tpr2, usem.at[0, 6], usem.at[1, 6], mate)
 
     def tp_near(up, second):
         if second:
             pl.semaphore_wait(near_ok, 1)
-        near_copy(up, 0).start()
-        near_copy(up, 1).start()
-
-    def tp_far(up, second):
+        for h in range(2):
+            for j in (1, 0):
+                near_copy(up, h, j).start()
+
+    def tp_far(up, second, h):
         def block(b, _):
-            at = rows(b)
+            at = half_block(h, b)
             up[tf, at, :] = (up[tf, at, :].astype(F32) + tpr0[1, at, :].astype(F32)).astype(BF16)
             return 0
 
-        near_copy(up, 1).wait_recv()
-        lax.fori_loop(0, nb, block, 0)
-        if second:
+        near_copy(up, h, 1).wait_recv()
+        lax.fori_loop(0, R // qb, block, 0)
+        if second and h == 0:
             pl.semaphore_wait(far_ok, 1)
-        far_copy(up).start()
+        far_copy(up, h).start()
 
     def tp_mate(up, second):
         def block(b, _):
-            at = rows(b)
+            at = half_block(0, b)
             v = up[t, at, :].astype(F32) + tpr0[0, at, :].astype(F32) + tpr1[at, :].astype(F32)
             up[t, at, :] = v.astype(BF16)
             return 0
 
-        near_copy(up, 0).wait_recv()
-        far_copy(up).wait_recv()
-        lax.fori_loop(0, nb, block, 0)
+        near_copy(up, 0, 0).wait_recv()
+        far_copy(up, 0).wait_recv()
+        lax.fori_loop(0, R // qb, block, 0)
         if second:
             pl.semaphore_wait(mate_ok, 1)
-        else:
-            pl.semaphore_signal(near_ok, 1, device_id=near, device_id_type=MESH)
-            pl.semaphore_signal(far_ok, 1, device_id=far, device_id_type=MESH)
         mate_copy(up).start()
 
     def tp_last(up, second):
+        near_copy(up, 1, 0).wait_recv()
+        far_copy(up, 1).wait_recv()
         mate_copy(up).wait_recv()
-        here = pl.ds(pl.multiple_of(i * R, R), R)
+        here = half(1)
+        v = up[t, here, :].astype(F32) + tpr0[0, here, :].astype(F32) + tpr1[here, :].astype(F32)
+        v = v + tpr2[...].astype(F32)
         x = xs[here, pl.ds(pl.multiple_of(t * pw, pw), pw)].astype(F32)
         if second:
-            u = up[t, here, :].astype(F32) + tpr2[...].astype(F32)
-            z = (x - mean[here, :]) * rstd[here, :]
+            u = v
+            z = (x - norms[here, 0:1]) * norms[here, 1:2]
             lane = lax.broadcasted_iota(jnp.int32, (R, 128), 1)
             one, two = jnp.sum(u, axis=1, keepdims=True), jnp.sum(u * z, axis=1, keepdims=True)
             row_r[t] = jnp.where(lane == 0, one, jnp.where(lane == 1, two, 0.0)).T[:8]
@@ -674,15 +690,17 @@
             for s in range(1, T):
                 both = both + row_r[s]
             both = jnp.concatenate([both, jnp.zeros((120, R), F32)], axis=0).T * (1.0 / D)
-            dx = rstd[here, :] * (u - both[:, 0:1] - z * both[:, 1:2])
+            dx = norms[here, 1:2] * (u - both[:, 0:1] - z * both[:, 1:2])
             dtok_o[...] = (env["kept"][...] + dx).astype(BF16)
         else:
-            v = up[t, here, :].astype(F32) + tpr2[...].astype(F32)
             mixed_o[...] = (x + v + bias[...]).astype(BF16)
+            pl.semaphore_signal(near_ok, 1, device_id=near, device_id_type=MESH)
+            pl.semaphore_signal(far_ok, 1, device_id=far, device_id_type=MESH)
             pl.semaphore_signal(mate_ok, 1, device_id=mate, device_id_type=MESH)
-        near_copy(up, 0).wait_send()
-        near_copy(up, 1).wait_send()
-        far_copy(up).wait_send()
+        for h in range(2):
+            near_copy(up, h, 0).wait_send()
+            near_copy(up, h, 1).wait_send()
+            far_copy(up, h).wait_send()
         mate_copy(up).wait_send()
 
     def row_copy(s):
@@ -750,12 +768,14 @@
         elif kind == "ffn":
             ffn(int(rest))
         elif kind == "att":
-            attention(env["acc"], int(rest))
-        elif kind == "dn" and rest == "0":
-            down_first(env["acc"])
-        elif kind == "dn":
-            for r in range(1, reach) if rest[0] == "1" else (reach,):
-                down_step("kv".index(rest[1]), r)
+            attention(int(rest))
+        elif kind == "qd":
+            for k in range(1, reach) if rest == "1" else (reach,):
+                qd_step(k)
+        elif kind == "ls":
+            stat_send() if rest == "0" else stat_wait()
+        elif kind == "d":
+            key_grads(int(rest[-1]))
         elif kind == "st":
             g, k, io = groups[rest[0]], int(rest[1]), rest[2]
             if k == 3:
@@ -771,7 +791,7 @@
         elif kind == "out":
             out_step(env["up"], env["wd"])
         elif kind == "far":
-            tp_far(env["up"], rest == "1")
+            tp_far(env["up"], rest[0] == "1", int(rest[1]))
         elif kind == "mt":
             tp_mate(env["up"], rest == "1")
         elif kind == "last":
@@ -787,11 +807,6 @@
             for k in range(1, reach) if hop == 1 else (reach,):
                 kv_step("kv".index(rest[-1]), k)
 
-    def attend_scope(acc):
-        env["acc"] = acc
-        for name in ORDER[ORDER.index("att0") : ORDER.index("dn0") + 1]:
-            step(name)
-
     def finish_scope(up, wd, kept):
         env["up"], env["wd"], env["kept"] = up, wd, kept
         for name in ORDER[ORDER.index("out") :]:
@@ -799,19 +814,25 @@
 
     sums[...] = jnp.zeros_like(sums)
     bsum[...] = jnp.zeros_like(bsum)
-    for name in ORDER[: ORDER.index("att0")]:
-        step(name)
-    pl.run_scoped(attend_scope, pltpu.VMEM(((reach + 1) * plane, 2 * HDIM), F32))
-    for name in ORDER[ORDER.index("dn0") + 1 : ORDER.index("out")]:
+    for name in ORDER[: ORDER.index("out")]:
         step(name)
     pl.run_scoped(
         finish_scope, pltpu.VMEM((T, plane, pw), BF16), pltpu.VMEM((D, HDIM), BF16), pltpu.VMEM((R, pw), F32)
     )
 
-    for h in range(2):
-        @pl.when(d >= reach)
+    for k in range(reach):
+        for h in range(2):
+            @pl.when((d >= k) & has[0])
+            def _():
+                kv_copy(h, k).wait_send()
+
+            @pl.when((d + k < dp) & has[1])
+            def _():
+                qd_copy(h, k).wait_send()
+
+        @pl.when(d >= k + 1)
         def _():
-            down_copy(h, 0).wait_send()
+            stat_copy(k + 1).wait_send()
     for a in range(2):
         rows_x(a).wait_send()
         rows_c(a).wait_send()
@@ -827,7 +848,7 @@
             c.wait()
 
 
-def block(tok, gh, w2, vecs, bq, b_in, bias, carried, tabs, first, dims):
+def block(tok, gh, w2, vecs, bq, b_in, bias, carried, tabs, firstq, dims):
     R, D, feats, dp, reach = dims
     plane, pf, F, T = 2 * R, 2 * feats, 2 * dp, lax.axis_size("tp")
     gw = w2.shape[2] // GROUPS
@@ -847,24 +868,23 @@
         out_specs=[ANY] * GROUPS + [VMEM] * 4 + [ANY] * 4,
         scratch_shapes=[
             vm((plane, D), BF16), vm((plane, D), BF16), vm((D, gw), BF16),
-            win, win, vm((plane, HDIM), BF16), vm((plane, HDIM), BF16),
+            win, win, win, win, vm((8, (reach + 1) * plane), F32),
             vm((plane, gw), BF16), vm((plane, gw), BF16), vm((plane, 3 * HDIM), BF16), vm((plane, HDIM), BF16),
-            vm((2, reach, plane, HDIM), BF16), vm((2, plane, HDIM), BF16),
             vm((T // 2, plane, pw), BF16), vm((plane, pw), BF16), vm((R, pw), BF16),
             vm((2, dp + 1, pf, 2 * HDIM), BF16), vm((2, dp + 1, pf, gw), BF16),
-            vm((plane, 1), F32), vm((plane, 1), F32),
+            vm((plane, 2), F32),
             vm((2, HDIM, feats), BF16), vm((2, 2, gw // 2, feats), BF16),
             vm((8, D), F32), vm((8, gw), F32), vm((F, 8, feats), F32), vm((F, 8, feats), F32),
             vm((T, 8, R), F32), vm((T, 8, feats), F32),
             dma((GROUPS + 2,)), dma((4, 4)), dma((2, GROUPS)), dma((GROUPS, dp, 2, 2)), dma((GROUPS, F)),
-            dma((2, 2, reach + 1)), dma((2, 2, reach)), dma((4, dp, 2)), dma((4, dp + 1)), dma((4, 2, 3)),
-            dma((4,)), dma((4, 2, F)), reg, reg, reg,
+            dma((2, 2, reach + 1)), dma((2, 2, reach + 1)), dma((2, reach + 1)), dma((4, dp, 2)), dma((4, dp + 1)), dma((4, 2, 3)),
+            dma((4,)), dma((4, 2, F)), dma((2, 7)), reg, reg, reg,
         ],
         compiler_params=pltpu.CompilerParams(
             collective_id=4, has_side_effects=True, vmem_limit_bytes=63 << 20
         ),
         name="block",
-    )(tok, gh, w2, vecs, bq, b_in, bias, carried, tabs, first)
+    )(tok, gh, w2, vecs, bq, b_in, bias, carried, tabs, firstq)
 
 
 def on_device(
@@ -946,7 +966,10 @@
     reach = min(dp - 1, -(-(SEQ_LEN - 1) // plane))
     here = start_row + jnp.arange(plane, dtype=jnp.int32)
     docs_here, pos_here = locate(here, seq_starts)
-    first = (here - pos_here.astype(jnp.int32)) - (start_row - reach * plane)
+    later = start_row + jnp.arange((reach + 1) * plane, dtype=jnp.int32)
+    _, pos_later = locate(later, seq_starts)
+    first_later = later - pos_later.astype(jnp.int32) - start_row
+    first_later = jnp.where(later < total, first_later, 1 << 30)[None, :]
     cosine, sine = rotary_tables(pos_here)
     ones = jnp.ones((plane, 128 - ROT), F32)
     none = jnp.zeros((plane, 128 - ROT), F32)
@@ -965,7 +988,7 @@
     carried_here = cut(cotangent).astype(F32) * row_scale[:, None]
     _, _, _, mixed, tokens_grad, norm_grads, bias_sums, g_qkv, g_dense, g_in, g_out = block(
         tokens, grad_here, w2, vecs, b_qkv.reshape(1, -1), b_in.reshape(1, -1), bias, carried_here, tabs,
-        first[:, None], dims,
+        first_later, dims,
     )
     qkv_weight_grad = g_qkv.transpose(1, 0, 2).astype(F32)
     dense_weight_grad = g_dense.astype(F32)

time: 485 us -> 450 us (0.928)
  the two profiles are of different devices: /device:TPU:19 before, /device:TPU:20 now
where the time goes in v6:
time: 450 us; the launch traced here: 441 us
  Pallas kernels  405 us (90%)
  local copies, waits for them, and re-layouts  17.4 us (4%)
  other arithmetic  17.1 us (4%)
    pallas_call x1, Pallas kernels, block(): pl.pallas_call(functools.partial(block_kernel, dims), out_shape=[sds((D,...  397 us
    unnamed x64, local copies, waits for them, and re-layouts  9.7 us

profile of v6, /device:TPU:20, one launch (start us, length us, event | category | flops | bytes accessed | tf_op | source)
XLA Modules:
  0.0 441.3 jit_solution(18221907966693268113)
XLA Ops:
  0.7 0.7 convert_reduce_fusion.2
  1.4 0.7 select_reduce_fusion.2
  2.3 1.9 multiply_cosine_fusion
  4.4 0.3 maximum_bitcast_fusion
  4.7 1.0 pad_maximum_fusion.tabs
  5.8 0.1 convert_reduce_fusion
  5.9 0.1 select_reduce_fusion
  6.0 0.6 compare_select_fusion.firstq
  6.7 0.1 reshape.177
  6.8 0.1 reshape.175
  6.9 0.1 convert_reduce_fusion.1
  7.2 0.6 reshape.158.v_ref
  7.8 8.1 %exchange.1 = f32[8,8,256]{2,1,0:T(8,128)} custom-call(f32[8,256]{1,0:T(8,128)} %reshape.158.v_ref), custom_call_target="tpu_custom_call" | custom-call | tf_op jit(solution)/shard_map/exchange/pallas_call | solution.py:92
  15.9 0.9 copy.91
  16.9 0.1 reshape.167
  17.1 0.1 reshape.168
  17.2 0.6 dynamic_slice.23
  17.8 0.1 reshape.165
  18.0 0.6 constant_dynamic-slice_fusion.1
  18.6 0.7 stack.16.vecs
  19.4 0.7 dynamic-slice_add_fusion
  20.0 0.1 slice_reduce_fusion.2
  20.1 0.1 select_reduce_fusion.1
  20.2 2.2 convert_multiply_fusion.carried
  22.4 0.5 copy.82
  22.9 0.5 copy.83
  23.4 0.3 copy.79
  23.8 0.3 copy.85
  24.1 1.0 constant_dynamic-update-slice_fusion
  25.0 0.1 copy.81
  25.2 0.8 bitcast_dynamic-update-slice_fusion
  26.0 0.9 fusion.3
  26.8 1.5 copy.84
  28.4 0.9 fusion.2
  29.2 0.9 fusion.1
  30.1 0.8 fusion.w2
  31.0 1.7 multiply_convert_fusion.gh
  32.7 397.2 %block.1 = (bf16[2048,1024]{1,0:T(8,128)(2,1)}, bf16[2048,1024]{1,0:T(8,128)(2,1)}, bf16[2048,1024]{1,0:T(8,128)(2,1)}, bf16[512,512]{1,0:T(8,128)(2,1)}, bf16[5...) custom-call(bf16[512,2048]{1,0:T(8,128)(2,1)} %tok.1, ...), custom_call_target="tpu_custom_call" | custom-call | tf_op jit(solution)/shard_map/block/pallas_call | solution.py:861
  429.9 2.9 convert_element_type.100
  432.8 1.5 convert_element_type.101
  434.3 1.4 convert_bitcast_fusion
  435.7 0.8 convert_element_type.99
  436.7 0.7 copy.90
  437.5 0.6 copy.89
  438.1 0.6 fusion.5
  438.7 0.6 copy.108
  439.3 0.8 copy.109
  440.1 0.8 copy.110
  (78 shorter events, 1.2 us)
Async XLA Ops:
  2.2 3.6 copy-start.10
  2.2 4.4 %copy-start.14 = (bf16[32,8]{0,1:T(8,128)(2,1)S(1)}, bf16[32,8]{0,1:T(8,128)(2,1)}, u32[]{:S(2)}) copy-start(bf16[32,8]{0,1:T(8,128)(2,1)} %param.22) | copy-start | bytes 1540
  2.2 4.6 %copy-start.15 = (bf16[3,2,32]{2,1,0:T(2,128)(2,1)S(1)}, bf16[3,2,32]{2,1,0:T(2,128)(2,1)}, u32[]{:S(2)}) copy-start(bf16[3,2,32]{2,1,0:T(2,128)(2,1)} %param.18) | copy-start | bytes 1156
  2.2 4.7 %copy-start.11 = (s32[512]{0:T(512)S(1)}, s32[512]{0:T(512)}, u32[]{:S(2)}) copy-start(s32[512]{0:T(512)} %param.30) | copy-start | bytes 6148
  2.2 4.8 %copy-start.16 = (bf16[256]{0:T(256)(128)(2,1)S(1)}, bf16[256]{0:T(256)(128)(2,1)}, u32[]{:S(2)}) copy-start(bf16[256]{0:T(256)(128)(2,1)} %param.25) | copy-start | bytes 1540
  2.3 4.8 %copy-start.17 = (bf16[256]{0:T(256)(128)(2,1)S(1)}, bf16[256]{0:T(256)(128)(2,1)}, u32[]{:S(2)}) copy-start(bf16[256]{0:T(256)(128)(2,1)} %param.26) | copy-start | bytes 1540
  2.3 4.8 %copy-start.18 = (bf16[256]{0:T(256)(128)(2,1)S(1)}, bf16[256]{0:T(256)(128)(2,1)}, u32[]{:S(2)}) copy-start(bf16[256]{0:T(256)(128)(2,1)} %param.27) | copy-start | bytes 1540
  2.3 4.8 %copy-start.19 = (bf16[256]{0:T(256)(128)(2,1)S(1)}, bf16[256]{0:T(256)(128)(2,1)}, u32[]{:S(2)}) copy-start(bf16[256]{0:T(256)(128)(2,1)} %param.28) | copy-start | bytes 1540
  2.3 4.8 %copy-start.20 = (bf16[256]{0:T(256)(128)(2,1)S(1)}, bf16[256]{0:T(256)(128)(2,1)}, u32[]{:S(2)}) copy-start(bf16[256]{0:T(256)(128)(2,1)} %param.20) | copy-start | bytes 1540
  2.3 4.8 %copy-start.21 = (bf16[256]{0:T(256)(128)(2,1)S(1)}, bf16[256]{0:T(256)(128)(2,1)}, u32[]{:S(2)}) copy-start(bf16[256]{0:T(256)(128)(2,1)} %param.24) | copy-start | bytes 1540
  4.7 17.6 %copy-start.2 = (bf16[256,2048]{1,0:T(8,128)(2,1)S(1)}, bf16[256,2048]{1,0:T(8,128)(2,1)}, u32[]{:S(2)}) copy-start(bf16[256,2048]{1,0:T(8,128)(2,1)} %param.21) | copy-start | bytes 3145732
  17.2 6.2 %copy-start.3 = (bf16[256,3,512]{2,0,1:T(8,128)(2,1)S(1)}, bf16[256,3,512]{2,0,1:T(8,128)(2,1)}, u32[]{:S(2)}) copy-start(bf16[256,3,512]{2,0,1:T(8,128)(2,1)} %param.17) | copy-start | bytes 2359300
  23.7 1.3 copy-start.9
  28.3 2.6 copy-start
  429.9 2.9 copy-start.1
  429.9 4.4 %copy-start.4 = (bf16[3,256,512]{2,1,0:T(8,128)(2,1)S(1)}, bf16[3,256,512]{2,1,0:T(8,128)(2,1)}, u32[]{:S(2)}) copy-start(bf16[3,256,512]{2,1,0:T(8,128)(2,1)} %get-tuple-element.24) | copy-start | bytes 2359300
  432.8 2.9 copy-start.7
  432.8 3.7 copy-start.8
  432.8 5.3 %copy-start.13 = (f32[8,256]{1,0:T(8,128)S(1)}, f32[8,256]{1,0:T(8,128)}, u32[]{:S(2)}) copy-start(f32[8,256]{1,0:T(8,128)} %get-tuple-element.27) | copy-start | bytes 24580
  432.8 6.4 %copy-start.6 = (bf16[512,512]{1,0:T(8,128)(2,1)S(1)}, bf16[512,512]{1,0:T(8,128)(2,1)}, u32[]{:S(2)}) copy-start(bf16[512,512]{1,0:T(8,128)(2,1)} %get-tuple-element.159) | copy-start | bytes 1572868
  434.3 5.7 %copy-start.5 = (bf16[512,512]{1,0:T(8,128)(2,1)S(1)}, bf16[512,512]{1,0:T(8,128)(2,1)}, u32[]{:S(2)}) copy-start(bf16[512,512]{1,0:T(8,128)(2,1)} %get-tuple-element.160) | copy-start | bytes 1572868
  438.7 2.2 copy-start.12

commit v7 on v6

--- a/solution.py
+++ b/solution.py
@@ -100,16 +100,19 @@
     )(value)
 
 
-GROUPS = 3
+NB = 4
+GROUPS = 1 + NB
 ORDER = (
-    "own1o", "pair0", "pair2", "own0i", "pair1", "rx0", "own0o", "mate0i", "own1i", "mate0o", "arr01",
-    "own2i", "arr02", "mate1i", "mate1o", "rx1", "rc0", "arr03", "rc1", "stats", "arr11", "mate2i", "arr12",
-    "proj", "datt", "arr13", "ffn0", "kv1k", "st13i", "kv1v", "qd1", "kv2k", "mate2o", "st12i", "kv2v",
-    "own2o", "att0", "att1", "arr21", "st12o", "st11i", "att2", "att3", "arr22", "qd2", "sta3i", "st11o",
-    "sta2i", "sta2o", "ls0", "sta1i", "arr23", "ffn1", "st23i", "sta1o", "out", "ls1", "dkv0", "fin1",
-    "far00", "far01", "st22i", "st22o", "fina", "dkv1", "mt0", "dkv2", "st21i", "dkv3", "st21o", "last0",
-    "stb3i", "hid", "qk", "stb2i", "stb2o", "far10", "fin2", "far11", "stb1i", "stb1o", "small", "mt1",
-    "finb", "last1",
+    "pair0", "own0i", "own0o", "own1o", "mate0o", "pair1", "pair4", "rx0", "pair3", "mate0i", "mate1i",
+    "mate1o", "own3i", "arr01", "own1i", "rc0", "pair2", "mate3i", "arr02", "own2i", "rx1", "arr11", "arr03",
+    "mate2i", "rc1", "stats", "arr12", "own4i", "proj", "mate4i", "datt", "arr13", "ffn0", "kv1k", "kv1v",
+    "qd1", "mate2o", "st13i", "st12o", "st12i", "own2o", "st11i", "mate3o", "kv2v", "own4o", "kv2k", "att0",
+    "att1", "att2", "att3", "ls0", "sta3i", "arr21", "sta2i", "qd2", "ls1", "dkv0", "mate4o", "sta2o", "dkv1",
+    "dkv2", "arr22", "dkv3", "sta1i", "arr41", "stb3i", "arr23", "own3o", "ffn1", "st23i", "arr31", "st22o",
+    "st22i", "arr32", "stb2i", "arr33", "stb2o", "arr42", "st21i", "ffn2", "st33i", "st11o", "arr43", "ffn3",
+    "out", "stb1i", "st43i", "st32o", "hid", "stb1o", "far00", "far01", "qk", "sta1o", "st21o", "st32i",
+    "far10", "finb", "st42o", "mt0", "far11", "fina", "fin1", "st42i", "st31i", "st31o", "last0", "small",
+    "mt1", "st41i", "fin2", "st41o", "fin3", "last1", "fin4",
 )
 
 
@@ -124,14 +127,17 @@
 
 def block_kernel(
     dims,
-    tok, gh, w2, vecs, bq, bin_, bias, carried, tabs, firstq,
-    wa_o, w0_o, w1_o, mixed_o, dtok_o, norm_o, bias_o, dq_o, dd_o, di_o, do_o,
-    xs, gs, wbuf, wk, wv, wq, wd, st, act, dpre, dqkv, att, tpr0, tpr1, tpr2,
-    rs_a, rs_f, norms, tra, trf, sums, bsum, sum_s, sum_r, row_r, nrm_r,
-    lsem, tsem, psem, zsem, zrec, ksem, qsem, lssem, ssem, rsem, fsem, bsem, xsem, usem, near_ok, far_ok, mate_ok,
+    tok, gh, w2, vecs, bq, bin_, bias, cot, row_scale, tabs, firstq,
+    *refs,
 ):
+    outs, refs = refs[:GROUPS], refs[GROUPS:]
+    (
+        mixed_o, dtok_o, norm_o, bias_o, dq_o, dd_o, di_o, do_o, xs, gs, wbuf, wins, st,
+        act, dpre, dqkv, att, tpr0, tpr1, tpr2, rs_a, rs_f, norms, tra, trf, sums, bsum, sum_s, sum_r, row_r, nrm_r,
+        lsem, tsem, psem, zsem, zrec, ksem, qsem, lssem, ssem, rsem, fsem, bsem, xsem, usem, near_ok, far_ok, mate_ok,
+    ) = refs
     R, D, feats, dp, reach = dims
-    F, T = 2 * dp, tpr0.shape[0] * 2
+    F, T = 2 * dp, row_r.shape[0]
     f = lax.axis_index("fsdp")
     t = lax.axis_index("tp")
     d, i = f // 2, lax.rem(f, 2)
@@ -140,15 +146,16 @@
     qb = min(256, plane)
     nb = plane // qb
     fb = min(256, pf)
-    gw = w2.shape[2] // GROUPS
-    hu = gw // 2
+    aw = 4 * HDIM
+    gw = act.shape[1]
+    hu = gw // NB
     pw = D // T
+    slots = reach + 1
     tn, tf = t + 1 - 2 * core, lax.rem(t + 2, T)
     mate, near, far = (f + 1 - 2 * i, t), (f, tn), (f, tf)
     has = (d + 1 < dp, d >= 1)
     inward = jnp.where(d < dp // 2, 0, 1)
     ways = {"i": inward, "o": 1 - inward}
-    outs = (wa_o, w0_o, w1_o)
     scale = 1.0 / math.sqrt(HDIM)
 
     barrier = pltpu.get_barrier_semaphore()
@@ -176,7 +183,8 @@
         return outs[g].at[pl.ds(s * feats, feats), :]
 
     def part(half, g):
-        return w2.at[half, :, pl.ds(g * gw, gw)]
+        cols = pl.ds(0, aw) if g == 0 else pl.ds(aw + (g - 1) * 2 * hu, 2 * hu)
+        return w2.at[half, :, cols]
 
     def pair_copy(g):
         return rc(part(1 - i, g), slot(g, f), psem.at[0, g], psem.at[1, g], mate)
@@ -288,13 +296,13 @@
             at = rows(b)
             h1 = (hat(at) * vecs[0:1, :] + vecs[1:2, :]).astype(BF16)
             y = plain(h1, wbuf[:, : 3 * HDIM]) + bq[...]
-            wq[0, at, :] = (turn(y[:, :HDIM], tabs, at, 1).astype(BF16).astype(F32) * scale).astype(BF16)
-            wk[reach, at, :] = turn(y[:, HDIM : 2 * HDIM], tabs, at, 1).astype(BF16)
-            wv[reach, at, :] = y[:, 2 * HDIM :].astype(BF16)
+            wins[2 * slots, at, :] = (turn(y[:, :HDIM], tabs, at, 1).astype(BF16).astype(F32) * scale).astype(BF16)
+            wins[reach, at, :] = turn(y[:, HDIM : 2 * HDIM], tabs, at, 1).astype(BF16)
+            wins[slots + reach, at, :] = y[:, 2 * HDIM :].astype(BF16)
             return 0
 
         mine_copy(0).wait()
-        load((wa_o, wbuf))
+        load((outs[0], wbuf))
         lax.fori_loop(0, nb, block, 0)
 
         @pl.when(has[0])
@@ -305,7 +313,7 @@
     def datt():
         def block(b, _):
             at = rows(b)
-            wd[0, at, :] = plain(gs[at, :], wbuf[:, 3 * HDIM :]).astype(BF16)
+            wins[3 * slots, at, :] = plain(gs[at, :], wbuf[:, 3 * HDIM :]).astype(BF16)
             return 0
 
         rows_done(1)
@@ -326,22 +334,22 @@
             cdf = 0.5 * (1.0 + lax.erf(pre * (1.0 / math.sqrt(2.0))))
             act[at, mine] = (pre * cdf).astype(BF16)
             slope = cdf + pre * jnp.exp(-0.5 * pre * pre) * (1.0 / math.sqrt(2.0 * math.pi))
-            dp_b = (plain(gs[at, :], wbuf[:, hu:]) * slope).astype(BF16)
+            dp_b = (plain(gs[at, :], wbuf[:, hu : 2 * hu]) * slope).astype(BF16)
             dpre[at, mine] = dp_b
             bsum[0:1, mine] += jnp.sum(dp_b.astype(F32), axis=0, keepdims=True)
             return 0
 
         mine_copy(1 + h).wait()
-        load((outs[1 + h], wbuf))
+        load((outs[1 + h], wbuf.at[:, pl.ds(0, 2 * hu)]))
         lax.fori_loop(0, nb, block, 0)
 
     def kv_copy(h, k):
-        w = (wk, wv)[h]
-        return rc(w.at[reach - k], w.at[reach - k - 1], ksem.at[h, 0, k], ksem.at[h, 1, k + 1], toward(0))
+        w = wins.at[h * slots + reach - k]
+        return rc(w, wins.at[h * slots + reach - k - 1], ksem.at[h, 0, k], ksem.at[h, 1, k + 1], toward(0))
 
     def kv_recv(h, k):
-        w = (wk, wv)[h]
-        return rc(w.at[reach - k], w.at[reach - k], ksem.at[h, 0, k - 1], ksem.at[h, 1, k], toward(0))
+        w = wins.at[h * slots + reach - k]
+        return rc(w, w, ksem.at[h, 0, k - 1], ksem.at[h, 1, k], toward(0))
 
     def kv_step(h, k):
         @pl.when(d >= k)
@@ -354,15 +362,15 @@
 
         @pl.when(d < k)
         def _():
-            (wk, wv)[h][reach - k] = jnp.zeros((plane, HDIM), BF16)
+            wins[h * slots + reach - k] = jnp.zeros((plane, HDIM), BF16)
 
     def qd_copy(h, k):
-        w = (wq, wd)[h]
-        return rc(w.at[k], w.at[k + 1], qsem.at[h, 0, k], qsem.at[h, 1, k + 1], toward(1))
+        w = wins.at[(2 + h) * slots + k]
+        return rc(w, wins.at[(2 + h) * slots + k + 1], qsem.at[h, 0, k], qsem.at[h, 1, k + 1], toward(1))
 
     def qd_recv(h, k):
-        w = (wq, wd)[h]
-        return rc(w.at[k], w.at[k], qsem.at[h, 0, k - 1], qsem.at[h, 1, k], toward(1))
+        w = wins.at[(2 + h) * slots + k]
+        return rc(w, w, qsem.at[h, 0, k - 1], qsem.at[h, 1, k], toward(1))
 
     def qd_step(k):
         @pl.when(d + k < dp)
@@ -377,7 +385,7 @@
         @pl.when(d + k >= dp)
         def _():
             for h in range(2):
-                (wq, wd)[h][k] = jnp.zeros((plane, HDIM), BF16)
+                wins[(2 + h) * slots + k] = jnp.zeros((plane, HDIM), BF16)
 
     def stat_at(k):
         return st.at[:, pl.ds(k * plane, plane)]
@@ -405,13 +413,17 @@
     base = reach * plane - SEQ_LEN
     parts = 4
 
+    def wide(n, start):
+        flat = wins.reshape(wins.shape[0] * plane, HDIM)
+        return flat[pl.ds(pl.multiple_of(n * slots * plane + start, qb), span), :]
+
     def attention(n):
         def block(b, _):
             at = rows(b)
-            keys_at = pl.ds(pl.multiple_of(base + b * qb, qb), span)
-            keys = wk.reshape((reach + 1) * plane, HDIM)[keys_at, :]
-            vals = wv.reshape((reach + 1) * plane, HDIM)[keys_at, :]
-            s = against(wq[0, at, :], keys)
+            keys_at = base + b * qb
+            keys = wide(0, keys_at)
+            vals = wide(1, keys_at)
+            s = against(wins[2 * slots, at, :], keys)
             c = base + b * qb + lax.broadcasted_iota(jnp.int32, (qb, span), 1)
             r = reach * plane + b * qb + lax.broadcasted_iota(jnp.int32, (qb, span), 0)
             low = jnp.broadcast_to(firstq[:, at].astype(F32), (128, qb)).T[:, 0:1] + float(reach * plane)
@@ -421,7 +433,7 @@
             total = jnp.sum(e, axis=1, keepdims=True)
             p = e * (1.0 / total)
             att[at, :] = plain(p.astype(BF16), vals).astype(BF16)
-            dpr = against(wd[0, at, :], vals)
+            dpr = against(wins[3 * slots, at, :], vals)
             delta = jnp.sum(p * dpr, axis=1, keepdims=True)
             ds = (p * (dpr - delta)).astype(BF16)
             dq = plain(ds, keys) * scale
@@ -437,15 +449,15 @@
         def block(b, _):
             at = rows(b)
             rows_at = pl.ds(pl.multiple_of(b * qb, qb), span)
-            q = wq.reshape((reach + 1) * plane, HDIM)[rows_at, :]
-            da = wd.reshape((reach + 1) * plane, HDIM)[rows_at, :]
-            s = against(wk[reach, at, :], q)
+            q = wide(2, b * qb)
+            da = wide(3, b * qb)
+            s = against(wins[reach, at, :], q)
             c = b * qb + lax.broadcasted_iota(jnp.int32, (qb, span), 0)
             r = b * qb + lax.broadcasted_iota(jnp.int32, (qb, span), 1)
             s = jnp.where((c >= firstq[:, rows_at]) & (c <= r), s - st[0:1, rows_at], -1e30)
             p = jnp.exp(s)
             dqkv[at, 2 * HDIM :] = plain(p.astype(BF16), da).astype(BF16)
-            dpr = against(wv[reach, at, :], da)
+            dpr = against(wins[slots + reach, at, :], da)
             ds = (p * (dpr - st[1:2, rows_at])).astype(BF16)
             dqkv[at, HDIM : 2 * HDIM] = turn(plain(ds, q), tabs, at, -1).astype(BF16)
             return 0
@@ -557,26 +569,35 @@
         for c in final_copies(g):
             c.start()
 
-    def out_step(up, wdense):
+    def out_step(up):
+        def dense(b, _):
+            at = rows(b)
+            for c in range(T):
+                y = against(att[at, :], wbuf[c * pw : (c + 1) * pw, :HDIM])
+                for e in range(2):
+                    v = up[2 * c + e, at, :].astype(F32) + y[:, e * HDIM : (e + 1) * HDIM]
+                    up[2 * c + e, at, :] = v.astype(BF16)
+            return 0
+
         def block(b, _):
             at = rows(b)
             sums[4:5, :] += jnp.sum(gs[at, :].astype(F32), axis=0, keepdims=True)
             for c in range(T):
                 cols = slice(c * pw, (c + 1) * pw)
-                y = against(att[at, :], wdense[cols, :]) + against(act[at, :], wbuf[cols, :])
-                up[c, at, :] = y.astype(BF16)
+                y = against(act[at, :], wbuf[cols, :])
+                for e in range(2):
+                    up[2 * c + e, at, :] = y[:, e * HDIM : (e + 1) * HDIM].astype(BF16)
             return 0
 
         load(
-            (w0_o.at[:, pl.ds(hu, hu)], wbuf.at[:, pl.ds(0, hu)]),
-            (w1_o.at[:, pl.ds(hu, hu)], wbuf.at[:, pl.ds(hu, hu)]),
-            (wa_o.at[:, pl.ds(3 * HDIM, HDIM)], wdense),
-            (carried, env["kept"]),
+            *[(outs[1 + h].at[:, pl.ds(hu, hu)], wbuf.at[:, pl.ds(h * hu, hu)]) for h in range(NB)],
         )
         lax.fori_loop(0, nb, block, 0)
+        load((outs[0].at[:, pl.ds(3 * HDIM, HDIM)], wbuf.at[:, pl.ds(0, HDIM)]))
+        lax.fori_loop(0, nb, dense, 0)
         tp_near(up, False)
 
-    def hidden_step(up):
+    def hidden_step():
         def block(b, _):
             at = rows(b)
             e2 = against(dpre[at, :], wbuf[...])
@@ -584,17 +605,28 @@
             sums[2:3, :] += jnp.sum(e2 * z, axis=0, keepdims=True)
             sums[3:4, :] += jnp.sum(e2, axis=0, keepdims=True)
             u = (e2 * vecs[2:3, :]).astype(BF16)
-            for c in range(T):
-                up[c, at, :] = u[:, c * pw : (c + 1) * pw]
-            return 0
-
+            for c in range(2 * T):
+                wins[c, at, :] = u[:, c * HDIM : (c + 1) * HDIM]
+            return 0
+
+        for k in range(reach):
+            for h in range(2):
+                @pl.when((d >= k) & has[0])
+                def _():
+                    kv_copy(h, k).wait_send()
+
+                @pl.when((d + k < dp) & has[1])
+                def _():
+                    qd_copy(h, k).wait_send()
+
+        pl.semaphore_signal(far_ok, 1, device_id=far, device_id_type=MESH)
+        pl.semaphore_signal(mate_ok, 1, device_id=mate, device_id_type=MESH)
         load(
-            (w0_o.at[:, pl.ds(0, hu)], wbuf.at[:, pl.ds(0, hu)]),
-            (w1_o.at[:, pl.ds(0, hu)], wbuf.at[:, pl.ds(hu, hu)]),
+            *[(outs[1 + h].at[:, pl.ds(0, hu)], wbuf.at[:, pl.ds(h * hu, hu)]) for h in range(NB)],
         )
         lax.fori_loop(0, nb, block, 0)
 
-    def qkv_step(up):
+    def qkv_step():
         def block(b, _):
             at = rows(b)
             e1 = against(dqkv[at, :], wbuf[:, : 3 * HDIM])
@@ -603,13 +635,13 @@
             sums[1:2, :] += jnp.sum(e1, axis=0, keepdims=True)
             bsum[1:2, : 3 * HDIM] += jnp.sum(dqkv[at, :].astype(F32), axis=0, keepdims=True)
             u = e1 * vecs[0:1, :]
-            for c in range(T):
-                up[c, at, :] = (up[c, at, :].astype(F32) + u[:, c * pw : (c + 1) * pw]).astype(BF16)
-            return 0
-
-        load((wa_o, wbuf))
+            for c in range(2 * T):
+                wins[c, at, :] = (wins[c, at, :].astype(F32) + u[:, c * HDIM : (c + 1) * HDIM]).astype(BF16)
+            return 0
+
+        load((outs[0], wbuf))
         lax.fori_loop(0, nb, block, 0)
-        tp_near(up, True)
+        tp_near(wins, True)
         for s in range(F):
             sum_s[s] = sums[:, s * feats : (s + 1) * feats]
         for s in range(1, F):
@@ -624,57 +656,76 @@
     def half_block(h, b):
         return pl.ds(pl.multiple_of((1 - i if h == 0 else i) * R + b * qb, qb), qb)
 
-    def near_copy(up, h, j):
+    def near_copy(up, second, h, j):
         blk = tn if j == 0 else lax.rem(tn + 2, T)
         n = 2 * h + j
-        return rc(up.at[blk, half(h)], tpr0.at[j, half(h)], usem.at[0, n], usem.at[1, n], near)
-
-    def far_copy(up, h):
-        return rc(up.at[tf, half(h)], tpr1.at[half(h)], usem.at[0, 4 + h], usem.at[1, 4 + h], far)
-
-    def mate_copy(up):
-        return rc(up.at[t, half(0)], tpr2, usem.at[0, 6], usem.at[1, 6], mate)
+        src = up.at[pl.ds(2 * blk, 2), half(h), :]
+        return rc(src, tpr0.at[j, :, half(h), :], usem.at[int(second), 0, n], usem.at[int(second), 1, n], near)
+
+    def landing(second):
+        return (wins.at[pl.ds(2 * T, 2)], wins.at[pl.ds(2 * T + 2, 2), pl.ds(0, R), :]) if second else (tpr1, tpr2)
+
+    def far_copy(up, h, second):
+        src, dst = up.at[pl.ds(2 * tf, 2), half(h), :], landing(second)[0].at[:, half(h), :]
+        return rc(src, dst, usem.at[int(second), 0, 4 + h], usem.at[int(second), 1, 4 + h], far)
+
+    def mate_copy(up, second):
+        n = int(second)
+        src = up.at[pl.ds(2 * t, 2), half(0), :]
+        return rc(src, landing(second)[1], usem.at[n, 0, 6], usem.at[n, 1, 6], mate)
 
     def tp_near(up, second):
         if second:
             pl.semaphore_wait(near_ok, 1)
         for h in range(2):
             for j in (1, 0):
-                near_copy(up, h, j).start()
+                near_copy(up, second, h, j).start()
 
     def tp_far(up, second, h):
         def block(b, _):
             at = half_block(h, b)
-            up[tf, at, :] = (up[tf, at, :].astype(F32) + tpr0[1, at, :].astype(F32)).astype(BF16)
-            return 0
-
-        near_copy(up, h, 1).wait_recv()
+            for blk, j in ((tf, 1), (t, 0)):
+                for e in range(2):
+                    v = up[2 * blk + e, at, :].astype(F32) + tpr0[j, e, at, :].astype(F32)
+                    up[2 * blk + e, at, :] = v.astype(BF16)
+            return 0
+
+        near_copy(up, second, h, 1).wait_recv()
+        near_copy(up, second, h, 0).wait_recv()
         lax.fori_loop(0, R // qb, block, 0)
-        if second and h == 0:
+        far_steps.append((second, h))
+        if second and (True, 1 - h) not in far_steps:
             pl.semaphore_wait(far_ok, 1)
-        far_copy(up, h).start()
+        if not second and (False, 1 - h) in far_steps:
+            pl.semaphore_signal(near_ok, 1, device_id=near, device_id_type=MESH)
+        far_copy(up, h, second).start()
+
+    def came_far(second, e, at):
+        return (wins[2 * T + e, at, :] if second else tpr1[e, at, :]).astype(F32)
 
     def tp_mate(up, second):
         def block(b, _):
             at = half_block(0, b)
-            v = up[t, at, :].astype(F32) + tpr0[0, at, :].astype(F32) + tpr1[at, :].astype(F32)
-            up[t, at, :] = v.astype(BF16)
-            return 0
-
-        near_copy(up, 0, 0).wait_recv()
-        far_copy(up, 0).wait_recv()
+            for e in range(2):
+                v = up[2 * t + e, at, :].astype(F32) + came_far(second, e, at)
+                up[2 * t + e, at, :] = v.astype(BF16)
+            return 0
+
+        far_copy(up, 0, second).wait_recv()
         lax.fori_loop(0, R // qb, block, 0)
         if second:
             pl.semaphore_wait(mate_ok, 1)
-        mate_copy(up).start()
+        mate_copy(up, second).start()
 
     def tp_last(up, second):
-        near_copy(up, 1, 0).wait_recv()
-        far_copy(up, 1).wait_recv()
-        mate_copy(up).wait_recv()
+        far_copy(up, 1, second).wait_recv()
+        mate_copy(up, second).wait_recv()
         here = half(1)
-        v = up[t, here, :].astype(F32) + tpr0[0, here, :].astype(F32) + tpr1[here, :].astype(F32)
-        v = v + tpr2[...].astype(F32)
+        v = []
+        for e in range(2):
+            last = wins[2 * T + 2 + e, :R, :] if second else tpr2[e]
+            v.append(up[2 * t + e, here, :].astype(F32) + came_far(second, e, here) + last.astype(F32))
+        v = jnp.concatenate(v, axis=1)
         x = xs[here, pl.ds(pl.multiple_of(t * pw, pw), pw)].astype(F32)
         if second:
             u = v
@@ -691,17 +742,18 @@
                 both = both + row_r[s]
             both = jnp.concatenate([both, jnp.zeros((120, R), F32)], axis=0).T * (1.0 / D)
             dx = norms[here, 1:2] * (u - both[:, 0:1] - z * both[:, 1:2])
-            dtok_o[...] = (env["kept"][...] + dx).astype(BF16)
+            kept = env["up"]
+            load((cot, kept.at[pl.ds(0, 2), pl.ds(0, R), :]))
+            c = jnp.concatenate([kept[0, :R, :], kept[1, :R, :]], axis=1).astype(F32)
+            c = c * jnp.broadcast_to(row_scale[...], (128, R)).T[:, 0:1]
+            dtok_o[...] = (c + dx).astype(BF16)
         else:
             mixed_o[...] = (x + v + bias[...]).astype(BF16)
-            pl.semaphore_signal(near_ok, 1, device_id=near, device_id_type=MESH)
-            pl.semaphore_signal(far_ok, 1, device_id=far, device_id_type=MESH)
-            pl.semaphore_signal(mate_ok, 1, device_id=mate, device_id_type=MESH)
         for h in range(2):
-            near_copy(up, h, 0).wait_send()
-            near_copy(up, h, 1).wait_send()
-            far_copy(up, h).wait_send()
-        mate_copy(up).wait_send()
+            near_copy(up, second, h, 0).wait_send()
+            near_copy(up, second, h, 1).wait_send()
+            far_copy(up, h, second).wait_send()
+        mate_copy(up, second).wait_send()
 
     def row_copy(s):
         return rc(row_r.at[t], row_r.at[t], xsem.at[0, 0, s], xsem.at[0, 1, s], (f, lax.rem(t + s, T)))
@@ -736,8 +788,8 @@
 
     env = {}
     far_out = tuple(range(dp - 1, 2, -1))
-    groups = {"a": 0, "b": 1, "1": 2, "2": 3}
-    paired = set()
+    groups = {"a": 0, "b": 1} | {str(n + 1): 2 + n for n in range(NB)}
+    paired, far_steps = set(), []
 
     def step(name):
         kind, rest = name.rstrip("0123456789abiokv"), ""
@@ -789,17 +841,17 @@
         elif kind == "fin":
             final(groups[rest])
         elif kind == "out":
-            out_step(env["up"], env["wd"])
+            out_step(env["up"])
         elif kind == "far":
-            tp_far(env["up"], rest[0] == "1", int(rest[1]))
+            tp_far(env["up"] if rest[0] == "0" else wins, rest[0] == "1", int(rest[1]))
         elif kind == "mt":
-            tp_mate(env["up"], rest == "1")
+            tp_mate(env["up"] if rest == "0" else wins, rest == "1")
         elif kind == "last":
-            tp_last(env["up"], rest == "1")
+            tp_last(env["up"] if rest == "0" else wins, rest == "1")
         elif kind == "hid":
-            hidden_step(env["up"])
+            hidden_step()
         elif kind == "q":
-            qkv_step(env["up"])
+            qkv_step()
         elif kind == "small":
             small_sums()
         else:
@@ -807,8 +859,8 @@
             for k in range(1, reach) if hop == 1 else (reach,):
                 kv_step("kv".index(rest[-1]), k)
 
-    def finish_scope(up, wd, kept):
-        env["up"], env["wd"], env["kept"] = up, wd, kept
+    def finish_scope(up):
+        env["up"] = up
         for name in ORDER[ORDER.index("out") :]:
             step(name)
 
@@ -816,20 +868,9 @@
     bsum[...] = jnp.zeros_like(bsum)
     for name in ORDER[: ORDER.index("out")]:
         step(name)
-    pl.run_scoped(
-        finish_scope, pltpu.VMEM((T, plane, pw), BF16), pltpu.VMEM((D, HDIM), BF16), pltpu.VMEM((R, pw), F32)
-    )
+    pl.run_scoped(finish_scope, pltpu.VMEM((2 * T, plane, HDIM), BF16))
 
     for k in range(reach):
-        for h in range(2):
-            @pl.when((d >= k) & has[0])
-            def _():
-                kv_copy(h, k).wait_send()
-
-            @pl.when((d + k < dp) & has[1])
-            def _():
-                qd_copy(h, k).wait_send()
-
         @pl.when(d >= k + 1)
         def _():
             stat_copy(k + 1).wait_send()
@@ -838,7 +879,7 @@
         rows_c(a).wait_send()
     for g in range(GROUPS):
         gather_sent(g)
-    for g in range(4):
+    for g in range(2 + NB):
         for k in range(1, dp):
             for way in range(2):
                 @pl.when(from_dist(k, 1 - way))
@@ -848,43 +889,44 @@
             c.wait()
 
 
-def block(tok, gh, w2, vecs, bq, b_in, bias, carried, tabs, firstq, dims):
+def block(tok, gh, w2, vecs, bq, b_in, bias, cot, row_scale, tabs, firstq, dims):
     R, D, feats, dp, reach = dims
     plane, pf, F, T = 2 * R, 2 * feats, 2 * dp, lax.axis_size("tp")
-    gw = w2.shape[2] // GROUPS
+    aw = 4 * HDIM
+    gw = (w2.shape[2] - aw) // 2
+    hu = gw // NB
     pw = D // T
     sds = jax.ShapeDtypeStruct
     vm = pltpu.VMEM
     dma = pltpu.SemaphoreType.DMA
     reg = pltpu.SemaphoreType.REGULAR
-    win = vm((reach + 1, plane, HDIM), BF16)
     return pl.pallas_call(
         functools.partial(block_kernel, dims),
-        out_shape=[sds((D, gw), BF16)] * GROUPS
+        out_shape=[sds((D, aw), BF16)] + [sds((D, 2 * hu), BF16)] * NB
         + [sds((R, pw), BF16), sds((R, pw), BF16), sds((8, feats), F32), sds((F, 8, gw), F32)]
         + [sds((3, feats, 2 * HDIM), BF16), sds((2 * HDIM, feats), BF16)]
         + [sds((feats, 2 * gw), BF16), sds((2 * gw, feats), BF16)],
-        in_specs=[ANY] * 3 + [VMEM] * 4 + [ANY] + [VMEM] * 2,
+        in_specs=[ANY] * 3 + [VMEM] * 4 + [ANY] + [VMEM] * 3,
         out_specs=[ANY] * GROUPS + [VMEM] * 4 + [ANY] * 4,
         scratch_shapes=[
-            vm((plane, D), BF16), vm((plane, D), BF16), vm((D, gw), BF16),
-            win, win, win, win, vm((8, (reach + 1) * plane), F32),
+            vm((plane, D), BF16), vm((plane, D), BF16), vm((D, max(aw, gw)), BF16),
+            vm((4 * (reach + 1), plane, HDIM), BF16), vm((8, (reach + 1) * plane), F32),
             vm((plane, gw), BF16), vm((plane, gw), BF16), vm((plane, 3 * HDIM), BF16), vm((plane, HDIM), BF16),
-            vm((T // 2, plane, pw), BF16), vm((plane, pw), BF16), vm((R, pw), BF16),
-            vm((2, dp + 1, pf, 2 * HDIM), BF16), vm((2, dp + 1, pf, gw), BF16),
+            vm((2, 2, plane, HDIM), BF16), vm((2, plane, HDIM), BF16), vm((2, R, HDIM), BF16),
+            vm((2, dp + 1, pf, 2 * HDIM), BF16), vm((NB, dp + 1, pf, 2 * hu), BF16),
             vm((plane, 2), F32),
-            vm((2, HDIM, feats), BF16), vm((2, 2, gw // 2, feats), BF16),
+            vm((2, HDIM, feats), BF16), vm((NB, 2, hu, feats), BF16),
             vm((8, D), F32), vm((8, gw), F32), vm((F, 8, feats), F32), vm((F, 8, feats), F32),
             vm((T, 8, R), F32), vm((T, 8, feats), F32),
             dma((GROUPS + 2,)), dma((4, 4)), dma((2, GROUPS)), dma((GROUPS, dp, 2, 2)), dma((GROUPS, F)),
-            dma((2, 2, reach + 1)), dma((2, 2, reach + 1)), dma((2, reach + 1)), dma((4, dp, 2)), dma((4, dp + 1)), dma((4, 2, 3)),
-            dma((4,)), dma((4, 2, F)), dma((2, 7)), reg, reg, reg,
+            dma((2, 2, reach + 1)), dma((2, 2, reach + 1)), dma((2, reach + 1)), dma((2 + NB, dp, 2)), dma((2 + NB, dp + 1)), dma((2 + NB, 2, 3)),
+            dma((NB + 2,)), dma((4, 2, F)), dma((2, 2, 7)), reg, reg, reg,
         ],
         compiler_params=pltpu.CompilerParams(
             collective_id=4, has_side_effects=True, vmem_limit_bytes=63 << 20
         ),
         name="block",
-    )(tok, gh, w2, vecs, bq, b_in, bias, carried, tabs, firstq)
+    )(tok, gh, w2, vecs, bq, b_in, bias, cot, row_scale, tabs, firstq)
 
 
 def on_device(
@@ -951,13 +993,14 @@
     carried = cotangent.astype(F32) * row_scale[:, None]
     grad_here = carried.astype(BF16)
 
-    wi = fc_in_weight.reshape(feats, 2, 2, units // 4).transpose(1, 0, 2, 3)
-    wo = fc_out_weight.reshape(2, 2, units // 4, feats).transpose(0, 3, 1, 2)
+    hu = units // 2 // NB
+    wi = fc_in_weight.reshape(feats, 2, NB, hu).transpose(1, 0, 2, 3)
+    wo = fc_out_weight.reshape(2, NB, hu, feats).transpose(0, 3, 1, 2)
     w2 = jnp.concatenate(
         [
             qkv_weight.reshape(feats, 3, heads_here, HDIM).transpose(2, 0, 1, 3).reshape(2, feats, 3 * HDIM),
             dense_weight.reshape(heads_here, HDIM, feats).transpose(0, 2, 1),
-            wi[:, :, 0], wo[:, :, 0], wi[:, :, 1], wo[:, :, 1],
+            jnp.stack([wi, wo], axis=3).reshape(2, feats, 2 * NB * hu),
         ],
         axis=2,
     )
@@ -985,11 +1028,11 @@
     offset = t * part_w
     cut = lambda vec: lax.dynamic_slice_in_dim(vec, offset, part_w, vec.ndim - 1)
     bias = (cut(b_dense) + cut(b_out)).reshape(1, -1)
-    carried_here = cut(cotangent).astype(F32) * row_scale[:, None]
-    _, _, _, mixed, tokens_grad, norm_grads, bias_sums, g_qkv, g_dense, g_in, g_out = block(
-        tokens, grad_here, w2, vecs, b_qkv.reshape(1, -1), b_in.reshape(1, -1), bias, carried_here, tabs,
+    cot_here = cut(cotangent).reshape(rows, 2, part_w // 2).transpose(1, 0, 2)
+    mixed, tokens_grad, norm_grads, bias_sums, g_qkv, g_dense, g_in, g_out = block(
+        tokens, grad_here, w2, vecs, b_qkv.reshape(1, -1), b_in.reshape(1, -1), bias, cot_here, row_scale[None, :], tabs,
         first_later, dims,
-    )
+    )[GROUPS:]
     qkv_weight_grad = g_qkv.transpose(1, 0, 2).astype(F32)
     dense_weight_grad = g_dense.astype(F32)
     fc_in_weight_grad = g_in.astype(F32)

time: 450 us -> 419 us (0.931)
  the two profiles are of different devices: /device:TPU:20 before, /device:TPU:0 now
where the time goes in v7:
time: 419 us; the launch traced here: 415 us
  Pallas kernels  373 us (89%)
  local copies, waits for them, and re-layouts  23.2 us (6%)
  other arithmetic  17.1 us (4%)
    pallas_call x1, Pallas kernels, block(): pl.pallas_call(functools.partial(block_kernel, dims), out_shape=[sds((D,...  363 us
    pallas_call x1, Pallas kernels, exchange(): pl.pallas_call(functools.partial(exchange_kernel, axis, spread), out_shap...  9.98 us

profile of v7, /device:TPU:0, one launch (start us, length us, event | category | flops | bytes accessed | tf_op | source)
XLA Modules:
  0.0 414.6 jit_solution(9978207581460311399)
XLA Ops:
  0.7 0.7 convert_reduce_fusion.2
  1.4 0.7 select_reduce_fusion.2
  2.2 1.9 multiply_cosine_fusion
  4.3 0.3 maximum_bitcast_fusion
  4.7 1.0 pad_maximum_fusion.2.tabs
  5.7 0.1 convert_reduce_fusion
  5.9 0.1 select_reduce_fusion
  6.0 0.6 compare_select_fusion.firstq
  6.7 0.1 reshape.185
  6.9 0.1 convert_reduce_fusion.1
  7.1 0.6 reshape.164.v_ref
  7.7 10.0 %exchange.1 = f32[8,8,256]{2,1,0:T(8,128)} custom-call(f32[8,256]{1,0:T(8,128)} %reshape.164.v_ref), custom_call_target="tpu_custom_call" | custom-call | tf_op jit(solution)/shard_map/exchange/pallas_call | solution.py:92
  17.7 0.9 copy.106
  18.7 0.1 reshape.174
  18.9 0.1 reshape.175
  19.0 0.6 dynamic_slice.23
  19.6 0.1 reshape.172
  19.8 0.6 constant_dynamic-slice_fusion.2
  20.4 0.7 stack.28.vecs
  21.1 0.7 dynamic-slice_add_fusion
  21.9 0.2 copy.105
  22.1 1.0 copy.101
  23.1 0.1 slice_reduce_fusion.2
  23.2 0.1 select_reduce_fusion.1
  23.3 1.7 multiply_convert_fusion.gh
  25.0 0.7 copy.93
  25.7 0.5 copy.94
  26.3 0.7 copy-done.3
  26.9 0.5 copy.95
  27.5 0.2 pad_maximum_fusion.1
  27.7 3.5 copy.96
  31.1 3.3 reshape.171
  34.5 1.4 copy.90
  35.9 0.9 copy.91
  36.8 1.4 copy.97
  38.3 0.1 copy.92
  38.4 2.0 pad_maximum_fusion.w2
  40.4 363.1 %block.1 = (bf16[2048,1024]{1,0:T(8,128)(2,1)}, bf16[2048,512]{1,0:T(8,128)(2,1)}, bf16[2048,512]{1,0:T(8,128)(2,1)}, bf16[2048,512]{1,0:T(8,128)(2,1)}, bf16[20...) custom-call(bf16[512,2048]{1,0:T(8,128)(2,1)} %tok.1, ...), custom_call_target="tpu_custom_call" | custom-call | tf_op jit(solution)/shard_map/block/pallas_call | solution.py:903
  403.5 2.9 convert_element_type.96
  406.4 1.5 convert_element_type.97
  407.9 1.4 convert_bitcast_fusion
  409.2 0.8 convert_element_type.95
  410.3 0.7 copy.104
  411.1 0.6 copy.103
  411.7 0.6 fusion.1
  412.2 0.6 copy.118
  412.8 0.8 copy.119
  413.6 0.8 copy.120
  (80 shorter events, 1.2 us)
Async XLA Ops:
  4.3 1.5 copy-start.11
  4.3 2.3 copy-start.15
  4.3 2.5 copy-start.16
  4.3 2.6 copy-start.12
  4.3 2.7 copy-start.17
  4.3 2.7 copy-start.18
  4.3 2.7 copy-start.19
  4.3 2.7 copy-start.20
  4.3 2.7 copy-start.21
  4.3 2.7 copy-start.22
  4.7 17.1 %copy-start = (bf16[512,2048]{1,0:T(8,128)(2,1)S(1)}, bf16[512,2048]{1,0:T(8,128)(2,1)}, u32[]{:S(2)}) copy-start(bf16[512,2048]{1,0:T(8,128)(2,1)} %param.29) | copy-start | bytes 6291460
  23.3 1.7 copy-start.10
  23.3 1.7 copy-start.2
  25.7 1.2 copy-start.3
  34.4 3.8 copy-start.9
  403.5 2.9 copy-start.1
  406.4 1.5 copy-start.4
  406.4 2.9 copy-start.7
  407.9 2.2 copy-start.8
  407.9 3.8 copy-start.14
  407.9 5.0 %copy-start.6 = (bf16[512,512]{1,0:T(8,128)(2,1)S(1)}, bf16[512,512]{1,0:T(8,128)(2,1)}, u32[]{:S(2)}) copy-start(bf16[512,512]{1,0:T(8,128)(2,1)} %get-tuple-element.159) | copy-start | bytes 1572868
  407.9 5.7 %copy-start.5 = (bf16[512,512]{1,0:T(8,128)(2,1)S(1)}, bf16[512,512]{1,0:T(8,128)(2,1)}, u32[]{:S(2)}) copy-start(bf16[512,512]{1,0:T(8,128)(2,1)} %get-tuple-element.160) | copy-start | bytes 1572868
  412.2 2.2 copy-start.13
